TPU v7x, 128 devices: a whole 4x4x4 slice. The times are simulated.
128 devices in a mesh: gx: 8 (over x_hi, y), gy: 16 (over z, x_lo, core).
Axes of the slice: x: 4 (x_hi: 2, x_lo: 2; x = x_hi * 2 + x_lo), y: 4, z: 4, core: 2. Of those that a mesh axis runs over, the one named last changes fastest.
Arguments:
- level_set: float32 [256, 256, 1024], P('gx', 'gy'), may hold values from -12 to 12
- flow_velocity: float32 [3, 128, 128, 512], P(None, ('gx', 'gy')), may hold values from -2 to 2
- band_mask: int32 [16, 16, 64], P('gx', 'gy'), may hold values from 0 to 1, as said below
Outputs:
- new_level_set: float32 [256, 256, 1024], P('gx', 'gy')
- flow_curvature: float32 [128, 128, 512], P(('gx', 'gy'))
- flow_fraction: float32 [128, 128, 512], P(('gx', 'gy'))
Inputs may be any that keep to these rules, and one draw needn't show every extreme that they name: `band_mask`: tiles in the band mark where the interface lies; their share varies along x.
All inputs are finite; a program needn't handle non-finite values.
Results may differ from a plain program's by a relative error of at most 0.0003.
Values sent between devices are 32-bit elements; how exact they have to be, the bound alone decides.
No kernel may reach another device: no remote copies, remote signals or barrier semaphores. Data moves between devices by JAX's collectives and lax.ppermute only.
A program may use at most 320 MiB of HBM per device.

v0:
```python
import jax
import jax.numpy as jnp
from jax import lax
from jax.sharding import PartitionSpec as P

SWEEPS = 4


time_step = 0.25
pseudo_step = 0.3
weno_eps = 1e-06
front_width = 1.5


def padded_2(cells, sides, width):
    for axis, dim in sides:
        count = lax.axis_size(axis)
        head = lax.slice_in_dim(cells, 0, width, axis=dim)
        tail = lax.slice_in_dim(cells, cells.shape[dim] - width, cells.shape[dim], axis=dim)
        cells = jnp.concatenate(
            [
                lax.ppermute(tail, axis, [(i, (i + 1) % count) for i in range(count)]),
                cells,
                lax.ppermute(head, axis, [((i + 1) % count, i) for i in range(count)]),
            ],
            axis=dim,
        )
    return cells


def squared(values):
    return values * values


def refine(coarse, along):
    inner_count = coarse.shape[along] - 2
    lower_cells = lax.slice_in_dim(coarse, 0, inner_count, axis=along)
    middle = lax.slice_in_dim(coarse, 1, inner_count + 1, axis=along)
    upper_cells = lax.slice_in_dim(coarse, 2, inner_count + 2, axis=along)
    even_cells = 0.25 * lower_cells + 0.75 * middle
    odd_cells = 0.75 * middle + 0.25 * upper_cells
    paired = jnp.stack([even_cells, odd_cells], axis=along + 1)
    new_shape = coarse.shape[:along] + (2 * inner_count,) + coarse.shape[along + 1 :]
    return paired.reshape(new_shape)


def refine_table(coarse_count):
    rows = jnp.arange(coarse_count, dtype=jnp.int32)[:, None]
    cols = jnp.arange(2 * coarse_count, dtype=jnp.int32)[None, :]
    centre_row = cols // 2
    neighbour = jnp.where(
        cols % 2 == 0, (centre_row - 1) % coarse_count, (centre_row + 1) % coarse_count
    )
    return 0.75 * (rows == centre_row).astype(jnp.float32) + 0.25 * (rows == neighbour).astype(
        jnp.float32
    )


def fine_velocity(coarse_padded):
    refined = refine(coarse_padded, 1)
    refined = refine(refined, 2)
    table = refine_table(refined.shape[3])
    return jnp.dot(
        refined, table, precision=lax.Precision.HIGHEST, preferred_element_type=jnp.float32
    )


def band_cells(tiles):
    tile_x, tile_y, tile_z = tiles.shape
    spread = jnp.broadcast_to(
        tiles.astype(jnp.float32)[:, None, :, None, :, None], (tile_x, 16, tile_y, 16, tile_z, 16)
    )
    return spread.reshape(tile_x * 16, tile_y * 16, tile_z * 16)


def weno_blend(first, second, third, fourth, fifth):
    cand_one = first / 3.0 - 7.0 * second / 6.0 + 11.0 * third / 6.0
    cand_two = -second / 6.0 + 5.0 * third / 6.0 + fourth / 3.0
    cand_three = third / 3.0 + 5.0 * fourth / 6.0 - fifth / 6.0
    rough_one = 13.0 / 12.0 * squared(first - 2.0 * second + third) + 0.25 * squared(
        first - 4.0 * second + 3.0 * third
    )
    rough_two = 13.0 / 12.0 * squared(second - 2.0 * third + fourth) + 0.25 * squared(
        second - fourth
    )
    rough_three = 13.0 / 12.0 * squared(third - 2.0 * fourth + fifth) + 0.25 * squared(
        3.0 * third - 4.0 * fourth + fifth
    )
    weight_one = 0.1 / squared(weno_eps + rough_one)
    weight_two = 0.6 / squared(weno_eps + rough_two)
    weight_three = 0.3 / squared(weno_eps + rough_three)
    return (weight_one * cand_one + weight_two * cand_two + weight_three * cand_three) / (
        weight_one + weight_two + weight_three
    )


def weno_pair(padded, along):
    count_out = padded.shape[along] - 6
    differences = lax.slice_in_dim(padded, 1, count_out + 6, axis=along) - lax.slice_in_dim(
        padded, 0, count_out + 5, axis=along
    )
    slopes = [
        lax.slice_in_dim(differences, offset, offset + count_out, axis=along) for offset in range(6)
    ]
    minus_side = weno_blend(slopes[0], slopes[1], slopes[2], slopes[3], slopes[4])
    plus_side = weno_blend(slopes[5], slopes[4], slopes[3], slopes[2], slopes[1])
    return (minus_side, plus_side)


def weno_periodic(values):
    differences = jnp.roll(values, -1, axis=2) - values
    slopes = [jnp.roll(differences, 3 - offset, axis=2) for offset in range(6)]
    minus_side = weno_blend(slopes[0], slopes[1], slopes[2], slopes[3], slopes[4])
    plus_side = weno_blend(slopes[5], slopes[4], slopes[3], slopes[2], slopes[1])
    return (minus_side, plus_side)


def advect_rate(padded, velocity, band):
    total = jnp.zeros(band.shape, jnp.float32)
    pairs = [
        weno_pair(padded[:, 3:-3], 0),
        weno_pair(padded[3:-3], 1),
        weno_periodic(padded[3:-3, 3:-3]),
    ]
    for along in range(3):
        minus_side, plus_side = pairs[along]
        speed = velocity[along]
        total = total + jnp.where(speed > 0, speed * minus_side, speed * plus_side)
    return -band * total


def rk_first(start, rate):
    return start + time_step * rate


def rk_second(start, first_section, rate):
    return 0.75 * start + 0.25 * (first_section + time_step * rate)


def rk_third(start, second_section, rate):
    return start / 3.0 + 2.0 / 3.0 * (second_section + time_step * rate)


def level_sign(values):
    return values / jnp.sqrt(values * values + 1.0)


def sweep_once(padded, sign_field):
    centre = padded[1:-1, 1:-1]
    backs = [
        centre - padded[:-2, 1:-1],
        centre - padded[1:-1, :-2],
        centre - jnp.roll(centre, 1, axis=2),
    ]
    fores = [
        padded[2:, 1:-1] - centre,
        padded[1:-1, 2:] - centre,
        jnp.roll(centre, -1, axis=2) - centre,
    ]
    growing = jnp.zeros(centre.shape, jnp.float32)
    falling = jnp.zeros(centre.shape, jnp.float32)
    for along in range(3):
        growing = growing + jnp.maximum(
            squared(jnp.maximum(backs[along], 0.0)), squared(jnp.minimum(fores[along], 0.0))
        )
        falling = falling + jnp.maximum(
            squared(jnp.minimum(backs[along], 0.0)), squared(jnp.maximum(fores[along], 0.0))
        )
    slope_norm = jnp.sqrt(jnp.where(sign_field > 0, growing, falling))
    return centre - pseudo_step * sign_field * (slope_norm - 1.0)


def curvature(padded):
    inner = padded[1:-1, 1:-1]
    grad_x = 0.5 * (padded[2:, 1:-1] - padded[:-2, 1:-1])
    grad_y = 0.5 * (padded[1:-1, 2:] - padded[1:-1, :-2])
    grad_z = 0.5 * (jnp.roll(inner, -1, axis=2) - jnp.roll(inner, 1, axis=2))
    length_inv = 1.0 / jnp.sqrt(grad_x * grad_x + grad_y * grad_y + grad_z * grad_z + 1.0)
    normal_x = grad_x * length_inv
    normal_y = grad_y * length_inv
    normal_z = (grad_z * length_inv)[1:-1, 1:-1]
    return (
        0.5 * (normal_x[2:, 1:-1] - normal_x[:-2, 1:-1])
        + 0.5 * (normal_y[1:-1, 2:] - normal_y[1:-1, :-2])
        + 0.5 * (jnp.roll(normal_z, -1, axis=2) - jnp.roll(normal_z, 1, axis=2))
    )


def volume_fraction(values):
    return 0.5 * (1.0 + jnp.tanh(values / front_width))


def restrict(values):
    size_x, size_y, size_z = values.shape
    paired = values.reshape(size_x // 2, 2, size_y // 2, 2, size_z).sum(axis=(1, 3))
    rows = jnp.arange(size_z, dtype=jnp.int32)[:, None]
    cols = jnp.arange(size_z // 2, dtype=jnp.int32)[None, :]
    table = 0.125 * (rows // 2 == cols).astype(jnp.float32)
    return jnp.dot(
        paired, table, precision=lax.Precision.HIGHEST, preferred_element_type=jnp.float32
    )


def per_device(level_set, flow_velocity, band_mask):
    blocked = lax.all_to_all(flow_velocity, "gy", split_axis=2, concat_axis=1, tiled=True)
    coarse_padded = padded_2(blocked, (("gx", 1), ("gy", 2)), 1)
    refined = fine_velocity(coarse_padded)
    velocity = (refined[0], refined[1], refined[2])
    band = band_cells(band_mask)

    def section_rate(values):
        padded = padded_2(values, (("gx", 0), ("gy", 1)), 3)
        return advect_rate(padded, velocity, band)

    first_section = rk_first(level_set, section_rate(level_set))
    second_section = rk_second(level_set, first_section, section_rate(first_section))
    advected = rk_third(level_set, second_section, section_rate(second_section))
    sign_field = level_sign(advected)
    current = advected
    for number in range(SWEEPS):
        padded = padded_2(current, (("gx", 0), ("gy", 1)), 1)
        current = sweep_once(padded, sign_field)
    curve_padded = padded_2(current, (("gx", 0), ("gy", 1)), 2)
    kappa = curvature(curve_padded)
    packed = jnp.stack([restrict(kappa), restrict(volume_fraction(current))], axis=0)
    returned = lax.all_to_all(packed, "gy", split_axis=1, concat_axis=2, tiled=True)
    return (current, returned[0], returned[1])


def solution(mesh):
    placed = (P("gx", "gy", None), P(None, ("gx", "gy"), None, None), P("gx", "gy", None))
    return jax.shard_map(
        per_device,
        mesh=mesh,
        in_specs=placed,
        out_specs=(P("gx", "gy", None), P(("gx", "gy"), None, None), P(("gx", "gy"), None, None)),
        check_vma=False,
    )
```

profile of v0, /device:TPU:1, one launch (start us, length us, event | category | flops | bytes accessed | tf_op | source)
XLA Modules:
  0.0 429.8 jit_solution(5668672458610079009)
XLA Ops:
  2.4 6.0 %collective-permute-start.5 = (f32[3,16,1024]{2,1,0:T(8,128)}, f32[3,16,1024]{2,1,0:T(8,128)}, u32[]{:S(2)}, u32[]{:S(2)}) collective-permute-start(f32[3,16,1024]{2,1,0:T(8,128)} %get-tuple-element.81), channel_id=1, source_target_pairs={{16,0},{32,16},{48,32},{64,48},{80,64},{96,80},{112,96},{0,112},{1... | collective-permute-start | bytes 589832 | tf_op jit(solution)/shard_map/ppermute | solution.py:24
  8.4 2.8 copy.59
  11.3 6.3 %all-to-all-start = ((f32[3,1,128,512]{3,0,1,2:T(4,128)}), f32[3,1,128,512]{3,0,1,2:T(4,128)S(1)}, u32[]{:S(2)}, u32[]{:S(2)}) async-start(f32[3,1,128,512]{3,0,1,2:T(4,128)} %copy.59), calls=%async_computation | async-start | bytes 2097152 | tf_op jit(solution)/shard_map/all_to_all | solution.py:205
  27.2 2.8 fusion.124
  34.9 2.8 fusion.122
  37.7 5.5 %collective-permute-done.7 = f32[38,3,1024]{2,0,1:T(8,128)S(1)} collective-permute-done((f32[38,3,1024]{2,0,1:T(8,128)S(1)}, f32[38,3,1024]{2,0,1:T(8,128)S(1)}, u32[]{:S(2)}, u32[]{:S(2)}) %collective-permute-start.7) | collective-permute-done | bytes 466976 | tf_op jit(solution)/shard_map/ppermute | solution.py:24
  45.9 5.9 %collective-permute-start.1 = (f32[3,1,8,512]{3,2,1,0:T(8,128)S(1)}, f32[3,1,8,512]{3,2,1,0:T(8,128)S(1)}, u32[]{:S(2)}, u32[]{:S(2)}) collective-permute-start(f32[3,1,8,512]{3,2,1,0:T(8,128)S(1)} %get-tuple-element.100), channel_id=1, source_target_pairs={{16,0},{32,16},{48,32},{64,48},{80,64},{96,80},{112,96},{0,112},{1... | collective-permute-start | bytes 147464 | tf_op jit(solution)/shard_map/ppermute | solution.py:24
  54.6 4.2 collective-permute-start.3
  63.5 2.8 copy.61
  66.3 3.6 reshape.168
  69.9 3.1 fusion.43
  73.4 4.1 copy.62
  77.5 5.7 %reshape.169 = f32[3,32,16,512]{3,2,1,0:T(8,128)} reshape(f32[3,32,8,2,512]{4,3,2,1,0:T(2,128)} %copy.62) | data formatting | bytes 6291456 | tf_op jit(solution)/shard_map/reshape | solution.py:44
  83.2 13.6 %fusion.26 = f32[3,32,16,1024]{3,2,1,0:T(8,128)S(1)} fusion(f32[3,32,16,512]{3,2,1,0:T(8,128)} %reshape.169, s32[1024]{0:T(1024)S(1)} %get-tuple-element.104, s32[1024]{0:T(1024)S(1)} %get-tuple-element.103), kind=kOutput, calls=%fused_computation.122 | convolution fusion | flops 9666297856 | bytes 9445376 | tf_op jit(solution)/shard_map/dot_general | solution.py:63
  96.8 32.8 %multiply_add_fusion.2 = (f32[32,16,1024]{2,1,0:T(8,128)S(1)}, pred[32,16,1024]{2,1,0:T(8,128)(4,1)S(1)}, pred[32,16,1024]{2,1,0:T(8,128)(4,1)S(1)}, pred[32,16,1024]{2,1,0:T(8,128)(4,1)}) fusion(f32[32,16,1024]{2,1,0:T(8,128)S(1)} %copy-done.3, f32[32,16,1024]{2,1,0:T(8,128)S(1)} %get-tuple-element.84, f32[32,16,2]{2,1,0:T(8,128)} %get-tuple-element.86, ...), kind=kLoop, calls=%fused_computation.139 | loop fusion | flops 206569472 | bytes 49938432 | tf_op jit(solution)/shard_map/add | solution.py:133
  133.1 2.9 fusion.117
  136.0 5.1 %collective-permute-start.9 = (f32[3,16,1024]{2,1,0:T(8,128)S(1)}, f32[3,16,1024]{2,1,0:T(8,128)S(1)}, u32[]{:S(2)}, u32[]{:S(2)}) collective-permute-start(f32[3,16,1024]{2,1,0:T(8,128)S(1)} %get-tuple-element.72), channel_id=1, source_target_pairs={{16,0},{32,16},{48,32},{64,48},{80,64},{96,80},{112,96},{0,112},{1... | collective-permute-start | bytes 589832 | tf_op jit(solution)/shard_map/ppermute | solution.py:24
  145.3 4.5 %collective-permute-start.11 = (f32[38,3,1024]{2,0,1:T(8,128)S(1)}, f32[38,3,1024]{2,0,1:T(8,128)S(1)}, u32[]{:S(2)}, u32[]{:S(2)}) collective-permute-start(f32[38,3,1024]{2,0,1:T(8,128)S(1)} %copy.68), channel_id=1, source_target_pairs={{1,0},{2,1},{3,2},{4,3},{5,4},{6,5},{7,6},{8,7},{9,8},{10,9},{11,1... | collective-permute-start | bytes 1400840 | tf_op jit(solution)/shard_map/ppermute | solution.py:24
  151.3 4.4 %collective-permute-done.11 = f32[38,3,1024]{2,0,1:T(8,128)S(1)} collective-permute-done((f32[38,3,1024]{2,0,1:T(8,128)S(1)}, f32[38,3,1024]{2,0,1:T(8,128)S(1)}, u32[]{:S(2)}, u32[]{:S(2)}) %collective-permute-start.11) | collective-permute-done | bytes 466976 | tf_op jit(solution)/shard_map/ppermute | solution.py:24
  159.9 32.6 %multiply_add_fusion.1 = f32[32,16,1024]{2,1,0:T(8,128)S(1)} fusion(f32[32,16,1024]{2,1,0:T(8,128)S(1)} %get-tuple-element.7, pred[32,16,1024]{2,1,0:T(8,128)(4,1)} %get-tuple-element.10, f32[32,16,1024]{2,1,0:T(8,128)S(1)} %maximum_subtract_fusion.1, f32[32,16,2]{2,1,0:T(8,128)} %get-tuple-element.74, f32[32,16,1022]{2,1,0:T(8,128)} %get-tuple-element.76, ...), kind=kLoop, calls=%fused_computation.138 | loop fusion | flops 206569472 | bytes 52035584 | tf_op jit(solution)/shard_map/add | solution.py:137
  196.0 2.9 fusion.112
  198.9 5.1 %collective-permute-start.13 = (f32[3,16,1024]{2,1,0:T(8,128)S(1)}, f32[3,16,1024]{2,1,0:T(8,128)S(1)}, u32[]{:S(2)}, u32[]{:S(2)}) collective-permute-start(f32[3,16,1024]{2,1,0:T(8,128)S(1)} %get-tuple-element.62), channel_id=1, source_target_pairs={{16,0},{32,16},{48,32},{64,48},{80,64},{96,80},{112,96},{0,112},{1... | collective-permute-start | bytes 589832 | tf_op jit(solution)/shard_map/ppermute | solution.py:24
  208.2 7.8 %collective-permute-start.15 = (f32[38,3,1024]{2,0,1:T(8,128)S(1)}, f32[38,3,1024]{2,0,1:T(8,128)S(1)}, u32[]{:S(2)}, u32[]{:S(2)}) collective-permute-start(f32[38,3,1024]{2,0,1:T(8,128)S(1)} %copy.72), channel_id=1, source_target_pairs={{1,0},{2,1},{3,2},{4,3},{5,4},{6,5},{7,6},{8,7},{9,8},{10,9},{11,1... | collective-permute-start | bytes 1400840 | tf_op jit(solution)/shard_map/ppermute | solution.py:24
  217.4 4.8 %collective-permute-done.15 = f32[38,3,1024]{2,0,1:T(8,128)S(1)} collective-permute-done((f32[38,3,1024]{2,0,1:T(8,128)S(1)}, f32[38,3,1024]{2,0,1:T(8,128)S(1)}, u32[]{:S(2)}, u32[]{:S(2)}) %collective-permute-start.15) | collective-permute-done | bytes 466976 | tf_op jit(solution)/shard_map/ppermute | solution.py:24
  226.5 32.4 %multiply_add_fusion = f32[32,16,1024]{2,1,0:T(8,128)S(1)} fusion(f32[32,16,1024]{2,1,0:T(8,128)S(1)} %multiply_add_fusion.1, pred[32,16,1024]{2,1,0:T(8,128)(4,1)} %get-tuple-element.10, f32[32,16,1024]{2,1,0:T(8,128)S(1)} %maximum_subtract_fusion.2, f32[32,16,2]{2,1,0:T(8,128)} %get-tuple-element.64, f32[32,16,1022]{2,1,0:T(8,128)} %get-tuple-element.66, ...), kind=kLoop, calls=%fused_computation.137 | loop fusion | flops 206569472 | bytes 52035584 | tf_op jit(solution)/shard_map/add | solution.py:141
  259.0 5.7 %collective-permute-start.17 = (f32[1,16,1024]{2,1,0:T(8,128)S(1)}, f32[1,16,1024]{2,1,0:T(8,128)S(1)}, u32[]{:S(2)}, u32[]{:S(2)}) collective-permute-start(f32[1,16,1024]{2,1,0:T(8,128)S(1)} %get-tuple-element.56), channel_id=1, source_target_pairs={{16,0},{32,16},{48,32},{64,48},{80,64},{96,80},{112,96},{0,112},{1... | collective-permute-start | bytes 196616 | tf_op jit(solution)/shard_map/ppermute | solution.py:24
  266.3 3.6 collective-permute-start.18
  270.0 3.5 collective-permute-start.19
  275.0 7.4 %multiply_subtract_fusion.3 = f32[32,16,1024]{2,1,0:T(8,128)S(1)} fusion(f32[32,16,1024]{2,1,0:T(8,128)S(1)} %multiply_add_fusion, f32[32,16,1]{2,1,0:T(8,128)S(1)} %get-tuple-element.58, f32[32,16,1023]{2,1,0:T(8,128)S(1)} %get-tuple-element.60, f32[32,16,1023]{2,1,0:T(8,128)S(1)} %get-tuple-element.59, f32[32,16,1]{2,1,0:T(8,128)S(1)} %get-tuple-element.57, ...), kind=kLoop, calls=%fused_computation.135 | loop fusion | flops 30932992 | bytes 8798208 | tf_op jit(solution)/shard_map/sub | solution.py:170
  282.6 5.8 %collective-permute-start.21 = (f32[1,16,1024]{2,1,0:T(8,128)S(1)}, f32[1,16,1024]{2,1,0:T(8,128)S(1)}, u32[]{:S(2)}, u32[]{:S(2)}) collective-permute-start(f32[1,16,1024]{2,1,0:T(8,128)S(1)} %get-tuple-element.50), channel_id=1, source_target_pairs={{16,0},{32,16},{48,32},{64,48},{80,64},{96,80},{112,96},{0,112},{1... | collective-permute-start | bytes 196616 | tf_op jit(solution)/shard_map/ppermute | solution.py:24
  290.7 6.2 %collective-permute-start.23 = (f32[34,1,1024]{2,1,0:T(1,128)S(1)}, f32[34,1,1024]{2,1,0:T(1,128)S(1)}, u32[]{:S(2)}, u32[]{:S(2)}) collective-permute-start(f32[34,1,1024]{2,1,0:T(1,128)S(1)} %get-tuple-element.32), channel_id=1, source_target_pairs={{1,0},{2,1},{3,2},{4,3},{5,4},{6,5},{7,6},{8,7},{9,8},{10,9},{11,1... | collective-permute-start | bytes 417800 | tf_op jit(solution)/shard_map/ppermute | solution.py:24
  297.9 7.5 %multiply_subtract_fusion.2 = f32[32,16,1024]{2,1,0:T(8,128)S(1)} fusion(f32[32,16,1024]{2,1,0:T(8,128)S(1)} %multiply_subtract_fusion.3, f32[32,16,1]{2,1,0:T(8,128)S(1)} %get-tuple-element.52, f32[32,16,1023]{2,1,0:T(8,128)S(1)} %get-tuple-element.54, f32[32,16,1023]{2,1,0:T(8,128)S(1)} %get-tuple-element.53, f32[32,16,1]{2,1,0:T(8,128)S(1)} %get-tuple-element.51, ...), kind=kLoop, calls=%fused_computation.134 | loop fusion | flops 30932992 | bytes 10895360 | tf_op jit(solution)/shard_map/sub | solution.py:170
  305.5 5.5 %collective-permute-start.25 = (f32[1,16,1024]{2,1,0:T(8,128)S(1)}, f32[1,16,1024]{2,1,0:T(8,128)S(1)}, u32[]{:S(2)}, u32[]{:S(2)}) collective-permute-start(f32[1,16,1024]{2,1,0:T(8,128)S(1)} %get-tuple-element.44), channel_id=1, source_target_pairs={{16,0},{32,16},{48,32},{64,48},{80,64},{96,80},{112,96},{0,112},{1... | collective-permute-start | bytes 196616 | tf_op jit(solution)/shard_map/ppermute | solution.py:24
  312.9 7.0 %collective-permute-start.27 = (f32[34,1,1024]{2,1,0:T(1,128)S(1)}, f32[34,1,1024]{2,1,0:T(1,128)S(1)}, u32[]{:S(2)}, u32[]{:S(2)}) collective-permute-start(f32[34,1,1024]{2,1,0:T(1,128)S(1)} %get-tuple-element.30), channel_id=1, source_target_pairs={{1,0},{2,1},{3,2},{4,3},{5,4},{6,5},{7,6},{8,7},{9,8},{10,9},{11,1... | collective-permute-start | bytes 417800 | tf_op jit(solution)/shard_map/ppermute | solution.py:24
  320.9 7.5 %multiply_subtract_fusion.1 = f32[32,16,1024]{2,1,0:T(8,128)S(1)} fusion(f32[32,16,1024]{2,1,0:T(8,128)S(1)} %multiply_subtract_fusion.2, f32[32,16,1]{2,1,0:T(8,128)S(1)} %get-tuple-element.46, f32[32,16,1023]{2,1,0:T(8,128)S(1)} %get-tuple-element.48, f32[32,16,1023]{2,1,0:T(8,128)S(1)} %get-tuple-element.47, f32[32,16,1]{2,1,0:T(8,128)S(1)} %get-tuple-element.45, ...), kind=kLoop, calls=%fused_computation.133 | loop fusion | flops 30932992 | bytes 10895360 | tf_op jit(solution)/shard_map/sub | solution.py:170
  328.5 5.5 %collective-permute-start.29 = (f32[1,16,1024]{2,1,0:T(8,128)S(1)}, f32[1,16,1024]{2,1,0:T(8,128)S(1)}, u32[]{:S(2)}, u32[]{:S(2)}) collective-permute-start(f32[1,16,1024]{2,1,0:T(8,128)S(1)} %get-tuple-element.38), channel_id=1, source_target_pairs={{16,0},{32,16},{48,32},{64,48},{80,64},{96,80},{112,96},{0,112},{1... | collective-permute-start | bytes 196616 | tf_op jit(solution)/shard_map/ppermute | solution.py:24
  335.9 7.4 %collective-permute-start.31 = (f32[34,1,1024]{2,1,0:T(1,128)S(1)}, f32[34,1,1024]{2,1,0:T(1,128)S(1)}, u32[]{:S(2)}, u32[]{:S(2)}) collective-permute-start(f32[34,1,1024]{2,1,0:T(1,128)S(1)} %get-tuple-element.28), channel_id=1, source_target_pairs={{1,0},{2,1},{3,2},{4,3},{5,4},{6,5},{7,6},{8,7},{9,8},{10,9},{11,1... | collective-permute-start | bytes 417800 | tf_op jit(solution)/shard_map/ppermute | solution.py:24
  344.3 8.6 %add_multiply_fusion = (f32[32,16,1024]{2,1,0:T(8,128)}, f32[32,16,1024]{2,1,0:T(8,128)S(1)}) fusion(f32[32,16,1024]{2,1,0:T(8,128)S(1)} %multiply_subtract_fusion.1, f32[32,16,1]{2,1,0:T(8,128)S(1)} %get-tuple-element.40, f32[32,16,1023]{2,1,0:T(8,128)S(1)} %get-tuple-element.42, f32[32,16,1023]{2,1,0:T(8,128)S(1)} %get-tuple-element.41, ...), kind=kLoop, calls=%fused_computation.130 | loop fusion | flops 32505856 | bytes 12992512 | tf_op jit(solution)/shard_map/mul | solution.py:190
  353.0 5.4 %collective-permute-start.33 = (f32[2,16,1024]{2,1,0:T(8,128)S(1)}, f32[2,16,1024]{2,1,0:T(8,128)S(1)}, u32[]{:S(2)}, u32[]{:S(2)}) collective-permute-start(f32[2,16,1024]{2,1,0:T(8,128)S(1)} %get-tuple-element.36), channel_id=1, source_target_pairs={{16,0},{32,16},{48,32},{64,48},{80,64},{96,80},{112,96},{0,112},{1... | collective-permute-start | bytes 393224 | tf_op jit(solution)/shard_map/ppermute | solution.py:24
  361.7 7.0 %collective-permute-start.35 = (f32[36,2,1024]{2,1,0:T(2,128)}, f32[36,2,1024]{2,1,0:T(2,128)S(1)}, u32[]{:S(2)}, u32[]{:S(2)}) collective-permute-start(f32[36,2,1024]{2,1,0:T(2,128)} %get-tuple-element.26), channel_id=1, source_target_pairs={{1,0},{2,1},{3,2},{4,3},{5,4},{6,5},{7,6},{8,7},{9,8},{10,9},{11,1... | collective-permute-start | bytes 884744 | tf_op jit(solution)/shard_map/ppermute | solution.py:24
  368.7 3.5 reshape.171
  372.2 3.2 reduce_sum.19
  378.3 4.3 %fusion.91 = (f32[34,18,1023]{2,1,0:T(8,128)}, f32[34,18,1023]{2,1,0:T(8,128)}) fusion(f32[36,20,1024]{2,1,0:T(8,128)S(1)} %pad_maximum_fusion.3), kind=kLoop, calls=%fused_computation.233 | loop fusion | bytes 10017216 | tf_op jit(solution)/shard_map/jit(_roll_static)/slice | solution.py:177
  382.7 12.2 %fusion.87 = (f32[34,18,1024]{2,1,0:T(8,128)S(1)}, f32[34,18,1024]{2,1,0:T(8,128)S(1)}) fusion(f32[34,18,1023]{2,1,0:T(8,128)} %get-tuple-element.12, f32[36,2,1024]{2,1,0:T(2,128)S(1)} %collective-permute-done.35, f32[2,16,1024]{2,1,0:T(8,128)S(1)} %collective-permute-done.33, f32[32,16,1024]{2,1,0:T(8,128)S(1)} %get-tuple-element.6, ...), kind=kLoop, calls=%fused_computation.232 | loop fusion | flops 18173952 | bytes 17984736 | tf_op jit(solution)/shard_map/mul | solution.py:181
  395.0 3.0 fusion.93
  398.0 3.4 fusion.66
  401.4 5.2 %fusion.9 = f32[32,16,1024]{2,1,0:T(8,128)} fusion(f32[34,18,1024]{2,1,0:T(8,128)S(1)} %get-tuple-element.18, f32[34,18,1024]{2,1,0:T(8,128)S(1)} %get-tuple-element.17, f32[32,16,1]{2,1,0:T(8,128)S(1)} %get-tuple-element.14, f32[32,16,1023]{2,1,0:T(8,128)} %get-tuple-element.16, f32[32,16,1023]{2,1,0:T(8,128)} %get-tuple-element.15, ...), kind=kLoop, calls=%fused_computation.42 | loop fusion | flops 4194304 | bytes 14680064 | tf_op jit(solution)/shard_map/add | solution.py:183
  412.3 16.2 %all_to_all.21 = f32[2,16,8,512]{3,2,0,1:T(8,128)S(1)} all-to-all(f32[2,16,8,512]{3,2,0,1:T(8,128)S(1)} %copy.75), channel_id=1, replica_groups=mesh['gx'=8,'gy'=16] {'gy'}, dimensions={1} | all-to-all | bytes 1048576 | tf_op jit(solution)/shard_map/all_to_all | solution.py:226
  (166 shorter events, 79.0 us)
Async XLA Ops:
  2.4 15.1 %copy-start.11 = (s32[2,1,64]{2,1,0:T(1,128)S(1)}, s32[2,1,64]{2,1,0:T(1,128)}, u32[]{:S(2)}) copy-start(s32[2,1,64]{2,1,0:T(1,128)} %param.5) | copy-start | bytes 1540
  2.4 21.6 %collective-permute-start.5 = (f32[3,16,1024]{2,1,0:T(8,128)}, f32[3,16,1024]{2,1,0:T(8,128)}, u32[]{:S(2)}, u32[]{:S(2)}) collective-permute-start(f32[3,16,1024]{2,1,0:T(8,128)} %get-tuple-element.81), channel_id=1, source_target_pairs={{16,0},{32,16},{48,32},{64,48},{80,64},{96,80},{112,96},{0,112},{1... | collective-permute-start | bytes 589832 | tf_op jit(solution)/shard_map/ppermute | solution.py:24
  8.4 9.1 %copy-start.2 = (f32[32,16,1024]{2,1,0:T(8,128)S(1)}, f32[32,16,1024]{2,1,0:T(8,128)}, u32[]{:S(2)}) copy-start(f32[32,16,1024]{2,1,0:T(8,128)} %param.3) | copy-start | bytes 6291460
  8.4 11.9 %collective-permute-start.4 = (f32[3,16,1024]{2,1,0:T(8,128)}, f32[3,16,1024]{2,1,0:T(8,128)}, u32[]{:S(2)}, u32[]{:S(2)}) collective-permute-start(f32[3,16,1024]{2,1,0:T(8,128)} %get-tuple-element.82), channel_id=1, source_target_pairs={{0,16},{16,32},{32,48},{48,64},{64,80},{80,96},{96,112},{112,0},{1... | collective-permute-start | bytes 589832 | tf_op jit(solution)/shard_map/ppermute | solution.py:22
  11.3 34.3 %all-to-all-start = ((f32[3,1,128,512]{3,0,1,2:T(4,128)}), f32[3,1,128,512]{3,0,1,2:T(4,128)S(1)}, u32[]{:S(2)}, u32[]{:S(2)}) async-start(f32[3,1,128,512]{3,0,1,2:T(4,128)} %copy.59), calls=%async_computation | async-start | bytes 2097152 | tf_op jit(solution)/shard_map/all_to_all | solution.py:205
  31.4 11.8 %collective-permute-start.7 = (f32[38,3,1024]{2,0,1:T(8,128)S(1)}, f32[38,3,1024]{2,0,1:T(8,128)S(1)}, u32[]{:S(2)}, u32[]{:S(2)}) collective-permute-start(f32[38,3,1024]{2,0,1:T(8,128)S(1)} %copy.64), channel_id=1, source_target_pairs={{1,0},{2,1},{3,2},{4,3},{5,4},{6,5},{7,6},{8,7},{9,8},{10,9},{11,1... | collective-permute-start | bytes 1400840 | tf_op jit(solution)/shard_map/ppermute | solution.py:24
  31.6 12.8 %collective-permute-start.6 = (f32[38,3,1024]{2,0,1:T(8,128)S(1)}, f32[38,3,1024]{2,0,1:T(8,128)S(1)}, u32[]{:S(2)}, u32[]{:S(2)}) collective-permute-start(f32[38,3,1024]{2,0,1:T(8,128)S(1)} %copy.63), channel_id=1, source_target_pairs={{0,1},{1,2},{2,3},{3,4},{4,5},{5,6},{6,7},{7,8},{8,9},{9,10},{10,1... | collective-permute-start | bytes 1400840 | tf_op jit(solution)/shard_map/ppermute | solution.py:22
  45.6 6.2 %copy-start.7 = (f32[38,3,1024]{2,1,0:T(4,128)S(1)}, f32[38,3,1024]{2,1,0:T(4,128)}, u32[]{:S(2)}) copy-start(f32[38,3,1024]{2,1,0:T(4,128)} %copy.66) | copy-start | bytes 1400836
  45.6 6.2 %copy-start.8 = (f32[38,3,1024]{2,1,0:T(4,128)S(1)}, f32[38,3,1024]{2,1,0:T(4,128)}, u32[]{:S(2)}) copy-start(f32[38,3,1024]{2,1,0:T(4,128)} %copy.65) | copy-start | bytes 1400836
  45.9 8.5 %collective-permute-start = (f32[3,1,8,512]{3,2,1,0:T(8,128)S(1)}, f32[3,1,8,512]{3,2,1,0:T(8,128)S(1)}, u32[]{:S(2)}, u32[]{:S(2)}) collective-permute-start(f32[3,1,8,512]{3,2,1,0:T(8,128)S(1)} %get-tuple-element.99), channel_id=1, source_target_pairs={{0,16},{16,32},{32,48},{48,64},{64,80},{80,96},{96,112},{112,0},{1... | collective-permute-start | bytes 147464 | tf_op jit(solution)/shard_map/ppermute | solution.py:22
  45.9 8.4 %collective-permute-start.1 = (f32[3,1,8,512]{3,2,1,0:T(8,128)S(1)}, f32[3,1,8,512]{3,2,1,0:T(8,128)S(1)}, u32[]{:S(2)}, u32[]{:S(2)}) collective-permute-start(f32[3,1,8,512]{3,2,1,0:T(8,128)S(1)} %get-tuple-element.100), channel_id=1, source_target_pairs={{16,0},{32,16},{48,32},{64,48},{80,64},{96,80},{112,96},{0,112},{1... | collective-permute-start | bytes 147464 | tf_op jit(solution)/shard_map/ppermute | solution.py:24
  54.5 6.6 %collective-permute-start.2 = (f32[3,18,1,512]{3,2,1,0:T(1,128)S(1)}, f32[3,18,1,512]{3,2,1,0:T(1,128)S(1)}, u32[]{:S(2)}, u32[]{:S(2)}) collective-permute-start(f32[3,18,1,512]{3,2,1,0:T(1,128)S(1)} %get-tuple-element.97), channel_id=1, source_target_pairs={{0,1},{1,2},{2,3},{3,4},{4,5},{5,6},{6,7},{7,8},{8,9},{9,10},{10,1... | collective-permute-start | bytes 331784 | tf_op jit(solution)/shard_map/ppermute | solution.py:22
  54.6 7.5 %collective-permute-start.3 = (f32[3,18,1,512]{3,2,1,0:T(1,128)S(1)}, f32[3,18,1,512]{3,2,1,0:T(1,128)S(1)}, u32[]{:S(2)}, u32[]{:S(2)}) collective-permute-start(f32[3,18,1,512]{3,2,1,0:T(1,128)S(1)} %get-tuple-element.98), channel_id=1, source_target_pairs={{1,0},{2,1},{3,2},{4,3},{5,4},{6,5},{7,6},{8,7},{9,8},{10,9},{11,1... | collective-permute-start | bytes 331784 | tf_op jit(solution)/shard_map/ppermute | solution.py:24
  77.5 19.3 %copy-start.9 = (f32[32,16,3]{2,1,0:T(8,128)S(1)}, f32[32,16,3]{2,1,0:T(8,128)}, u32[]{:S(2)}) copy-start(f32[32,16,3]{2,1,0:T(8,128)} %slice.799) | copy-start | bytes 18436
  83.2 13.6 %copy-start = (f32[37,16,1024]{2,1,0:T(8,128)S(1)}, f32[37,16,1024]{2,1,0:T(8,128)}, u32[]{:S(2)}) copy-start(f32[37,16,1024]{2,1,0:T(8,128)} %slice_subtract_fusion.6) | copy-start | bytes 7274500
  83.2 13.6 %copy-start.1 = (f32[32,21,1024]{2,1,0:T(8,128)S(1)}, f32[32,21,1024]{2,1,0:T(8,128)}, u32[]{:S(2)}) copy-start(f32[32,21,1024]{2,1,0:T(8,128)} %slice_subtract_fusion.3) | copy-start | bytes 8257540
  83.2 13.6 %copy-start.3 = (f32[32,16,1024]{2,1,0:T(8,128)S(1)}, f32[32,16,1024]{2,1,0:T(8,128)}, u32[]{:S(2)}) copy-start(f32[32,16,1024]{2,1,0:T(8,128)} %param.3) | copy-start | bytes 6291460
  83.2 13.6 %copy-start.6 = (f32[32,16,1023]{2,1,0:T(8,128)S(1)}, f32[32,16,1023]{2,1,0:T(8,128)}, u32[]{:S(2)}) copy-start(f32[32,16,1023]{2,1,0:T(8,128)} %get-tuple-element.91) | copy-start | bytes 6285316
  136.0 8.1 %collective-permute-start.8 = (f32[3,16,1024]{2,1,0:T(8,128)S(1)}, f32[3,16,1024]{2,1,0:T(8,128)S(1)}, u32[]{:S(2)}, u32[]{:S(2)}) collective-permute-start(f32[3,16,1024]{2,1,0:T(8,128)S(1)} %get-tuple-element.71), channel_id=1, source_target_pairs={{0,16},{16,32},{32,48},{48,64},{64,80},{80,96},{96,112},{112,0},{1... | collective-permute-start | bytes 589832 | tf_op jit(solution)/shard_map/ppermute | solution.py:22
  136.0 8.1 %collective-permute-start.9 = (f32[3,16,1024]{2,1,0:T(8,128)S(1)}, f32[3,16,1024]{2,1,0:T(8,128)S(1)}, u32[]{:S(2)}, u32[]{:S(2)}) collective-permute-start(f32[3,16,1024]{2,1,0:T(8,128)S(1)} %get-tuple-element.72), channel_id=1, source_target_pairs={{16,0},{32,16},{48,32},{64,48},{80,64},{96,80},{112,96},{0,112},{1... | collective-permute-start | bytes 589832 | tf_op jit(solution)/shard_map/ppermute | solution.py:24
  145.3 10.3 %collective-permute-start.11 = (f32[38,3,1024]{2,0,1:T(8,128)S(1)}, f32[38,3,1024]{2,0,1:T(8,128)S(1)}, u32[]{:S(2)}, u32[]{:S(2)}) collective-permute-start(f32[38,3,1024]{2,0,1:T(8,128)S(1)} %copy.68), channel_id=1, source_target_pairs={{1,0},{2,1},{3,2},{4,3},{5,4},{6,5},{7,6},{8,7},{9,8},{10,9},{11,1... | collective-permute-start | bytes 1400840 | tf_op jit(solution)/shard_map/ppermute | solution.py:24
  149.9 8.5 %collective-permute-start.10 = (f32[38,3,1024]{2,0,1:T(8,128)S(1)}, f32[38,3,1024]{2,0,1:T(8,128)S(1)}, u32[]{:S(2)}, u32[]{:S(2)}) collective-permute-start(f32[38,3,1024]{2,0,1:T(8,128)S(1)} %copy.67), channel_id=1, source_target_pairs={{0,1},{1,2},{2,3},{3,4},{4,5},{5,6},{6,7},{7,8},{8,9},{9,10},{10,1... | collective-permute-start | bytes 1400840 | tf_op jit(solution)/shard_map/ppermute | solution.py:22
  198.9 8.1 %collective-permute-start.12 = (f32[3,16,1024]{2,1,0:T(8,128)S(1)}, f32[3,16,1024]{2,1,0:T(8,128)S(1)}, u32[]{:S(2)}, u32[]{:S(2)}) collective-permute-start(f32[3,16,1024]{2,1,0:T(8,128)S(1)} %get-tuple-element.61), channel_id=1, source_target_pairs={{0,16},{16,32},{32,48},{48,64},{64,80},{80,96},{96,112},{112,0},{1... | collective-permute-start | bytes 589832 | tf_op jit(solution)/shard_map/ppermute | solution.py:22
  198.9 8.1 %collective-permute-start.13 = (f32[3,16,1024]{2,1,0:T(8,128)S(1)}, f32[3,16,1024]{2,1,0:T(8,128)S(1)}, u32[]{:S(2)}, u32[]{:S(2)}) collective-permute-start(f32[3,16,1024]{2,1,0:T(8,128)S(1)} %get-tuple-element.62), channel_id=1, source_target_pairs={{16,0},{32,16},{48,32},{64,48},{80,64},{96,80},{112,96},{0,112},{1... | collective-permute-start | bytes 589832 | tf_op jit(solution)/shard_map/ppermute | solution.py:24
  208.2 13.9 %collective-permute-start.15 = (f32[38,3,1024]{2,0,1:T(8,128)S(1)}, f32[38,3,1024]{2,0,1:T(8,128)S(1)}, u32[]{:S(2)}, u32[]{:S(2)}) collective-permute-start(f32[38,3,1024]{2,0,1:T(8,128)S(1)} %copy.72), channel_id=1, source_target_pairs={{1,0},{2,1},{3,2},{4,3},{5,4},{6,5},{7,6},{8,7},{9,8},{10,9},{11,1... | collective-permute-start | bytes 1400840 | tf_op jit(solution)/shard_map/ppermute | solution.py:24
  216.0 9.0 %collective-permute-start.14 = (f32[38,3,1024]{2,0,1:T(8,128)S(1)}, f32[38,3,1024]{2,0,1:T(8,128)S(1)}, u32[]{:S(2)}, u32[]{:S(2)}) collective-permute-start(f32[38,3,1024]{2,0,1:T(8,128)S(1)} %copy.71), channel_id=1, source_target_pairs={{0,1},{1,2},{2,3},{3,4},{4,5},{5,6},{6,7},{7,8},{8,9},{9,10},{10,1... | collective-permute-start | bytes 1400840 | tf_op jit(solution)/shard_map/ppermute | solution.py:22
  258.9 7.0 %collective-permute-start.16 = (f32[1,16,1024]{2,1,0:T(8,128)S(1)}, f32[1,16,1024]{2,1,0:T(8,128)S(1)}, u32[]{:S(2)}, u32[]{:S(2)}) collective-permute-start(f32[1,16,1024]{2,1,0:T(8,128)S(1)} %get-tuple-element.55), channel_id=1, source_target_pairs={{0,16},{16,32},{32,48},{48,64},{64,80},{80,96},{96,112},{112,0},{1... | collective-permute-start | bytes 196616 | tf_op jit(solution)/shard_map/ppermute | solution.py:22
  259.0 7.0 %collective-permute-start.17 = (f32[1,16,1024]{2,1,0:T(8,128)S(1)}, f32[1,16,1024]{2,1,0:T(8,128)S(1)}, u32[]{:S(2)}, u32[]{:S(2)}) collective-permute-start(f32[1,16,1024]{2,1,0:T(8,128)S(1)} %get-tuple-element.56), channel_id=1, source_target_pairs={{16,0},{32,16},{48,32},{64,48},{80,64},{96,80},{112,96},{0,112},{1... | collective-permute-start | bytes 196616 | tf_op jit(solution)/shard_map/ppermute | solution.py:24
  266.3 7.9 %collective-permute-start.18 = (f32[34,1,1024]{2,1,0:T(1,128)S(1)}, f32[34,1,1024]{2,1,0:T(1,128)S(1)}, u32[]{:S(2)}, u32[]{:S(2)}) collective-permute-start(f32[34,1,1024]{2,1,0:T(1,128)S(1)} %get-tuple-element.33), channel_id=1, source_target_pairs={{0,1},{1,2},{2,3},{3,4},{4,5},{5,6},{6,7},{7,8},{8,9},{9,10},{10,1... | collective-permute-start | bytes 417800 | tf_op jit(solution)/shard_map/ppermute | solution.py:22
  270.0 5.1 %collective-permute-start.19 = (f32[34,1,1024]{2,1,0:T(1,128)S(1)}, f32[34,1,1024]{2,1,0:T(1,128)S(1)}, u32[]{:S(2)}, u32[]{:S(2)}) collective-permute-start(f32[34,1,1024]{2,1,0:T(1,128)S(1)} %get-tuple-element.34), channel_id=1, source_target_pairs={{1,0},{2,1},{3,2},{4,3},{5,4},{6,5},{7,6},{8,7},{9,8},{10,9},{11,1... | collective-permute-start | bytes 417800 | tf_op jit(solution)/shard_map/ppermute | solution.py:24
  282.5 7.4 %collective-permute-start.20 = (f32[1,16,1024]{2,1,0:T(8,128)S(1)}, f32[1,16,1024]{2,1,0:T(8,128)S(1)}, u32[]{:S(2)}, u32[]{:S(2)}) collective-permute-start(f32[1,16,1024]{2,1,0:T(8,128)S(1)} %get-tuple-element.49), channel_id=1, source_target_pairs={{0,16},{16,32},{32,48},{48,64},{64,80},{80,96},{96,112},{112,0},{1... | collective-permute-start | bytes 196616 | tf_op jit(solution)/shard_map/ppermute | solution.py:22
  282.6 7.3 %collective-permute-start.21 = (f32[1,16,1024]{2,1,0:T(8,128)S(1)}, f32[1,16,1024]{2,1,0:T(8,128)S(1)}, u32[]{:S(2)}, u32[]{:S(2)}) collective-permute-start(f32[1,16,1024]{2,1,0:T(8,128)S(1)} %get-tuple-element.50), channel_id=1, source_target_pairs={{16,0},{32,16},{48,32},{64,48},{80,64},{96,80},{112,96},{0,112},{1... | collective-permute-start | bytes 196616 | tf_op jit(solution)/shard_map/ppermute | solution.py:24
  290.1 7.5 %collective-permute-start.22 = (f32[34,1,1024]{2,1,0:T(1,128)S(1)}, f32[34,1,1024]{2,1,0:T(1,128)S(1)}, u32[]{:S(2)}, u32[]{:S(2)}) collective-permute-start(f32[34,1,1024]{2,1,0:T(1,128)S(1)} %get-tuple-element.31), channel_id=1, source_target_pairs={{0,1},{1,2},{2,3},{3,4},{4,5},{5,6},{6,7},{7,8},{8,9},{9,10},{10,1... | collective-permute-start | bytes 417800 | tf_op jit(solution)/shard_map/ppermute | solution.py:22
  290.7 7.2 %collective-permute-start.23 = (f32[34,1,1024]{2,1,0:T(1,128)S(1)}, f32[34,1,1024]{2,1,0:T(1,128)S(1)}, u32[]{:S(2)}, u32[]{:S(2)}) collective-permute-start(f32[34,1,1024]{2,1,0:T(1,128)S(1)} %get-tuple-element.32), channel_id=1, source_target_pairs={{1,0},{2,1},{3,2},{4,3},{5,4},{6,5},{7,6},{8,7},{9,8},{10,9},{11,1... | collective-permute-start | bytes 417800 | tf_op jit(solution)/shard_map/ppermute | solution.py:24
  305.4 7.2 %collective-permute-start.24 = (f32[1,16,1024]{2,1,0:T(8,128)S(1)}, f32[1,16,1024]{2,1,0:T(8,128)S(1)}, u32[]{:S(2)}, u32[]{:S(2)}) collective-permute-start(f32[1,16,1024]{2,1,0:T(8,128)S(1)} %get-tuple-element.43), channel_id=1, source_target_pairs={{0,16},{16,32},{32,48},{48,64},{64,80},{80,96},{96,112},{112,0},{1... | collective-permute-start | bytes 196616 | tf_op jit(solution)/shard_map/ppermute | solution.py:22
  305.5 7.1 %collective-permute-start.25 = (f32[1,16,1024]{2,1,0:T(8,128)S(1)}, f32[1,16,1024]{2,1,0:T(8,128)S(1)}, u32[]{:S(2)}, u32[]{:S(2)}) collective-permute-start(f32[1,16,1024]{2,1,0:T(8,128)S(1)} %get-tuple-element.44), channel_id=1, source_target_pairs={{16,0},{32,16},{48,32},{64,48},{80,64},{96,80},{112,96},{0,112},{1... | collective-permute-start | bytes 196616 | tf_op jit(solution)/shard_map/ppermute | solution.py:24
  312.8 7.7 %collective-permute-start.26 = (f32[34,1,1024]{2,1,0:T(1,128)S(1)}, f32[34,1,1024]{2,1,0:T(1,128)S(1)}, u32[]{:S(2)}, u32[]{:S(2)}) collective-permute-start(f32[34,1,1024]{2,1,0:T(1,128)S(1)} %get-tuple-element.29), channel_id=1, source_target_pairs={{0,1},{1,2},{2,3},{3,4},{4,5},{5,6},{6,7},{7,8},{8,9},{9,10},{10,1... | collective-permute-start | bytes 417800 | tf_op jit(solution)/shard_map/ppermute | solution.py:22
  312.9 8.0 %collective-permute-start.27 = (f32[34,1,1024]{2,1,0:T(1,128)S(1)}, f32[34,1,1024]{2,1,0:T(1,128)S(1)}, u32[]{:S(2)}, u32[]{:S(2)}) collective-permute-start(f32[34,1,1024]{2,1,0:T(1,128)S(1)} %get-tuple-element.30), channel_id=1, source_target_pairs={{1,0},{2,1},{3,2},{4,3},{5,4},{6,5},{7,6},{8,7},{9,8},{10,9},{11,1... | collective-permute-start | bytes 417800 | tf_op jit(solution)/shard_map/ppermute | solution.py:24
  328.4 7.2 %collective-permute-start.28 = (f32[1,16,1024]{2,1,0:T(8,128)S(1)}, f32[1,16,1024]{2,1,0:T(8,128)S(1)}, u32[]{:S(2)}, u32[]{:S(2)}) collective-permute-start(f32[1,16,1024]{2,1,0:T(8,128)S(1)} %get-tuple-element.37), channel_id=1, source_target_pairs={{0,16},{16,32},{32,48},{48,64},{64,80},{80,96},{96,112},{112,0},{1... | collective-permute-start | bytes 196616 | tf_op jit(solution)/shard_map/ppermute | solution.py:22
  328.5 7.1 %collective-permute-start.29 = (f32[1,16,1024]{2,1,0:T(8,128)S(1)}, f32[1,16,1024]{2,1,0:T(8,128)S(1)}, u32[]{:S(2)}, u32[]{:S(2)}) collective-permute-start(f32[1,16,1024]{2,1,0:T(8,128)S(1)} %get-tuple-element.38), channel_id=1, source_target_pairs={{16,0},{32,16},{48,32},{64,48},{80,64},{96,80},{112,96},{0,112},{1... | collective-permute-start | bytes 196616 | tf_op jit(solution)/shard_map/ppermute | solution.py:24
  335.8 8.2 %collective-permute-start.30 = (f32[34,1,1024]{2,1,0:T(1,128)S(1)}, f32[34,1,1024]{2,1,0:T(1,128)S(1)}, u32[]{:S(2)}, u32[]{:S(2)}) collective-permute-start(f32[34,1,1024]{2,1,0:T(1,128)S(1)} %get-tuple-element.27), channel_id=1, source_target_pairs={{0,1},{1,2},{2,3},{3,4},{4,5},{5,6},{6,7},{7,8},{8,9},{9,10},{10,1... | collective-permute-start | bytes 417800 | tf_op jit(solution)/shard_map/ppermute | solution.py:22
  335.9 8.4 %collective-permute-start.31 = (f32[34,1,1024]{2,1,0:T(1,128)S(1)}, f32[34,1,1024]{2,1,0:T(1,128)S(1)}, u32[]{:S(2)}, u32[]{:S(2)}) collective-permute-start(f32[34,1,1024]{2,1,0:T(1,128)S(1)} %get-tuple-element.28), channel_id=1, source_target_pairs={{1,0},{2,1},{3,2},{4,3},{5,4},{6,5},{7,6},{8,7},{9,8},{10,9},{11,1... | collective-permute-start | bytes 417800 | tf_op jit(solution)/shard_map/ppermute | solution.py:24
  352.9 45.2 %copy-start.4 = (f32[32,16,1024]{2,1,0:T(8,128)}, f32[32,16,1024]{2,1,0:T(8,128)S(1)}, u32[]{:S(2)}) copy-start(f32[32,16,1024]{2,1,0:T(8,128)S(1)} %get-tuple-element.6) | copy-start | bytes 6291460
  352.9 7.7 %collective-permute-start.32 = (f32[2,16,1024]{2,1,0:T(8,128)S(1)}, f32[2,16,1024]{2,1,0:T(8,128)S(1)}, u32[]{:S(2)}, u32[]{:S(2)}) collective-permute-start(f32[2,16,1024]{2,1,0:T(8,128)S(1)} %get-tuple-element.35), channel_id=1, source_target_pairs={{0,16},{16,32},{32,48},{48,64},{64,80},{80,96},{96,112},{112,0},{1... | collective-permute-start | bytes 393224 | tf_op jit(solution)/shard_map/ppermute | solution.py:22
  353.0 7.6 %collective-permute-start.33 = (f32[2,16,1024]{2,1,0:T(8,128)S(1)}, f32[2,16,1024]{2,1,0:T(8,128)S(1)}, u32[]{:S(2)}, u32[]{:S(2)}) collective-permute-start(f32[2,16,1024]{2,1,0:T(8,128)S(1)} %get-tuple-element.36), channel_id=1, source_target_pairs={{16,0},{32,16},{48,32},{64,48},{80,64},{96,80},{112,96},{0,112},{1... | collective-permute-start | bytes 393224 | tf_op jit(solution)/shard_map/ppermute | solution.py:24
  361.7 15.9 %collective-permute-start.34 = (f32[36,2,1024]{2,1,0:T(2,128)}, f32[36,2,1024]{2,1,0:T(2,128)S(1)}, u32[]{:S(2)}, u32[]{:S(2)}) collective-permute-start(f32[36,2,1024]{2,1,0:T(2,128)} %get-tuple-element.25), channel_id=1, source_target_pairs={{0,1},{1,2},{2,3},{3,4},{4,5},{5,6},{6,7},{7,8},{8,9},{9,10},{10,1... | collective-permute-start | bytes 884744 | tf_op jit(solution)/shard_map/ppermute | solution.py:22
  361.7 15.9 %collective-permute-start.35 = (f32[36,2,1024]{2,1,0:T(2,128)}, f32[36,2,1024]{2,1,0:T(2,128)S(1)}, u32[]{:S(2)}, u32[]{:S(2)}) collective-permute-start(f32[36,2,1024]{2,1,0:T(2,128)} %get-tuple-element.26), channel_id=1, source_target_pairs={{1,0},{2,1},{3,2},{4,3},{5,4},{6,5},{7,6},{8,7},{9,8},{10,9},{11,1... | collective-permute-start | bytes 884744 | tf_op jit(solution)/shard_map/ppermute | solution.py:24
  409.1 3.1 copy-start.10
  (2 other events, 4.0 us)
where the time goes:
time: 438 us; the launch traced here: 430 us
  other arithmetic  176 us (40%)
  starting transfers between devices  110 us (25%)
  local copies, waits for them, and re-layouts  73.2 us (17%)
  waiting for transfers between devices  34.3 us (8%)
  matrix products  17.2 us (4%)
  blocking collectives  16.2 us (4%)
    ppermute x18, starting transfers between devices, padded_2(): lax.ppermute(head, axis, [((i + 1) % count, i) for i in range(count)])  97.6 us
    add x1, other arithmetic, rk_first(): return start + time_step * rate  32.8 us
    add x1, other arithmetic, rk_second(): return 0.75 * start + 0.25 * (first_section + time_step * rate)  32.6 us
    add x1, other arithmetic, rk_third(): return start / 3.0 + 2.0 / 3.0 * (second_section + time_step * rate)  32.4 us
    sub x3, other arithmetic, sweep_once(): return centre - pseudo_step * sign_field * (slope_norm - 1.0)  22.4 us
    slice x15, local copies, waits for them, and re-layouts, weno_periodic(): slopes = [jnp.roll(differences, 3 - offset, axis=2) for offset in range(6)]  21.9 us
    ppermute x18, waiting for transfers between devices, padded_2(): lax.ppermute(head, axis, [((i + 1) % count, i) for i in range(count)])  17.5 us
    ppermute x18, waiting for transfers between devices, padded_2(): lax.ppermute(tail, axis, [(i, (i + 1) % count) for i in range(count)])  16.9 us
  transfers between devices with their start and end apart: 37, of which 22 were waited for; matrix products, arithmetic and copies ran while one was open for 11% of the time, Pallas kernels for 0%

commit v1 on v0

v1 whole, which is shorter than its diff:
```python
import functools

import jax
import jax.numpy as jnp
from jax import lax
from jax.experimental import pallas as pl
from jax.experimental.pallas import tpu as pltpu
from jax.sharding import PartitionSpec as P

SWEEPS = 4
TIME_STEP = 0.25
PSEUDO_STEP = 0.3
EPS = 1e-06
FRONT = 1.5
WIDE = SWEEPS + 2

ROWS, LANES = 8, 128
HIGH = lax.Precision.HIGHEST


def params(mib):
    return pltpu.CompilerParams(vmem_limit_bytes=mib * 2**20)


def f32(*shape):
    return jax.ShapeDtypeStruct(shape, jnp.float32)


def cost(vector_ops):
    return pl.CostEstimate(flops=vector_ops * 1024, bytes_accessed=2**23, transcendentals=0)


def shifted(col, step):
    lane = lax.broadcasted_iota(jnp.int32, (ROWS, LANES), 1)
    turned = pltpu.roll(col, (-step) % LANES, 1)
    if step > 0:
        return jnp.where(lane >= LANES - step, pltpu.roll(turned, ROWS - 1, 0), turned)
    return jnp.where(lane < -step, pltpu.roll(turned, 1, 0), turned)


def inverse(values):
    return pl.reciprocal(values, approx=True)


def correction(rough1, rough2, rough3, third1, third2):
    r1, r2, r3 = inverse(rough1), inverse(rough2), inverse(rough3)
    w1 = r1 * r1
    w12 = w1 + 6.0 * (r2 * r2)
    w3 = 3.0 * (r3 * r3)
    return (4.0 * w1 * third1 + (w3 - w12) * third2) * inverse(w12 + w3)


def upwind_part(speed, central, corr):
    return speed * central + jnp.abs(speed) * corr


class March:
    def __init__(self, get):
        self.get = get
        self.made = {}

    def once(self, name, j, make):
        key = (name, j)
        if key not in self.made:
            self.made[key] = make()
        return self.made[key]

    def p(self, j):
        return self.once("p", j, lambda: self.get(j))

    def d(self, j):
        return self.once("d", j, lambda: self.p(j + 1) - self.p(j))

    def curve(self, j):
        return self.once("c", j, lambda: self.d(j) - self.d(j - 1))

    def gap(self, j):
        return self.once("g", j, lambda: self.curve(j + 1) - self.curve(j))

    def third(self, j):
        return self.once("t", j, lambda: self.gap(j) - self.gap(j - 1))

    def base(self, j):
        return self.once("h", j, lambda: (4.0 / 3.0) * (self.gap(j) * self.gap(j)) + EPS)

    def cross(self, j):
        return self.once("x", j, lambda: self.curve(j) * self.curve(j + 1))

    def twice(self, j):
        return self.once("a", j, lambda: (self.curve(j) + self.curve(j)) * self.curve(j))

    def less(self, j):
        return self.once("l", j, lambda: self.base(j) - self.cross(j))

    def mid(self, j):
        return self.once("m", j, lambda: self.base(j) + self.cross(j))

    def up(self, j):
        return self.once("u", j, lambda: self.less(j) + self.twice(j + 1))

    def down(self, j):
        return self.once("v", j, lambda: self.less(j) + self.twice(j))

    def central(self, i):
        return 6.0 * (self.p(i + 1) - self.p(i - 1)) - (self.gap(i) + self.gap(i - 1))

    def part(self, i, speed):
        minus = speed < 0
        corr = correction(
            jnp.where(minus, self.up(i - 2), self.down(i + 1)),
            jnp.where(minus, self.mid(i - 1), self.mid(i)),
            jnp.where(minus, self.down(i), self.up(i - 1)),
            jnp.where(minus, self.third(i - 1), self.third(i + 1)),
            self.third(i),
        )
        return upwind_part(speed, self.central(i), corr)


def depth_part(col, speed):
    before, after = shifted(col, -1), shifted(col, 1)
    here = (after - col) - (col - before)
    m1, p1 = shifted(here, -1), shifted(here, 1)
    m2, p2 = shifted(here, -2), shifted(here, 2)
    minus = speed < 0
    a = jnp.where(minus, m2, p2)
    b = jnp.where(minus, m1, p1)
    d = jnp.where(minus, p1, m1)
    g1, g2, g3 = b - a, here - b, d - here
    corr = correction(
        (4.0 / 3.0) * (g1 * g1) + EPS + b * (b + g1),
        (4.0 / 3.0) * (g2 * g2) + EPS + b * here,
        (4.0 / 3.0) * (g3 * g3) + EPS + here * (here - g3),
        g2 - g1,
        g3 - g2,
    )
    return upwind_part(speed, 6.0 * (after - before) - (p1 - m1), corr)


def loop(low, high, body):
    def step(i, carry):
        body(i)
        return carry

    lax.fori_loop(low, high, step, 0)


def pack_velocity(rows_ref, out_ref):
    def to(g):
        for c in range(3):
            for r in range(10):
                block, low = (g, r - 1) if 1 <= r <= 8 else ((g + 15, 7) if r == 0 else (g + 1, 0))
                start = c * 512 + lax.rem(block, 16) * 32 + low
                out_ref[g, pl.ds((c * 10 + r) * 4, 4), :] = rows_ref[pl.ds(start, 4, stride=8), :]

    loop(0, 16, to)


def unpack_level(rows_ref, p_ref, ylo_ref, yhi_ref):
    def to(x):
        for y in range(16):
            col = rows_ref[pl.ds(x * 128 + (y // 8) * 64 + y % 8, 8, stride=8), :]
            p_ref[x, y] = col
            if y < 3:
                ylo_ref[x, y] = col
            if y >= 13:
                yhi_ref[x, y - 13] = col

    loop(0, 32, to)


def refine_velocity(lo_ref, mid_ref, hi_ref, band_ref, v_ref, fine):
    k = lax.broadcasted_iota(jnp.int32, (256, 256), 0)
    n = lax.broadcasted_iota(jnp.int32, (256, 256), 1)
    beside = jnp.where(n % 2 == 0, n // 2 - 1, n // 2 + 1)
    beside = jnp.where(beside < 0, 255, jnp.where(beside > 127, 128, beside))
    table = jnp.where(k == n // 2, 0.75, 0.0) + jnp.where(k == beside, 0.25, 0.0)
    row = lax.broadcasted_iota(jnp.int32, (120, 128), 0) % 4
    lane = lax.broadcasted_iota(jnp.int32, (120, 128), 1)

    def along_z(slot, plane):
        after = jnp.where(row == 3, pltpu.roll(plane, 3, 0), pltpu.roll(plane, 119, 0))
        prior = jnp.where(row == 0, pltpu.roll(plane, 117, 0), pltpu.roll(plane, 1, 0))
        wide = jnp.concatenate([plane, jnp.where(lane < 64, after, prior)], axis=1)
        out = jnp.dot(wide, table, precision=HIGH, preferred_element_type=jnp.float32)
        fine[slot, pl.ds(0, 120, stride=2), :] = out[:, :128]
        fine[slot, pl.ds(1, 120, stride=2), :] = out[:, 128:]

    along_z(0, lo_ref[...])
    loop(0, 16, lambda i: along_z(i + 1, mid_ref[i]))
    along_z(17, hi_ref[...])

    def along_xy(i):
        band = band_ref[lax.div(i, 8)]
        for c in range(3):
            for odd in range(2):
                line = []
                for r in range(10):
                    at = pl.ds((c * 10 + r) * 8, 8)
                    line.append(0.75 * fine[i + 1, at, :] + 0.25 * fine[i + 2 * odd, at, :])
                for y in range(16):
                    m = y // 2 + 1
                    v_ref[c, 2 * i + odd, y] = (0.75 * line[m] + 0.25 * line[m - 1 + 2 * (y % 2)]) * band

    loop(0, 16, along_xy)


def inner_rate(p_ref, v_ref, acc_ref):
    def x_line(y):
        march = March(lambda x: p_ref[x, y])
        for x in range(32):
            if 3 <= x < 29:
                acc_ref[x, y] = march.part(x, v_ref[0, x, y])
            else:
                acc_ref[x, y] = jnp.zeros((ROWS, LANES), jnp.float32)

    def y_line(x):
        march = March(lambda y: p_ref[x, y])
        for y in range(16):
            total = acc_ref[x, y] + depth_part(march.p(y), v_ref[2, x, y])
            if 3 <= y < 13:
                total = total + march.part(y, v_ref[1, x, y])
            acc_ref[x, y] = total

    loop(0, 16, x_line)
    loop(0, 32, y_line)


def section(start, current, rate, number):
    if number == 0:
        return current + rate
    if number == 1:
        return 0.75 * start + 0.25 * (current + rate)
    return start * (1.0 / 3.0) + (2.0 / 3.0) * (current + rate)


def edge_rate(number, edge, acc_ref, start_ref, p_ref, v_ref, xlo_ref, xhi_ref, ylo_ref, yhi_ref, new_ref, nlo_ref, nhi_ref, side):
    def x_line(y):
        low = March(lambda x: xlo_ref[x + 3, y] if x < 0 else p_ref[x, y])
        high = March(lambda x: xhi_ref[x - 32, y] if x >= 32 else p_ref[x, y])
        for k in range(3):
            side[k, y] = low.part(k, v_ref[0, k, y])
            side[k + 3, y] = high.part(29 + k, v_ref[0, 29 + k, y])

    loop(0, 16, x_line)

    def y_line(x, side_x):
        low = March(lambda y: ylo_ref[x, y + 3] if y < 0 else p_ref[x, y])
        high = March(lambda y: yhi_ref[x, y - 16] if y >= 16 else p_ref[x, y])
        for y in range(16):
            rate = acc_ref[x, y]
            if side_x is not None:
                rate = rate + side[side_x, y]
            if y < 3:
                rate = rate + low.part(y, v_ref[1, x, y])
            if y >= 13:
                rate = rate + high.part(y, v_ref[1, x, y])
            start = None if number == 0 else start_ref[x, y]
            new = section(start, p_ref[x, y], rate, number)
            new_ref[x, y] = new
            if y < edge:
                nlo_ref[x, y] = new
            if y >= 16 - edge:
                nhi_ref[x, y - (16 - edge)] = new

    loop(0, 3, lambda x: y_line(x, x))
    loop(3, 29, lambda x: y_line(x, None))
    loop(29, 32, lambda x: y_line(x, x - 26))


def finish(adv_ref, xlo_ref, xhi_ref, ylo_ref, yhi_ref, clo_ref, chi_ref, new_ref, send_ref, q0, q1, push, nx, ny, nz, lump):
    w = WIDE
    size_x, size_y = 32 + 2 * w, 16 + 2 * w

    def place(x, y, col):
        q0[x, y] = col
        push[x, y] = (PSEUDO_STEP * col) * lax.rsqrt(col * col + 1.0)

    def fill_mid(x):
        for y in range(w):
            place(x + w, y, ylo_ref[x, y])
            place(x + w, y + 16 + w, yhi_ref[x, y])
        for y in range(16):
            place(x + w, y + w, adv_ref[x, y])

    def fill_side(x):
        for y in range(w):
            place(x, y, clo_ref[x, y])
            place(x, y + 16 + w, chi_ref[x, y])
            place(x + 32 + w, y, clo_ref[x + w, y])
            place(x + 32 + w, y + 16 + w, chi_ref[x + w, y])
        for y in range(16):
            place(x, y + w, xlo_ref[x, y])
            place(x + 32 + w, y + w, xhi_ref[x, y])

    loop(0, 32, fill_mid)
    loop(0, w, fill_side)

    def sweep(src, dst, k):
        def line(x):
            cols = {}

            def at(y):
                if y not in cols:
                    cols[y] = src[x, y]
                return cols[y]

            for y in range(k, size_y - k):
                col = at(y)
                c = push[x, y]
                sign = jnp.where(c > 0, 1.0, -1.0)
                here = sign * col
                total = None
                for pair in (
                    (src[x - 1, y], src[x + 1, y]),
                    (at(y - 1), at(y + 1)),
                    (shifted(col, -1), shifted(col, 1)),
                ):
                    rise = jnp.maximum(here - jnp.minimum(sign * pair[0], sign * pair[1]), 0.0)
                    total = rise * rise if total is None else total + rise * rise
                slope = total * lax.rsqrt(jnp.maximum(total, 1e-30))
                dst[x, y] = (col + c) - c * slope

        loop(k, size_x - k, line)

    buffers = (q0, q1)
    for k in range(SWEEPS):
        sweep(buffers[k % 2], buffers[(k + 1) % 2], k + 1)
    last = buffers[SWEEPS % 2]

    def normals(x):
        xs = x + w - 1
        cols = {}

        def at(y):
            if y not in cols:
                cols[y] = last[xs, y + w]
            return cols[y]

        across, along, deep = {}, {}, {}
        for y in range(-1, 17):
            gx = last[xs + 1, y + w] - last[xs - 1, y + w]
            gy = at(y + 1) - at(y - 1)
            gz = shifted(at(y), 1) - shifted(at(y), -1)
            scale = lax.rsqrt(gx * gx + gy * gy + gz * gz + 4.0)
            across[y], along[y], deep[y] = gx * scale, gy * scale, gz * scale
        for j in range(8):
            a, b = 2 * j, 2 * j + 1
            nx[x, j] = across[a] + across[b]
            ny[x, j] = (along[b] + along[b + 1]) - (along[a - 1] + along[a])
            nz[x, j] = deep[a] + deep[b]

    loop(0, 34, normals)

    def gather(i):
        a, b = 2 * i + 1, 2 * i + 2
        for j in range(8):
            deep = nz[a, j] + nz[b, j]
            total = (nx[b, j] + nx[b + 1, j]) - (nx[a - 1, j] + nx[a, j]) + (ny[a, j] + ny[b, j])
            lump[pl.ds(i * 64 + j * 8, 8), :] = total + (shifted(deep, 1) - shifted(deep, -1))
            share = None
            for x in range(2):
                for y in range(2):
                    xx, yy = 2 * i + x, 2 * j + y
                    col = last[xx + w, yy + w]
                    new_ref[pl.ds(xx * 128 + (yy // 8) * 64 + yy % 8, 8, stride=8), :] = col
                    bend = jnp.tanh(col * (1.0 / FRONT))
                    share = bend if share is None else share + bend
            lump[pl.ds(1024 + i * 64 + j * 8, 8), :] = share

    loop(0, 16, gather)

    k = lax.broadcasted_iota(jnp.int32, (256, 128), 0)
    n = lax.broadcasted_iota(jnp.int32, (256, 128), 1)
    table = jnp.where(lax.div(k, 2) == n, 1.0 / 16.0, 0.0)

    def restrict(i):
        for kind in range(2):
            base = kind * 1024 + i * 64
            left = [lump[pl.ds(base + 2 * z, 8, stride=8), :] for z in range(4)]
            right = [lump[pl.ds(base + 2 * z + 1, 8, stride=8), :] for z in range(4)]
            wide = jnp.concatenate([jnp.concatenate(left, axis=0), jnp.concatenate(right, axis=0)], axis=1)
            out = jnp.dot(wide, table, precision=HIGH, preferred_element_type=jnp.float32)
            send_ref[i, pl.ds(kind * 32, 32), :] = out + 0.5 if kind else out

    loop(0, 16, restrict)


def call(kernel, outs, *args, scratch=(), mib=48, ops=1000, name=None):
    return pl.pallas_call(
        kernel,
        out_shape=outs,
        in_specs=[pl.BlockSpec(memory_space=pltpu.VMEM)] * len(args),
        out_specs=jax.tree.map(lambda _: pl.BlockSpec(memory_space=pltpu.VMEM), outs),
        scratch_shapes=[pltpu.VMEM(s, jnp.float32) for s in scratch],
        compiler_params=params(mib),
        cost_estimate=cost(ops),
        name=name,
    )(*args)


def moved(values, axis, step):
    count = lax.axis_size(axis)
    return lax.ppermute(values, axis, [(i, (i + step) % count) for i in range(count)])


def star(p, ylo, yhi, width):
    return (
        moved(p[32 - width :], "gx", 1),
        moved(p[:width], "gx", -1),
        moved(yhi, "gy", 1),
        moved(ylo, "gy", -1),
    )


def per_device(level_set, flow_velocity, band_mask):
    col = (ROWS, LANES)
    block = f32(32, 16, *col)
    level_rows = level_set.reshape(32, 2, 8, 8, 128).transpose(0, 1, 3, 2, 4).reshape(4096, 128)
    flow_rows = flow_velocity.reshape(3, 16, 8, 4, 128).transpose(0, 1, 3, 2, 4).reshape(1536, 128)
    band = band_mask.reshape(2, 8, 8).astype(jnp.float32) * (-TIME_STEP / 12.0)
    band = jnp.broadcast_to(band[..., None], (2, 8, 8, 16)).reshape(2, 8, 128)

    send = call(pack_velocity, f32(16, 120, 128), flow_rows, name="pack", mib=8)
    coarse = lax.all_to_all(send, "gy", split_axis=0, concat_axis=0, tiled=True)
    start, ylo, yhi = call(
        unpack_level, (block, f32(32, 3, *col), f32(32, 3, *col)), level_rows, name="unpack", mib=8
    )
    halo = star(start, ylo, yhi, 3)
    below, above = moved(coarse[15], "gx", 1), moved(coarse[0], "gx", -1)
    velocity = call(
        refine_velocity, f32(3, 32, 16, *col), below, coarse, above, band, scratch=[(18, 240, 128)], name="refine", mib=24
    )
    current = start
    for number in range(3):
        acc = call(inner_rate, block, current, velocity, name="inner", mib=24, ops=512 * 140)
        edge = WIDE if number == 2 else 3
        current, ylo, yhi = call(
            functools.partial(edge_rate, number, edge),
            (block, f32(32, edge, *col), f32(32, edge, *col)),
            acc, start, current, velocity, *halo,
            scratch=[(6, 16, *col)],
            name="edge", mib=24, ops=512 * 30,
        )
        halo = star(current, ylo, yhi, edge)
    xlo, xhi, ylo, yhi = halo
    sides = jnp.concatenate([xlo, xhi], axis=0)
    clo = moved(sides[:, 16 - WIDE :], "gy", 1)
    chi = moved(sides[:, :WIDE], "gy", -1)
    ext = (32 + 2 * WIDE, 16 + 2 * WIDE, *col)
    new_rows, packed = call(
        finish,
        (f32(4096, 128), f32(16, 64, 128)),
        current, xlo, xhi, ylo, yhi, clo, chi,
        scratch=[ext, ext, ext] + [(34, 8, *col)] * 3 + [(2048, 128)],
        name="finish", mib=48, ops=512 * 250,
    )
    returned = lax.all_to_all(packed, "gy", split_axis=0, concat_axis=0, tiled=True).reshape(16, 2, 4, 8, 128)
    new_level = new_rows.reshape(32, 2, 8, 8, 128).transpose(0, 1, 3, 2, 4).reshape(32, 16, 1024)
    flows = [returned[:, k].transpose(0, 2, 1, 3).reshape(1, 128, 512) for k in range(2)]
    return (new_level, flows[0], flows[1])


def solution(mesh):
    placed = (P("gx", "gy", None), P(None, ("gx", "gy"), None, None), P("gx", "gy", None))
    return jax.shard_map(
        per_device,
        mesh=mesh,
        in_specs=placed,
        out_specs=(P("gx", "gy", None), P(("gx", "gy"), None, None), P(("gx", "gy"), None, None)),
        check_vma=False,
    )
```

time: 438 us -> 204 us (0.47); the launches traced: 430 us -> 203 us
  other arithmetic: 176 us -> 0.02 us
  Pallas kernels: 0 us -> 94.1 us
  local copies, waits for them, and re-layouts: 73.2 us -> 6.86 us
  starting transfers between devices: 110 us -> 51.5 us
  matrix products: 17.2 us -> 0 us
    add x4 -> x0, other arithmetic: 103 us -> none  [the longest x1 32.8 us: rk_first(): return start + time_step * rate]
    pallas_call x0 -> x10, Pallas kernels: none -> 94.1 us  [call(): pl.pallas_call(kernel, out_shape=outs, in_specs=[pl.BlockSpec(memory_spac...]
    ppermute x36 -> x20, starting transfers between devices: 104 us -> 43.7 us  [moved(): lax.ppermute(values, axis, [(i, (i + step) % count) for i in range(count)])]
    slice x51 -> x5, local copies, waits for them, and re-layouts: 40.8 us -> 0.91 us  [the longest x4 0.87 us: star(): p[:width]]
    sub x11 -> x0, other arithmetic: 29.7 us -> none  [the longest x3 22.4 us: sweep_once(): return centre - pseudo_step * sign_field * (slope_norm - 1.0)]
    mul x3 -> x1, other arithmetic: 24.1 us -> 0.02 us  [per_device(): band = band_mask.reshape(2, 8, 8).astype(jnp.float32) * (-TIME_STEP / 12.0)]
    dot_general x3 -> x0, matrix products: 17.2 us -> none  [the longest x1 13.6 us: fine_velocity(): jnp.dot(refined, table, precision=lax.Precision.HIGHEST, preferred_elemen...]
    reshape x4 -> x2, local copies, waits for them, and re-layouts: 15.3 us -> 1.75 us  [the longest x1 0.92 us: per_device(): band = jnp.broadcast_to(band[..., None], (2, 8, 8, 16)).reshape(2, 8, 128)]
  transfers between devices with their start and end apart: 37 -> 21, of which waited for: 22 -> 5; matrix products, arithmetic and copies ran while one was open for 11% -> 2% of each run, Pallas kernels for 0% -> 24%
where the time goes in v1:
time: 204 us; the launch traced here: 203 us
  Pallas kernels  94.1 us (46%)
  starting transfers between devices  51.5 us (25%)
  waiting for transfers between devices  34.6 us (17%)
  blocking collectives  14.6 us (7%)
  local copies, waits for them, and re-layouts  6.86 us (3%)
    pallas_call x10, Pallas kernels, call(): pl.pallas_call(kernel, out_shape=outs, in_specs=[pl.BlockSpec(memory_spac...  94.1 us
    ppermute x20, starting transfers between devices, moved(): lax.ppermute(values, axis, [(i, (i + step) % count) for i in range(count)])  43.7 us
    ppermute x20, waiting for transfers between devices, moved(): lax.ppermute(values, axis, [(i, (i + step) % count) for i in range(count)])  29.5 us
    all_to_all x1, blocking collectives, per_device(): lax.all_to_all(packed, 'gy', split_axis=0, concat_axis=0, tiled=True)  14.6 us
    all_to_all x1, starting transfers between devices, per_device(): coarse = lax.all_to_all(send, 'gy', split_axis=0, concat_axis=0, tiled=True)  7.89 us
    all_to_all x1, waiting for transfers between devices, per_device(): coarse = lax.all_to_all(send, 'gy', split_axis=0, concat_axis=0, tiled=True)  5.15 us
  transfers between devices with their start and end apart: 21, of which 5 were waited for; matrix products, arithmetic and copies ran while one was open for 2% of the time, Pallas kernels for 24%

profile of v1, /device:TPU:1, one launch (start us, length us, event | category | flops | bytes accessed | tf_op | source)
XLA Modules:
  0.0 202.6 jit_solution(8295119847818603937)
XLA Ops:
  0.6 1.1 copy-done.1
  1.8 1.3 pack.1
  3.0 7.9 %all-to-all-start = ((f32[16,120,128]{2,1,0:T(8,128)}), f32[16,120,128]{2,1,0:T(8,128)S(1)}, u32[]{:S(2)}, u32[]{:S(2)}) async-start(f32[16,120,128]{2,1,0:T(8,128)} %pack.1), calls=%async_computation | async-start | bytes 1966080 | tf_op jit(solution)/shard_map/all_to_all | solution.py:424
  10.9 1.6 copy-done
  12.5 1.4 unpack.1
  13.9 0.8 fusion.3
  14.7 4.9 %collective-permute-start.3 = (f32[3,16,8,128]{3,2,1,0:T(8,128)}, f32[3,16,8,128]{3,2,1,0:T(8,128)}, u32[]{:S(2)}, u32[]{:S(2)}) collective-permute-start(f32[3,16,8,128]{3,2,1,0:T(8,128)} %get-tuple-element.37), channel_id=1, source_target_pairs={{0,112},{16,0},{32,16},{48,32},{64,48},{80,64},{96,80},{112,96},{1... | collective-permute-start | bytes 589832 | tf_op jit(solution)/shard_map/ppermute | solution.py:403
  19.6 1.3 collective-permute-start.4
  20.9 0.0 collective-permute-start.5
  20.9 5.1 %all-to-all-done.mid_ref = f32[16,120,128]{2,1,0:T(8,128)S(1)} async-done(((f32[16,120,128]{2,1,0:T(8,128)}), f32[16,120,128]{2,1,0:T(8,128)S(1)}, u32[]{:S(2)}, u32[]{:S(2)}) %all-to-all-start) | async-done | bytes 983072 | tf_op jit(solution)/shard_map/all_to_all | solution.py:424
  26.0 0.6 slice_bitcast_fusion.2
  26.7 5.0 %collective-permute-start.1 = (f32[120,128]{1,0:T(8,128)S(1)}, f32[120,128]{1,0:T(8,128)S(1)}, u32[]{:S(2)}, u32[]{:S(2)}) collective-permute-start(f32[120,128]{1,0:T(8,128)S(1)} %get-tuple-element.39), channel_id=1, source_target_pairs={{0,112},{16,0},{32,16},{48,32},{64,48},{80,64},{96,80},{112,96},{1... | collective-permute-start | bytes 184328 | tf_op jit(solution)/shard_map/ppermute | solution.py:403
  31.7 4.5 %collective-permute-done.1.hi_ref = f32[120,128]{1,0:T(8,128)S(1)} collective-permute-done((f32[120,128]{1,0:T(8,128)S(1)}, f32[120,128]{1,0:T(8,128)S(1)}, u32[]{:S(2)}, u32[]{:S(2)}) %collective-permute-start.1) | collective-permute-done | bytes 61472 | tf_op jit(solution)/shard_map/ppermute | solution.py:403
  36.1 0.0 collective-permute-start
  36.1 0.1 mul.15
  36.2 0.7 broadcast_in_dim.2
  36.9 0.9 reshape.50.band_ref
  37.9 6.0 %collective-permute-done.lo_ref = f32[120,128]{1,0:T(8,128)} collective-permute-done((f32[120,128]{1,0:T(8,128)}, f32[120,128]{1,0:T(8,128)}, u32[]{:S(2)}, u32[]{:S(2)}) %collective-permute-start) | collective-permute-done | bytes 61472 | tf_op jit(solution)/shard_map/ppermute | solution.py:403
  43.9 7.0 %refine.1.v_ref = f32[3,32,16,8,128]{4,3,2,1,0:T(8,128)S(1)} custom-call(f32[120,128]{1,0:T(8,128)} %collective-permute-done.lo_ref, f32[16,120,128]{2,1,0:T(8,128)S(1)} %all-to-all-done.mid_ref, f32[120,128]{1,0:T(8,128)S(1)} %collective-permute-done.1.hi_ref, f32[2,8,128]{2,1,0:T(8,128)S(1)} %reshape.50.band_ref), custom_call_target="tpu_custom_call" | custom-call | flops 1024000 | bytes 8388608 | tf_op jit(solution)/shard_map/refine/pallas_call | solution.py:389
  50.9 13.5 %inner.3.acc_ref = f32[32,16,8,128]{3,2,1,0:T(8,128)S(1)} custom-call(f32[32,16,8,128]{3,2,1,0:T(8,128)S(1)} %get-tuple-element.17.p_ref.start_ref, f32[3,32,16,8,128]{4,3,2,1,0:T(8,128)S(1)} %refine.1.v_ref), custom_call_target="tpu_custom_call" | custom-call | flops 73400320 | bytes 8388608 | tf_op jit(solution)/shard_map/inner/pallas_call | solution.py:389
  64.4 0.0 collective-permute-done.3.xhi_ref
  64.4 0.0 collective-permute-done.5.yhi_ref
  64.4 4.2 %edge.3 = (f32[32,16,8,128]{3,2,1,0:T(8,128)S(1)}, f32[32,3,8,128]{3,2,1,0:T(8,128)S(1)}, f32[32,3,8,128]{3,2,1,0:T(8,128)S(1)}) custom-call(f32[32,16,8,128]{3,2,1,0:T(8,128)S(1)} %inner.3.acc_ref, f32[32,16,8,128]{3,2,1,0:T(8,128)S(1)} %get-tuple-element.17.p_ref.start_ref, f32[32,16,8,128]{3,2,1,0:T(8,128)S(1)} %get-tuple-element.17.p_ref.start_ref, ...), custom_call_target="tpu_custom_call" | custom-call | flops 15728640 | bytes 8388608 | tf_op jit(solution)/shard_map/edge/pallas_call | solution.py:389
  68.6 2.7 %collective-permute-start.8 = (f32[32,3,8,128]{3,2,1,0:T(8,128)S(1)}, f32[32,3,8,128]{3,2,1,0:T(8,128)S(1)}, u32[]{:S(2)}, u32[]{:S(2)}) collective-permute-start(f32[32,3,8,128]{3,2,1,0:T(8,128)S(1)} %get-tuple-element.21), channel_id=1, source_target_pairs={{0,1},{1,2},{2,3},{3,4},{4,5},{5,6},{6,7},{7,8},{8,9},{9,10},{10,1... | collective-permute-start | bytes 1179656 | tf_op jit(solution)/shard_map/ppermute | solution.py:403
  71.3 0.0 collective-permute-start.9
  71.3 2.4 %collective-permute-start.7 = (f32[3,16,8,128]{3,2,1,0:T(8,128)S(1)}, f32[3,16,8,128]{3,2,1,0:T(8,128)S(1)}, u32[]{:S(2)}, u32[]{:S(2)}) collective-permute-start(f32[3,16,8,128]{3,2,1,0:T(8,128)S(1)} %get-tuple-element.35), channel_id=1, source_target_pairs={{0,112},{16,0},{32,16},{48,32},{64,48},{80,64},{96,80},{112,96},{1... | collective-permute-start | bytes 589832 | tf_op jit(solution)/shard_map/ppermute | solution.py:403
  73.8 13.5 %inner.4.acc_ref = f32[32,16,8,128]{3,2,1,0:T(8,128)S(1)} custom-call(f32[32,16,8,128]{3,2,1,0:T(8,128)S(1)} %get-tuple-element.20.p_ref, f32[3,32,16,8,128]{4,3,2,1,0:T(8,128)S(1)} %refine.1.v_ref), custom_call_target="tpu_custom_call" | custom-call | flops 73400320 | bytes 8388608 | tf_op jit(solution)/shard_map/inner/pallas_call | solution.py:389
  87.3 0.0 collective-permute-done.7.xhi_ref
  87.3 0.0 collective-permute-done.6.xlo_ref
  87.3 0.0 collective-permute-done.9.yhi_ref
  87.3 3.3 %edge.4 = (f32[32,16,8,128]{3,2,1,0:T(8,128)S(1)}, f32[32,3,8,128]{3,2,1,0:T(8,128)S(1)}, f32[32,3,8,128]{3,2,1,0:T(8,128)S(1)}) custom-call(f32[32,16,8,128]{3,2,1,0:T(8,128)S(1)} %inner.4.acc_ref, f32[32,16,8,128]{3,2,1,0:T(8,128)S(1)} %get-tuple-element.17.p_ref.start_ref, f32[32,16,8,128]{3,2,1,0:T(8,128)S(1)} %get-tuple-element.20.p_ref, ...), custom_call_target="tpu_custom_call" | custom-call | flops 15728640 | bytes 8388608 | tf_op jit(solution)/shard_map/edge/pallas_call | solution.py:389
  90.6 1.5 collective-permute-start.12
  92.1 1.1 collective-permute-start.13
  93.2 5.4 %collective-permute-start.11 = (f32[3,16,8,128]{3,2,1,0:T(8,128)S(1)}, f32[3,16,8,128]{3,2,1,0:T(8,128)S(1)}, u32[]{:S(2)}, u32[]{:S(2)}) collective-permute-start(f32[3,16,8,128]{3,2,1,0:T(8,128)S(1)} %get-tuple-element.33), channel_id=1, source_target_pairs={{0,112},{16,0},{32,16},{48,32},{64,48},{80,64},{96,80},{112,96},{1... | collective-permute-start | bytes 589832 | tf_op jit(solution)/shard_map/ppermute | solution.py:403
  98.6 0.0 collective-permute-start.10
  98.6 13.5 %inner.5.acc_ref = f32[32,16,8,128]{3,2,1,0:T(8,128)S(1)} custom-call(f32[32,16,8,128]{3,2,1,0:T(8,128)S(1)} %get-tuple-element.23.p_ref, f32[3,32,16,8,128]{4,3,2,1,0:T(8,128)S(1)} %refine.1.v_ref), custom_call_target="tpu_custom_call" | custom-call | flops 73400320 | bytes 8388608 | tf_op jit(solution)/shard_map/inner/pallas_call | solution.py:389
  112.2 3.3 %edge.5 = (f32[32,16,8,128]{3,2,1,0:T(8,128)S(1)}, f32[32,6,8,128]{3,2,1,0:T(8,128)S(1)}, f32[32,6,8,128]{3,2,1,0:T(8,128)S(1)}) custom-call(f32[32,16,8,128]{3,2,1,0:T(8,128)S(1)} %inner.5.acc_ref, f32[32,16,8,128]{3,2,1,0:T(8,128)S(1)} %get-tuple-element.17.p_ref.start_ref, f32[32,16,8,128]{3,2,1,0:T(8,128)S(1)} %get-tuple-element.23.p_ref, ...), custom_call_target="tpu_custom_call" | custom-call | flops 15728640 | bytes 8388608 | tf_op jit(solution)/shard_map/edge/pallas_call | solution.py:389
  115.5 0.1 fusion
  115.6 0.1 collective-permute-start.14
  115.7 5.1 %collective-permute-start.15 = (f32[6,16,8,128]{3,2,1,0:T(8,128)S(1)}, f32[6,16,8,128]{3,2,1,0:T(8,128)S(1)}, u32[]{:S(2)}, u32[]{:S(2)}) collective-permute-start(f32[6,16,8,128]{3,2,1,0:T(8,128)S(1)} %get-tuple-element.31), channel_id=1, source_target_pairs={{0,112},{16,0},{32,16},{48,32},{64,48},{80,64},{96,80},{112,96},{1... | collective-permute-start | bytes 1179656 | tf_op jit(solution)/shard_map/ppermute | solution.py:403
  120.8 1.5 collective-permute-start.16
  122.3 3.1 %collective-permute-start.17 = (f32[32,6,8,128]{3,2,1,0:T(8,128)S(1)}, f32[32,6,8,128]{3,2,1,0:T(8,128)S(1)}, u32[]{:S(2)}, u32[]{:S(2)}) collective-permute-start(f32[32,6,8,128]{3,2,1,0:T(8,128)S(1)} %get-tuple-element.28), channel_id=1, source_target_pairs={{0,15},{1,0},{2,1},{3,2},{4,3},{5,4},{6,5},{7,6},{8,7},{9,8},{10,9... | collective-permute-start | bytes 2359304 | tf_op jit(solution)/shard_map/ppermute | solution.py:403
  125.4 0.5 collective-permute-done.14.xlo_ref
  126.0 9.5 %collective-permute-start.19 = (f32[12,6,8,128]{3,2,1,0:T(8,128)S(1)}, f32[12,6,8,128]{3,2,1,0:T(8,128)S(1)}, u32[]{:S(2)}, u32[]{:S(2)}) collective-permute-start(f32[12,6,8,128]{3,2,1,0:T(8,128)S(1)} %get-tuple-element.41), channel_id=1, source_target_pairs={{0,15},{1,0},{2,1},{3,2},{4,3},{5,4},{6,5},{7,6},{8,7},{9,8},{10,9... | collective-permute-start | bytes 884744 | tf_op jit(solution)/shard_map/ppermute | solution.py:403
  135.6 18.5 %collective-permute-done.19.chi_ref = f32[12,6,8,128]{3,2,1,0:T(8,128)S(1)} collective-permute-done((f32[12,6,8,128]{3,2,1,0:T(8,128)S(1)}, f32[12,6,8,128]{3,2,1,0:T(8,128)S(1)}, u32[]{:S(2)}, u32[]{:S(2)}) %collective-permute-start.19) | collective-permute-done | bytes 294944 | tf_op jit(solution)/shard_map/ppermute | solution.py:403
  154.1 33.1 %finish.1 = (f32[4096,128]{1,0:T(8,128)}, f32[16,64,128]{2,1,0:T(8,128)S(1)}) custom-call(f32[32,16,8,128]{3,2,1,0:T(8,128)S(1)} %get-tuple-element.26.adv_ref, f32[6,16,8,128]{3,2,1,0:T(8,128)S(1)} %collective-permute-done.14.xlo_ref, f32[6,16,8,128]{3,2,1,0:T(8,128)S(1)} %collective-permute-done.15.xhi_ref, ...), custom_call_target="tpu_custom_call" | custom-call | flops 131072000 | bytes 8388608 | tf_op jit(solution)/shard_map/finish/pallas_call | solution.py:389
  187.1 14.6 %all_to_all.10 = f32[16,64,128]{2,1,0:T(8,128)S(1)} all-to-all(f32[16,64,128]{2,1,0:T(8,128)S(1)} %get-tuple-element.30), channel_id=1, replica_groups=mesh['gx'=8,'gy'=16] {'gy'}, dimensions={0} | all-to-all | bytes 1048576 | tf_op jit(solution)/shard_map/all_to_all | solution.py:457
  201.8 0.8 slice_bitcast_fusion
  (24 shorter events, 0.2 us)
Async XLA Ops:
  0.6 1.1 copy-start.1
  3.0 33.1 %copy-start.2 = (s32[2,1,64]{2,1,0:T(1,128)S(1)}, s32[2,1,64]{2,1,0:T(1,128)}, u32[]{:S(2)}) copy-start(s32[2,1,64]{2,1,0:T(1,128)} %param.5) | copy-start | bytes 1540
  3.0 23.0 %all-to-all-start = ((f32[16,120,128]{2,1,0:T(8,128)}), f32[16,120,128]{2,1,0:T(8,128)S(1)}, u32[]{:S(2)}, u32[]{:S(2)}) async-start(f32[16,120,128]{2,1,0:T(8,128)} %pack.1), calls=%async_computation | async-start | bytes 1966080 | tf_op jit(solution)/shard_map/all_to_all | solution.py:424
  10.9 1.6 copy-start
  14.7 49.7 %collective-permute-start.3 = (f32[3,16,8,128]{3,2,1,0:T(8,128)}, f32[3,16,8,128]{3,2,1,0:T(8,128)}, u32[]{:S(2)}, u32[]{:S(2)}) collective-permute-start(f32[3,16,8,128]{3,2,1,0:T(8,128)} %get-tuple-element.37), channel_id=1, source_target_pairs={{0,112},{16,0},{32,16},{48,32},{64,48},{80,64},{96,80},{112,96},{1... | collective-permute-start | bytes 589832 | tf_op jit(solution)/shard_map/ppermute | solution.py:403
  19.6 44.8 %collective-permute-start.2 = (f32[3,16,8,128]{3,2,1,0:T(8,128)}, f32[3,16,8,128]{3,2,1,0:T(8,128)}, u32[]{:S(2)}, u32[]{:S(2)}) collective-permute-start(f32[3,16,8,128]{3,2,1,0:T(8,128)} %get-tuple-element.38), channel_id=1, source_target_pairs={{0,16},{16,32},{32,48},{48,64},{64,80},{80,96},{96,112},{112,0},{1... | collective-permute-start | bytes 589832 | tf_op jit(solution)/shard_map/ppermute | solution.py:403
  19.6 44.8 %collective-permute-start.4 = (f32[32,3,8,128]{3,2,1,0:T(8,128)}, f32[32,3,8,128]{3,2,1,0:T(8,128)S(1)}, u32[]{:S(2)}, u32[]{:S(2)}) collective-permute-start(f32[32,3,8,128]{3,2,1,0:T(8,128)} %get-tuple-element.18), channel_id=1, source_target_pairs={{0,1},{1,2},{2,3},{3,4},{4,5},{5,6},{6,7},{7,8},{8,9},{9,10},{10,1... | collective-permute-start | bytes 1179656 | tf_op jit(solution)/shard_map/ppermute | solution.py:403
  20.9 43.6 %collective-permute-start.5 = (f32[32,3,8,128]{3,2,1,0:T(8,128)}, f32[32,3,8,128]{3,2,1,0:T(8,128)}, u32[]{:S(2)}, u32[]{:S(2)}) collective-permute-start(f32[32,3,8,128]{3,2,1,0:T(8,128)} %get-tuple-element.19), channel_id=1, source_target_pairs={{0,15},{1,0},{2,1},{3,2},{4,3},{5,4},{6,5},{7,6},{8,7},{9,8},{10,9... | collective-permute-start | bytes 1179656 | tf_op jit(solution)/shard_map/ppermute | solution.py:403
  26.7 9.5 %collective-permute-start.1 = (f32[120,128]{1,0:T(8,128)S(1)}, f32[120,128]{1,0:T(8,128)S(1)}, u32[]{:S(2)}, u32[]{:S(2)}) collective-permute-start(f32[120,128]{1,0:T(8,128)S(1)} %get-tuple-element.39), channel_id=1, source_target_pairs={{0,112},{16,0},{32,16},{48,32},{64,48},{80,64},{96,80},{112,96},{1... | collective-permute-start | bytes 184328 | tf_op jit(solution)/shard_map/ppermute | solution.py:403
  36.1 7.7 %collective-permute-start = (f32[120,128]{1,0:T(8,128)}, f32[120,128]{1,0:T(8,128)}, u32[]{:S(2)}, u32[]{:S(2)}) collective-permute-start(f32[120,128]{1,0:T(8,128)} %get-tuple-element.40), channel_id=1, source_target_pairs={{0,16},{16,32},{32,48},{48,64},{64,80},{80,96},{96,112},{112,0},{1... | collective-permute-start | bytes 184328 | tf_op jit(solution)/shard_map/ppermute | solution.py:403
  68.6 18.7 %collective-permute-start.8 = (f32[32,3,8,128]{3,2,1,0:T(8,128)S(1)}, f32[32,3,8,128]{3,2,1,0:T(8,128)S(1)}, u32[]{:S(2)}, u32[]{:S(2)}) collective-permute-start(f32[32,3,8,128]{3,2,1,0:T(8,128)S(1)} %get-tuple-element.21), channel_id=1, source_target_pairs={{0,1},{1,2},{2,3},{3,4},{4,5},{5,6},{6,7},{7,8},{8,9},{9,10},{10,1... | collective-permute-start | bytes 1179656 | tf_op jit(solution)/shard_map/ppermute | solution.py:403
  71.3 16.0 %collective-permute-start.9 = (f32[32,3,8,128]{3,2,1,0:T(8,128)S(1)}, f32[32,3,8,128]{3,2,1,0:T(8,128)S(1)}, u32[]{:S(2)}, u32[]{:S(2)}) collective-permute-start(f32[32,3,8,128]{3,2,1,0:T(8,128)S(1)} %get-tuple-element.22), channel_id=1, source_target_pairs={{0,15},{1,0},{2,1},{3,2},{4,3},{5,4},{6,5},{7,6},{8,7},{9,8},{10,9... | collective-permute-start | bytes 1179656 | tf_op jit(solution)/shard_map/ppermute | solution.py:403
  71.3 15.9 %collective-permute-start.7 = (f32[3,16,8,128]{3,2,1,0:T(8,128)S(1)}, f32[3,16,8,128]{3,2,1,0:T(8,128)S(1)}, u32[]{:S(2)}, u32[]{:S(2)}) collective-permute-start(f32[3,16,8,128]{3,2,1,0:T(8,128)S(1)} %get-tuple-element.35), channel_id=1, source_target_pairs={{0,112},{16,0},{32,16},{48,32},{64,48},{80,64},{96,80},{112,96},{1... | collective-permute-start | bytes 589832 | tf_op jit(solution)/shard_map/ppermute | solution.py:403
  73.8 13.5 %collective-permute-start.6 = (f32[3,16,8,128]{3,2,1,0:T(8,128)S(1)}, f32[3,16,8,128]{3,2,1,0:T(8,128)S(1)}, u32[]{:S(2)}, u32[]{:S(2)}) collective-permute-start(f32[3,16,8,128]{3,2,1,0:T(8,128)S(1)} %get-tuple-element.36), channel_id=1, source_target_pairs={{0,16},{16,32},{32,48},{48,64},{64,80},{80,96},{96,112},{112,0},{1... | collective-permute-start | bytes 589832 | tf_op jit(solution)/shard_map/ppermute | solution.py:403
  90.6 21.5 %collective-permute-start.12 = (f32[32,3,8,128]{3,2,1,0:T(8,128)S(1)}, f32[32,3,8,128]{3,2,1,0:T(8,128)S(1)}, u32[]{:S(2)}, u32[]{:S(2)}) collective-permute-start(f32[32,3,8,128]{3,2,1,0:T(8,128)S(1)} %get-tuple-element.24), channel_id=1, source_target_pairs={{0,1},{1,2},{2,3},{3,4},{4,5},{5,6},{6,7},{7,8},{8,9},{9,10},{10,1... | collective-permute-start | bytes 1179656 | tf_op jit(solution)/shard_map/ppermute | solution.py:403
  92.1 20.1 %collective-permute-start.13 = (f32[32,3,8,128]{3,2,1,0:T(8,128)S(1)}, f32[32,3,8,128]{3,2,1,0:T(8,128)S(1)}, u32[]{:S(2)}, u32[]{:S(2)}) collective-permute-start(f32[32,3,8,128]{3,2,1,0:T(8,128)S(1)} %get-tuple-element.25), channel_id=1, source_target_pairs={{0,15},{1,0},{2,1},{3,2},{4,3},{5,4},{6,5},{7,6},{8,7},{9,8},{10,9... | collective-permute-start | bytes 1179656 | tf_op jit(solution)/shard_map/ppermute | solution.py:403
  93.2 18.9 %collective-permute-start.11 = (f32[3,16,8,128]{3,2,1,0:T(8,128)S(1)}, f32[3,16,8,128]{3,2,1,0:T(8,128)S(1)}, u32[]{:S(2)}, u32[]{:S(2)}) collective-permute-start(f32[3,16,8,128]{3,2,1,0:T(8,128)S(1)} %get-tuple-element.33), channel_id=1, source_target_pairs={{0,112},{16,0},{32,16},{48,32},{64,48},{80,64},{96,80},{112,96},{1... | collective-permute-start | bytes 589832 | tf_op jit(solution)/shard_map/ppermute | solution.py:403
  98.6 13.5 %collective-permute-start.10 = (f32[3,16,8,128]{3,2,1,0:T(8,128)S(1)}, f32[3,16,8,128]{3,2,1,0:T(8,128)S(1)}, u32[]{:S(2)}, u32[]{:S(2)}) collective-permute-start(f32[3,16,8,128]{3,2,1,0:T(8,128)S(1)} %get-tuple-element.34), channel_id=1, source_target_pairs={{0,16},{16,32},{32,48},{48,64},{64,80},{80,96},{96,112},{112,0},{1... | collective-permute-start | bytes 589832 | tf_op jit(solution)/shard_map/ppermute | solution.py:403
  115.6 10.3 %collective-permute-start.14 = (f32[6,16,8,128]{3,2,1,0:T(8,128)S(1)}, f32[6,16,8,128]{3,2,1,0:T(8,128)S(1)}, u32[]{:S(2)}, u32[]{:S(2)}) collective-permute-start(f32[6,16,8,128]{3,2,1,0:T(8,128)S(1)} %get-tuple-element.32), channel_id=1, source_target_pairs={{0,16},{16,32},{32,48},{48,64},{64,80},{80,96},{96,112},{112,0},{1... | collective-permute-start | bytes 1179656 | tf_op jit(solution)/shard_map/ppermute | solution.py:403
  115.7 10.3 %collective-permute-start.15 = (f32[6,16,8,128]{3,2,1,0:T(8,128)S(1)}, f32[6,16,8,128]{3,2,1,0:T(8,128)S(1)}, u32[]{:S(2)}, u32[]{:S(2)}) collective-permute-start(f32[6,16,8,128]{3,2,1,0:T(8,128)S(1)} %get-tuple-element.31), channel_id=1, source_target_pairs={{0,112},{16,0},{32,16},{48,32},{64,48},{80,64},{96,80},{112,96},{1... | collective-permute-start | bytes 1179656 | tf_op jit(solution)/shard_map/ppermute | solution.py:403
  120.8 33.3 %collective-permute-start.16 = (f32[32,6,8,128]{3,2,1,0:T(8,128)S(1)}, f32[32,6,8,128]{3,2,1,0:T(8,128)S(1)}, u32[]{:S(2)}, u32[]{:S(2)}) collective-permute-start(f32[32,6,8,128]{3,2,1,0:T(8,128)S(1)} %get-tuple-element.27), channel_id=1, source_target_pairs={{0,1},{1,2},{2,3},{3,4},{4,5},{5,6},{6,7},{7,8},{8,9},{9,10},{10,1... | collective-permute-start | bytes 2359304 | tf_op jit(solution)/shard_map/ppermute | solution.py:403
  122.3 31.7 %collective-permute-start.17 = (f32[32,6,8,128]{3,2,1,0:T(8,128)S(1)}, f32[32,6,8,128]{3,2,1,0:T(8,128)S(1)}, u32[]{:S(2)}, u32[]{:S(2)}) collective-permute-start(f32[32,6,8,128]{3,2,1,0:T(8,128)S(1)} %get-tuple-element.28), channel_id=1, source_target_pairs={{0,15},{1,0},{2,1},{3,2},{4,3},{5,4},{6,5},{7,6},{8,7},{9,8},{10,9... | collective-permute-start | bytes 2359304 | tf_op jit(solution)/shard_map/ppermute | solution.py:403
  126.0 28.1 %collective-permute-start.19 = (f32[12,6,8,128]{3,2,1,0:T(8,128)S(1)}, f32[12,6,8,128]{3,2,1,0:T(8,128)S(1)}, u32[]{:S(2)}, u32[]{:S(2)}) collective-permute-start(f32[12,6,8,128]{3,2,1,0:T(8,128)S(1)} %get-tuple-element.41), channel_id=1, source_target_pairs={{0,15},{1,0},{2,1},{3,2},{4,3},{5,4},{6,5},{7,6},{8,7},{9,8},{10,9... | collective-permute-start | bytes 884744 | tf_op jit(solution)/shard_map/ppermute | solution.py:403
  135.6 18.5 %collective-permute-start.18 = (f32[12,6,8,128]{3,2,1,0:T(8,128)S(1)}, f32[12,6,8,128]{3,2,1,0:T(8,128)S(1)}, u32[]{:S(2)}, u32[]{:S(2)}) collective-permute-start(f32[12,6,8,128]{3,2,1,0:T(8,128)S(1)} %get-tuple-element.42), channel_id=1, source_target_pairs={{0,1},{1,2},{2,3},{3,4},{4,5},{5,6},{6,7},{7,8},{8,9},{9,10},{10,1... | collective-permute-start | bytes 884744 | tf_op jit(solution)/shard_map/ppermute | solution.py:403

commit v2 on v1

v2 whole, which is shorter than its diff:
```python
import functools

import jax
import jax.numpy as jnp
from jax import lax
from jax.experimental import pallas as pl
from jax.experimental.pallas import tpu as pltpu
from jax.sharding import PartitionSpec as P

SWEEPS = 4
TIME_STEP = 0.25
PSEUDO_STEP = 0.3
EPS = 1e-06
FRONT = 1.5
WIDE = SWEEPS + 2

ROWS, LANES = 8, 128
HIGH = lax.Precision.HIGHEST


def params(mib):
    return pltpu.CompilerParams(vmem_limit_bytes=mib * 2**20)


def f32(*shape):
    return jax.ShapeDtypeStruct(shape, jnp.float32)


def cost(vector_ops):
    return pl.CostEstimate(flops=vector_ops * 1024, bytes_accessed=2**23, transcendentals=0)


def shifted(col, step):
    lane = lax.broadcasted_iota(jnp.int32, (ROWS, LANES), 1)
    turned = pltpu.roll(col, (-step) % LANES, 1)
    if step > 0:
        return jnp.where(lane >= LANES - step, pltpu.roll(turned, ROWS - 1, 0), turned)
    return jnp.where(lane < -step, pltpu.roll(turned, 1, 0), turned)


def inverse(values):
    return pl.reciprocal(values, approx=True)


def correction(rough1, rough2, rough3, third1, third2):
    r1, r2, r3 = inverse(rough1), inverse(rough2), inverse(rough3)
    w1 = r1 * r1
    w12 = w1 + 6.0 * (r2 * r2)
    w3 = 3.0 * (r3 * r3)
    return (4.0 * w1 * third1 + (w3 - w12) * third2) * inverse(w12 + w3)


def upwind_part(speed, central, corr):
    return speed * central + jnp.abs(speed) * corr


class March:
    def __init__(self, get):
        self.get = get
        self.made = {}

    def once(self, name, j, make):
        key = (name, j)
        if key not in self.made:
            self.made[key] = make()
        return self.made[key]

    def p(self, j):
        return self.once("p", j, lambda: self.get(j))

    def d(self, j):
        return self.once("d", j, lambda: self.p(j + 1) - self.p(j))

    def curve(self, j):
        return self.once("c", j, lambda: self.d(j) - self.d(j - 1))

    def gap(self, j):
        return self.once("g", j, lambda: self.curve(j + 1) - self.curve(j))

    def third(self, j):
        return self.once("t", j, lambda: self.gap(j) - self.gap(j - 1))

    def base(self, j):
        return self.once("h", j, lambda: (4.0 / 3.0) * (self.gap(j) * self.gap(j)) + EPS)

    def cross(self, j):
        return self.once("x", j, lambda: self.curve(j) * self.curve(j + 1))

    def twice(self, j):
        return self.once("a", j, lambda: (self.curve(j) + self.curve(j)) * self.curve(j))

    def less(self, j):
        return self.once("l", j, lambda: self.base(j) - self.cross(j))

    def mid(self, j):
        return self.once("m", j, lambda: self.base(j) + self.cross(j))

    def up(self, j):
        return self.once("u", j, lambda: self.less(j) + self.twice(j + 1))

    def down(self, j):
        return self.once("v", j, lambda: self.less(j) + self.twice(j))

    def central(self, i):
        return 6.0 * (self.p(i + 1) - self.p(i - 1)) - (self.gap(i) + self.gap(i - 1))

    def part(self, i, speed):
        minus = speed < 0
        corr = correction(
            jnp.where(minus, self.up(i - 2), self.down(i + 1)),
            jnp.where(minus, self.mid(i - 1), self.mid(i)),
            jnp.where(minus, self.down(i), self.up(i - 1)),
            jnp.where(minus, self.third(i - 1), self.third(i + 1)),
            self.third(i),
        )
        return upwind_part(speed, self.central(i), corr)


def depth_rate(slope, here, turned, speed):
    m2, m1, p1, p2 = turned
    minus = speed < 0
    a = jnp.where(minus, m2, p2)
    b = jnp.where(minus, m1, p1)
    d = jnp.where(minus, p1, m1)
    g1, g2, g3 = b - a, here - b, d - here
    corr = correction(
        (4.0 / 3.0) * (g1 * g1) + EPS + b * (b + g1),
        (4.0 / 3.0) * (g2 * g2) + EPS + b * here,
        (4.0 / 3.0) * (g3 * g3) + EPS + here * (here - g3),
        g2 - g1,
        g3 - g2,
    )
    return upwind_part(speed, slope - (p1 - m1), corr)


def depth_part(col, speed):
    before, after = shifted(col, -1), shifted(col, 1)
    here = (after - col) - (col - before)
    return depth_rate(6.0 * (after - before), here, [shifted(here, step) for step in (-2, -1, 1, 2)], speed)


def loop(low, high, body):
    def step(i, carry):
        body(i)
        return carry

    lax.fori_loop(low, high, step, 0)


def pack_velocity(rows_ref, out_ref):
    def to(g):
        for c in range(3):
            for r in range(10):
                block, low = (g, r - 1) if 1 <= r <= 8 else ((g + 15, 7) if r == 0 else (g + 1, 0))
                start = c * 512 + lax.rem(block, 16) * 32 + low
                out_ref[g, pl.ds((c * 10 + r) * 4, 4), :] = rows_ref[pl.ds(start, 4, stride=8), :]

    loop(0, 16, to)


def unpack_level(rows_ref, p_ref, ylo_ref, yhi_ref):
    def to(x):
        for y in range(16):
            col = rows_ref[pl.ds(x * 128 + (y // 8) * 64 + y % 8, 8, stride=8), :]
            p_ref[x, y] = col
            if y < 3:
                ylo_ref[x, y] = col
            if y >= 13:
                yhi_ref[x, y - 13] = col

    loop(0, 32, to)


def refine_table():
    k = lax.broadcasted_iota(jnp.int32, (256, 256), 0)
    n = lax.broadcasted_iota(jnp.int32, (256, 256), 1)
    beside = jnp.where(n % 2 == 0, n // 2 - 1, n // 2 + 1)
    beside = jnp.where(beside < 0, 255, jnp.where(beside > 127, 128, beside))
    return jnp.where(k == n // 2, 0.75, 0.0) + jnp.where(k == beside, 0.25, 0.0)


def refine_z(plane, table):
    count = plane.shape[0]
    row = lax.broadcasted_iota(jnp.int32, plane.shape, 0) % 4
    lane = lax.broadcasted_iota(jnp.int32, plane.shape, 1)
    after = jnp.where(row == 3, pltpu.roll(plane, 3, 0), pltpu.roll(plane, count - 1, 0))
    prior = jnp.where(row == 0, pltpu.roll(plane, count - 3, 0), pltpu.roll(plane, 1, 0))
    wide = jnp.concatenate([plane, jnp.where(lane < 64, after, prior)], axis=1)
    out = jnp.dot(wide, table, precision=HIGH, preferred_element_type=jnp.float32)
    return out[:, :128], out[:, 128:]


def band_blocks(band_ref):
    k = lax.broadcasted_iota(jnp.int32, (64, 128), 0)
    n = lax.broadcasted_iota(jnp.int32, (64, 128), 1)
    spread = jnp.where(lax.rem(k, 8) == lax.div(n, 16), -TIME_STEP / 12.0, 0.0)
    row = lax.broadcasted_iota(jnp.int32, (8, 64), 0)
    tile = lax.div(lax.broadcasted_iota(jnp.int32, (8, 64), 1), 8)
    blocks = []
    for half in range(2):
        mask = jnp.broadcast_to(band_ref[half].astype(jnp.float32), (8, 64))
        mask = jnp.where(row == tile, mask, 0.0)
        blocks.append(jnp.dot(mask, spread, precision=HIGH, preferred_element_type=jnp.float32))
    return blocks


def refine_inner(mid_ref, band_ref, v_ref, ends_ref, fine, band):
    table = refine_table()
    for half, block in enumerate(band_blocks(band_ref)):
        band[half] = block

    def along_z(k):
        left, right = refine_z(mid_ref[pl.ds(k * 480, 480), :], table)
        fine[pl.ds(k * 960, 480, stride=2), :] = left
        fine[pl.ds(k * 960 + 1, 480, stride=2), :] = right

    loop(0, 4, along_z)
    for end, plane in enumerate((0, 15)):
        ends_ref[end] = fine[pl.ds(plane * 240, 240), :]

    def along_xy(i):
        for c in range(3):
            near, far = [], []
            for r in range(10):
                at = (c * 10 + r) * 8
                near.append(fine[pl.ds(i * 240 + at, 8), :])
                far.append(fine[pl.ds(i * 240 + 240 + at, 8), :])
            for k in range(2):
                x = 2 * i + 1 + k
                line = [0.75 * a + 0.25 * b for a, b in (zip(far, near) if k else zip(near, far))]
                along_y(c, x, line, band[lax.div(x, 16)], v_ref)

    loop(0, 15, along_xy)


def along_y(c, x, line, band, v_ref):
    scaled = [band * value for value in line]
    for y in range(16):
        m = y // 2 + 1
        v_ref[c, x, y] = 0.75 * scaled[m] + 0.25 * scaled[m - 1 + 2 * (y % 2)]


def refine_ends(lo_ref, hi_ref, ends_ref, band_ref, p_ref, v_in, acc_in, v_out, acc_out, fine, ends, part, sems):
    table = refine_table()
    blocks = band_blocks(band_ref)
    for side, ref in enumerate((lo_ref, hi_ref)):
        left, right = refine_z(ref[pl.ds(384, 120), :], table)
        fine[pl.ds(side * 240, 120, stride=2), :] = left
        fine[pl.ds(side * 240 + 1, 120, stride=2), :] = right
    for side in range(2):
        for c in range(3):
            line = []
            for r in range(10):
                at = (c * 10 + r) * 8
                line.append(0.75 * ends_ref[side, pl.ds(at, 8), :] + 0.25 * fine[pl.ds(side * 240 + at, 8), :])
            along_y(c, side, line, blocks[side], ends)
    for side in range(2):
        x = 31 * side
        march = March(lambda y: p_ref[x, y])
        for y in range(16):
            total = depth_part(march.p(y), ends[2, side, y])
            if 3 <= y < 13:
                total = total + march.part(y, ends[1, side, y])
            part[side, y] = total
    copies = []
    for side in range(2):
        copies.append((part.at[side], acc_out.at[31 * side]))
        for c in range(3):
            copies.append((ends.at[c, side], v_out.at[c, 31 * side]))
    copies = [pltpu.make_async_copy(src, dst, sems.at[k]) for k, (src, dst) in enumerate(copies)]
    for copy in copies:
        copy.start()
    for copy in copies:
        copy.wait()


def inner_rate(first, p_ref, v_ref, acc_ref, curve, slope, even, odd):
    def x_line(y):
        march = March(lambda x: p_ref[x, y])
        for x in range(32):
            col = march.p(x)
            before, after = shifted(col, -1), shifted(col, 1)
            curve[x, y] = (after - col) - (col - before)
            slope[x, y] = 6.0 * (after - before)
            if 3 <= x < 29:
                acc_ref[x, y] = march.part(x, v_ref[0, x, y])
            else:
                acc_ref[x, y] = jnp.zeros((ROWS, LANES), jnp.float32)

    loop(0, 16, x_line)

    def turn(x, turned):
        for y in range(16):
            col = curve[x, y]
            for k, step in enumerate((-2, -1, 1, 2)):
                turned[k, y] = shifted(col, step)

    def y_line(x, turned):
        march = March(lambda y: p_ref[x, y])
        for y in range(16):
            total = acc_ref[x, y] + depth_rate(slope[x, y], curve[x, y], [turned[k, y] for k in range(4)], v_ref[2, x, y])
            if 3 <= y < 13:
                total = total + march.part(y, v_ref[1, x, y])
            acc_ref[x, y] = total

    low = 1 if first else 0
    count = 30 if first else 32
    turn(low, even)

    def two(k):
        x = low + 2 * k
        turn(x + 1, odd)
        y_line(x, even)
        turn(jnp.minimum(x + 2, 31), even)
        y_line(x + 1, odd)

    loop(0, count // 2, two)


def section(start, current, rate, number):
    if number == 0:
        return current + rate
    if number == 1:
        return 0.75 * start + 0.25 * (current + rate)
    return start * (1.0 / 3.0) + (2.0 / 3.0) * (current + rate)


def edge_rate(
    number, edge, acc_ref, start_ref, p_ref, v_ref, xlo_ref, xhi_ref, ylo_ref, yhi_ref,
    new_ref, nxlo_ref, nxhi_ref, nylo_ref, nyhi_ref, side,
):
    def from_rows(ref, x, y):
        return ref[pl.ds((x * 16 + y) * 8, 8), :]

    def x_line(y):
        low = March(lambda x: from_rows(xlo_ref, x + 3, y) if x < 0 else p_ref[x, y])
        high = March(lambda x: from_rows(xhi_ref, x - 32, y) if x >= 32 else p_ref[x, y])
        for k in range(3):
            side[k, y] = low.part(k, v_ref[0, k, y])
            side[k + 3, y] = high.part(29 + k, v_ref[0, 29 + k, y])

    loop(0, 16, x_line)

    def y_line(x, side_x, outs):
        low = March(lambda y: ylo_ref[x, y + 3] if y < 0 else p_ref[x, y])
        high = March(lambda y: yhi_ref[x, y - 16] if y >= 16 else p_ref[x, y])
        for y in range(16):
            rate = acc_ref[x, y]
            if side_x is not None:
                rate = rate + side[side_x, y]
            if y < 3:
                rate = rate + low.part(y, v_ref[1, x, y])
            if y >= 13:
                rate = rate + high.part(y, v_ref[1, x, y])
            start = None if number == 0 else start_ref[x, y]
            new = section(start, p_ref[x, y], rate, number)
            new_ref[x, y] = new
            if outs is not None:
                outs[0][pl.ds((outs[1] * 16 + y) * 8, 8), :] = new
            if y < edge:
                nylo_ref[x, y] = new
            if y >= 16 - edge:
                nyhi_ref[x, y - (16 - edge)] = new

    loop(0, 3, lambda x: y_line(x, x, (nxlo_ref, x)))
    loop(29, 32, lambda x: y_line(x, x - 26, (nxhi_ref, x - (32 - edge))))
    if edge > 3:
        loop(3, edge, lambda x: y_line(x, None, (nxlo_ref, x)))
        loop(32 - edge, 29, lambda x: y_line(x, None, (nxhi_ref, x - (32 - edge))))
    loop(edge, 32 - edge, lambda x: y_line(x, None, None))


def pushes(col):
    push = (PSEUDO_STEP * col) * lax.rsqrt(col * col + 1.0)
    return push, jnp.where(col > 0, 1.0, -1.0)


def turn(src, x, ys, turned):
    for y in ys:
        col = src[x, y]
        turned[0, y] = shifted(col, -1)
        turned[1, y] = shifted(col, 1)


def sweep_line(src, dst, push, sign, x, ys, turned):
    cols = {}

    def at(y):
        if y not in cols:
            cols[y] = src[x, y]
        return cols[y]

    for y in ys:
        col, c, s = at(y), push[x, y], sign[x, y]
        here = s * col
        total = None
        for pair in ((src[x - 1, y], src[x + 1, y]), (at(y - 1), at(y + 1)), (turned[0, y], turned[1, y])):
            floor = 1e-15 if total is None else 0.0
            rise = jnp.maximum(here - jnp.minimum(s * pair[0], s * pair[1]), floor)
            total = rise * rise if total is None else total + rise * rise
        dst[x, y] = (col + c) - (c * total) * lax.rsqrt(total)


def sweep_rows(src, dst, push, sign, place, pairs, ys, even, odd):
    turn(src, place(0), ys, even)

    def two(j):
        x = place(j)
        turn(src, x + 1, ys, odd)
        sweep_line(src, dst, push, sign, x, ys, even)
        turn(src, place(jnp.minimum(j + 1, pairs - 1)), ys, even)
        sweep_line(src, dst, push, sign, x + 1, ys, odd)

    loop(0, pairs, two)


def sweep_core(adv_ref, *refs):
    levels, (push, sign, even, odd) = refs[:SWEEPS], refs[SWEEPS:]

    def prepare(x):
        for y in range(16):
            push[x, y], sign[x, y] = pushes(adv_ref[x, y])

    loop(0, 32, prepare)
    src = adv_ref
    for k in range(1, SWEEPS + 1):
        dst = levels[k - 1]
        sweep_rows(src, dst, push, sign, lambda j, k=k: k + 2 * j, 16 - k, range(k, 16 - k), even, odd)
        src = dst


def pack_corners(xlo_ref, xhi_ref, _, low_ref, high_ref):
    k = 0
    for dx in range(1, WIDE):
        for ref, x in ((xlo_ref, WIDE - dx), (xhi_ref, dx - 1)):
            for dy in range(1, WIDE - dx + 1):
                low_ref[k] = ref[pl.ds((x * 16 + dy - 1) * 8, 8), :]
                high_ref[k] = ref[pl.ds((x * 16 + 16 - dy) * 8, 8), :]
                k += 1


CORNERS = WIDE * (WIDE - 1)


def finish(
    adv_ref, xlo_ref, xhi_ref, ylo_ref, yhi_ref, clo_ref, chi_ref, one_ref, two_ref, three_ref, four_ref,
    new_ref, send_ref, q0, q1, push, sign, nx, ny, nz, lump, even, odd,
):
    w = WIDE
    size_x, size_y = 32 + 2 * w, 16 + 2 * w

    def put(x, y, col):
        q0[x, y] = col
        push[x, y], sign[x, y] = pushes(col)

    def fill_mid(x):
        for y in range(w):
            put(x + w, y, ylo_ref[x, y])
            put(x + w, y + 16 + w, yhi_ref[x, y])
        for y in range(16):
            put(x + w, y + w, adv_ref[x, y])

    def fill_side(x):
        for y in range(16):
            put(x, y + w, xlo_ref[pl.ds((x * 16 + y) * 8, 8), :])
            put(x + 32 + w, y + w, xhi_ref[pl.ds((x * 16 + y) * 8, 8), :])

    loop(0, 32, fill_mid)
    loop(0, w, fill_side)
    k = 0
    for dx in range(1, w):
        for x in (w - dx, w + 31 + dx):
            for dy in range(1, w - dx + 1):
                put(x, w - dy, clo_ref[k])
                put(x, w + 15 + dy, chi_ref[k])
                k += 1

    src, dst = q0, q1
    for k, core_ref in enumerate((one_ref, two_ref, three_ref, four_ref), 1):
        def end_rows(j, k=k):
            return k + 2 * j + jnp.where(j >= 3, 32 - 2 * k, 0)

        sweep_rows(src, dst, push, sign, end_rows, 6, range(k, size_y - k), even, odd)
        sides = [*range(k, k + w), *range(size_y - k - w, size_y - k)]
        sweep_rows(src, dst, push, sign, lambda j, k=k: w + k + 2 * j, 16 - k, sides, even, odd)
        inside = range(k, 16 - k)
        if k < SWEEPS:
            for x in (k, k + 1, 30 - k, 31 - k):
                for y in inside:
                    dst[x + w, y + w] = core_ref[x, y]
            inside = (k, k + 1, 14 - k, 15 - k)

        def take(x, core_ref=core_ref, inside=inside, dst=dst):
            for y in inside:
                dst[x + w, y + w] = core_ref[x, y]

        loop(k, 32 - k, take)
        src, dst = dst, src
    last = src

    def normals(x):
        xs = x + w - 1
        cols = {}

        def at(y):
            if y not in cols:
                cols[y] = last[xs, y + w]
            return cols[y]

        across, along, deep = {}, {}, {}
        for y in range(-1, 17):
            gx = last[xs + 1, y + w] - last[xs - 1, y + w]
            gy = at(y + 1) - at(y - 1)
            gz = shifted(at(y), 1) - shifted(at(y), -1)
            scale = lax.rsqrt(gx * gx + gy * gy + gz * gz + 4.0)
            across[y], along[y], deep[y] = gx * scale, gy * scale, gz * scale
        for j in range(8):
            a, b = 2 * j, 2 * j + 1
            nx[x, j] = across[a] + across[b]
            ny[x, j] = (along[b] + along[b + 1]) - (along[a - 1] + along[a])
            nz[x, j] = deep[a] + deep[b]

    loop(0, 34, normals)

    def gather(i):
        a, b = 2 * i + 1, 2 * i + 2
        for j in range(8):
            deep = nz[a, j] + nz[b, j]
            total = (nx[b, j] + nx[b + 1, j]) - (nx[a - 1, j] + nx[a, j]) + (ny[a, j] + ny[b, j])
            lump[pl.ds(i * 64 + j * 8, 8), :] = total + (shifted(deep, 1) - shifted(deep, -1))
            share = None
            for x in range(2):
                for y in range(2):
                    xx, yy = 2 * i + x, 2 * j + y
                    col = last[xx + w, yy + w]
                    new_ref[pl.ds(xx * 128 + (yy // 8) * 64 + yy % 8, 8, stride=8), :] = col
                    bend = jnp.tanh(col * (1.0 / FRONT))
                    share = bend if share is None else share + bend
            lump[pl.ds(1024 + i * 64 + j * 8, 8), :] = share

    loop(0, 16, gather)

    k = lax.broadcasted_iota(jnp.int32, (256, 128), 0)
    n = lax.broadcasted_iota(jnp.int32, (256, 128), 1)
    table = jnp.where(lax.div(k, 2) == n, 1.0 / 16.0, 0.0)

    def restrict(g):
        halves = []
        for odd_row in range(2):
            rows = []
            for kind in range(2):
                for i in range(4):
                    base = kind * 1024 + (4 * g + i) * 64 + odd_row
                    rows += [lump[pl.ds(base + 2 * z, 8, stride=8), :] for z in range(4)]
            halves.append(jnp.concatenate(rows, axis=0))
        out = jnp.dot(jnp.concatenate(halves, axis=1), table, precision=HIGH, preferred_element_type=jnp.float32)
        for i in range(4):
            send_ref[4 * g + i, pl.ds(0, 32), :] = out[i * 32 : i * 32 + 32]
            send_ref[4 * g + i, pl.ds(32, 32), :] = out[128 + i * 32 : 160 + i * 32] + 0.5

    loop(0, 4, restrict)


def call(kernel, outs, *args, scratch=(), mib=48, ops=1000, name=None, anywhere=(), aliases=None):
    def spec(k):
        return pl.BlockSpec(memory_space=pl.ANY if k in anywhere else pltpu.VMEM)

    aliases = aliases or {}
    flat = outs if isinstance(outs, tuple) else (outs,)
    specs = tuple(pl.BlockSpec(memory_space=pl.ANY if k in aliases.values() else pltpu.VMEM) for k in range(len(flat)))
    return pl.pallas_call(
        kernel,
        out_shape=outs,
        in_specs=[spec(k) for k in range(len(args))],
        out_specs=specs if isinstance(outs, tuple) else specs[0],
        scratch_shapes=[pltpu.VMEM(s, jnp.float32) if isinstance(s, tuple) else s for s in scratch],
        input_output_aliases=aliases,
        compiler_params=params(mib),
        cost_estimate=cost(ops),
        name=name,
    )(*args)


def moved(values, axis, step):
    count = lax.axis_size(axis)
    return lax.ppermute(values, axis, [(i, (i + step) % count) for i in range(count)])


def star(xlo, xhi, ylo, yhi):
    return (moved(xhi, "gx", 1), moved(xlo, "gx", -1), moved(yhi, "gy", 1), moved(ylo, "gy", -1))


def per_device(level_set, flow_velocity, band_mask):
    col = (ROWS, LANES)
    block = f32(32, 16, *col)
    level_rows = level_set.reshape(32, 2, 8, 8, 128).transpose(0, 1, 3, 2, 4).reshape(4096, 128)
    flow_rows = flow_velocity.reshape(3, 16, 8, 4, 128).transpose(0, 1, 3, 2, 4).reshape(1536, 128)

    send = call(pack_velocity, f32(16, 120, 128), flow_rows, name="pack", mib=8)
    coarse = lax.all_to_all(send, "gy", split_axis=0, concat_axis=0, tiled=True)
    start, ylo, yhi = call(
        unpack_level, (block, f32(32, 3, *col), f32(32, 3, *col)), level_rows, name="unpack", mib=8
    )
    xlo = jnp.concatenate([start[:3].reshape(384, 128), coarse[0]], axis=0)
    xhi = jnp.concatenate([start[29:].reshape(384, 128), coarse[15]], axis=0)
    halo = star(xlo, xhi, ylo, yhi)
    velocity, ends = call(
        refine_inner, (f32(3, 32, 16, *col), f32(2, 240, 128)), coarse.reshape(1920, 128), band_mask,
        scratch=[(3840, 128), (2, *col)], name="refine", mib=24,
    )
    current = start
    for number in range(3):
        acc = call(
            functools.partial(inner_rate, number == 0), block, current, velocity,
            scratch=[block.shape, block.shape, (4, 16, *col), (4, 16, *col)], name="inner", mib=24, ops=512 * 140,
        )
        if number == 0:
            velocity, acc = call(
                refine_ends, (f32(3, 32, 16, *col), block), halo[0], halo[1], ends, band_mask, current, velocity, acc,
                scratch=[(480, 128), (3, 2, 16, *col), (2, 16, *col), pltpu.SemaphoreType.DMA((8,))],
                name="ends", mib=16, anywhere=(5, 6), aliases={5: 0, 6: 1},
            )
        edge = WIDE if number == 2 else 3
        x_edge, y_edge = f32(edge * 128, 128), f32(32, edge, *col)
        current, *edges = call(
            functools.partial(edge_rate, number, edge), (block, x_edge, x_edge, y_edge, y_edge),
            acc, start, current, velocity, *halo,
            scratch=[(6, 16, *col)], name="edge", mib=24, ops=512 * 30,
        )
        halo = star(*edges)
    xlo, xhi, ylo, yhi = halo
    levels = call(
        sweep_core, (block,) * SWEEPS, current,
        scratch=[block.shape, block.shape, (2, 16, *col), (2, 16, *col)], name="core", mib=8, ops=512 * 90,
    )
    corner = f32(CORNERS, *col)
    corner_low, corner_high = call(
        pack_corners, (corner, corner), xlo, xhi, levels[-1], name="corners", mib=4, anywhere=(2,)
    )
    clo, chi = moved(corner_high, "gy", 1), moved(corner_low, "gy", -1)
    ext = (32 + 2 * WIDE, 16 + 2 * WIDE, *col)
    new_rows, packed = call(
        finish, (f32(4096, 128), f32(16, 64, 128)), current, xlo, xhi, ylo, yhi, clo, chi, *levels,
        scratch=[ext] * 4 + [(34, 8, *col)] * 3 + [(2048, 128), (2, 28, *col), (2, 28, *col)],
        name="finish", mib=30, ops=512 * 250,
    )
    returned = lax.all_to_all(packed, "gy", split_axis=0, concat_axis=0, tiled=True).reshape(16, 2, 4, 8, 128)
    new_level = new_rows.reshape(32, 2, 8, 8, 128).transpose(0, 1, 3, 2, 4).reshape(32, 16, 1024)
    flows = [returned[:, k].transpose(0, 2, 1, 3).reshape(1, 128, 512) for k in range(2)]
    return (new_level, flows[0], flows[1])


def solution(mesh):
    placed = (P("gx", "gy", None), P(None, ("gx", "gy"), None, None), P("gx", "gy", None))
    return jax.shard_map(
        per_device,
        mesh=mesh,
        in_specs=placed,
        out_specs=(P("gx", "gy", None), P(("gx", "gy"), None, None), P(("gx", "gy"), None, None)),
        check_vma=False,
    )
```

time: 204 us -> 172 us (0.84)
  Pallas kernels: 94.1 us -> 79.2 us
  waiting for transfers between devices: 34.6 us -> 20.8 us
  starting transfers between devices: 51.5 us -> 46.6 us
  blocking collectives: 14.6 us -> 17.6 us
  local copies, waits for them, and re-layouts: 6.86 us -> 4.33 us
    ppermute x20 -> x18, waiting for transfers between devices: 29.5 us -> 11.1 us  [moved(): lax.ppermute(values, axis, [(i, (i + step) % count) for i in range(count)])]
    pallas_call x10 -> x13, Pallas kernels: 94.1 us -> 79.2 us  [call(): pl.pallas_call(kernel, out_shape=outs, in_specs=[spec(k) for k in range(l...]
    ppermute x20 -> x18, starting transfers between devices: 43.7 us -> 38.8 us  [moved(): lax.ppermute(values, axis, [(i, (i + step) % count) for i in range(count)])]
    all_to_all x1, waiting for transfers between devices: 5.15 us -> 9.71 us  [per_device(): coarse = lax.all_to_all(send, 'gy', split_axis=0, concat_axis=0, tiled=True)]
    all_to_all x1, blocking collectives: 14.6 us -> 17.6 us  [per_device(): lax.all_to_all(packed, 'gy', split_axis=0, concat_axis=0, tiled=True)]
  transfers between devices with their start and end apart: 21 -> 19, of which waited for: 5 -> 4; matrix products, arithmetic and copies ran while one was open for 2% -> 2% of each run, Pallas kernels for 24% -> 26%
where the time goes in v2:
time: 172 us; the launch traced here: 171 us
  Pallas kernels  79.2 us (46%)
  starting transfers between devices  46.6 us (27%)
  waiting for transfers between devices  20.8 us (12%)
  blocking collectives  17.6 us (10%)
  local copies, waits for them, and re-layouts  4.33 us (3%)
  other arithmetic  1.89 us (1%)
    pallas_call x13, Pallas kernels, call(): pl.pallas_call(kernel, out_shape=outs, in_specs=[spec(k) for k in range(l...  79.2 us
    ppermute x18, starting transfers between devices, moved(): lax.ppermute(values, axis, [(i, (i + step) % count) for i in range(count)])  38.8 us
    all_to_all x1, blocking collectives, per_device(): lax.all_to_all(packed, 'gy', split_axis=0, concat_axis=0, tiled=True)  17.6 us
    ppermute x18, waiting for transfers between devices, moved(): lax.ppermute(values, axis, [(i, (i + step) % count) for i in range(count)])  11.1 us
    all_to_all x1, waiting for transfers between devices, per_device(): coarse = lax.all_to_all(send, 'gy', split_axis=0, concat_axis=0, tiled=True)  9.71 us
    all_to_all x1, starting transfers between devices, per_device(): coarse = lax.all_to_all(send, 'gy', split_axis=0, concat_axis=0, tiled=True)  7.76 us
  transfers between devices with their start and end apart: 19, of which 4 were waited for; matrix products, arithmetic and copies ran while one was open for 2% of the time, Pallas kernels for 26%

profile of v2, /device:TPU:1, one launch (start us, length us, event | category | flops | bytes accessed | tf_op | source)
XLA Modules:
  0.0 171.3 jit_solution(15252778399957437032)
XLA Ops:
  0.6 1.1 copy-done.1
  1.8 1.3 pack.1
  3.0 7.8 %all-to-all-start = ((f32[16,120,128]{2,1,0:T(8,128)}), f32[16,120,128]{2,1,0:T(8,128)S(1)}, u32[]{:S(2)}, u32[]{:S(2)}) async-start(f32[16,120,128]{2,1,0:T(8,128)} %pack.1), calls=%async_computation | async-start | bytes 1966080 | tf_op jit(solution)/shard_map/all_to_all | solution.py:600
  10.8 0.0 copy-start
  10.8 1.6 copy-done
  12.4 1.4 unpack.1
  13.8 1.6 collective-permute-start.2
  15.4 0.8 fusion
  16.2 9.7 %all-to-all-done = f32[16,120,128]{2,1,0:T(8,128)S(1)} async-done(((f32[16,120,128]{2,1,0:T(8,128)}), f32[16,120,128]{2,1,0:T(8,128)S(1)}, u32[]{:S(2)}, u32[]{:S(2)}) %all-to-all-start) | async-done | bytes 983072 | tf_op jit(solution)/shard_map/all_to_all | solution.py:600
  25.9 0.9 pad_maximum_fusion
  26.8 1.4 collective-permute-start
  28.2 0.9 pad_maximum_fusion.1
  29.2 3.9 %collective-permute-start.1 = (f32[504,128]{1,0:T(8,128)S(1)}, f32[504,128]{1,0:T(8,128)S(1)}, u32[]{:S(2)}, u32[]{:S(2)}) collective-permute-start(f32[504,128]{1,0:T(8,128)S(1)} %pad_maximum_fusion.1), channel_id=1, source_target_pairs={{0,112},{16,0},{32,16},{48,32},{64,48},{80,64},{96,80},{112,96},{1... | collective-permute-start | bytes 774152 | tf_op jit(solution)/shard_map/ppermute | solution.py:586
  33.0 3.9 %refine.1 = (f32[3,32,16,8,128]{4,3,2,1,0:T(8,128)S(1)}, f32[2,240,128]{2,1,0:T(8,128)S(1)}) custom-call(f32[1920,128]{1,0:T(8,128)S(1)} %bitcast.35, s32[2,1,64]{2,1,0:T(1,128)S(1)} %copy-done.2), custom_call_target="tpu_custom_call" | custom-call | flops 1024000 | bytes 8388608 | tf_op jit(solution)/shard_map/refine/pallas_call | solution.py:571
  36.9 9.9 %inner.3.acc_in = f32[32,16,8,128]{3,2,1,0:T(8,128)S(1)} custom-call(f32[32,16,8,128]{3,2,1,0:T(8,128)S(1)} %get-tuple-element.33.p_ref.start_ref, f32[3,32,16,8,128]{4,3,2,1,0:T(8,128)S(1)} %get-tuple-element.35.v_ref.v_in), custom_call_target="tpu_custom_call" | custom-call | flops 73400320 | bytes 8388608 | tf_op jit(solution)/shard_map/inner/pallas_call | solution.py:571
  46.8 0.0 collective-permute-done.1.hi_ref.xhi_ref
  46.8 1.8 %ends.1 = (f32[3,32,16,8,128]{4,3,2,1,0:T(8,128)S(1)}, f32[32,16,8,128]{3,2,1,0:T(8,128)S(1)}) custom-call(f32[504,128]{1,0:T(8,128)S(1)} %collective-permute-done.lo_ref.xlo_ref, f32[504,128]{1,0:T(8,128)S(1)} %collective-permute-done.1.hi_ref.xhi_ref, f32[2,240,128]{2,1,0:T(8,128)S(1)} %get-tuple-element.34.ends_ref, ...), custom_call_target="tpu_custom_call", output_to_operand_aliasing={{0}: (5, {}), {1}: (6, {})} | custom-call | flops 1024000 | bytes 8388608 | tf_op jit(solution)/shard_map/ends/pallas_call | solution.py:571
  48.6 0.0 collective-permute-done.2.ylo_ref
  48.6 0.0 collective-permute-done.3.yhi_ref
  48.6 4.0 %edge.3 = (f32[32,16,8,128]{3,2,1,0:T(8,128)S(1)}, f32[384,128]{1,0:T(8,128)S(1)}, f32[384,128]{1,0:T(8,128)S(1)}, f32[32,3,8,128]{3,2,1,0:T(8,128)S(1)}, f32[32,3,8,128]{3,2,1,0:T(8,128)S(1)}) custom-call(f32[32,16,8,128]{3,2,1,0:T(8,128)S(1)} %get-tuple-element.36.acc_ref, f32[32,16,8,128]{3,2,1,0:T(8,128)S(1)} %get-tuple-element.33.p_ref.start_ref, ...), custom_call_target="tpu_custom_call" | custom-call | flops 15728640 | bytes 8388608 | tf_op jit(solution)/shard_map/edge/pallas_call | solution.py:571
  52.7 1.8 %collective-permute-start.6 = (f32[32,3,8,128]{3,2,1,0:T(8,128)S(1)}, f32[32,3,8,128]{3,2,1,0:T(8,128)S(1)}, u32[]{:S(2)}, u32[]{:S(2)}) collective-permute-start(f32[32,3,8,128]{3,2,1,0:T(8,128)S(1)} %get-tuple-element.43), channel_id=1, source_target_pairs={{0,1},{1,2},{2,3},{3,4},{4,5},{5,6},{6,7},{7,8},{8,9},{9,10},{10,1... | collective-permute-start | bytes 1179656 | tf_op jit(solution)/shard_map/ppermute | solution.py:586
  54.5 0.2 collective-permute-start.7
  54.7 5.1 %collective-permute-start.5 = (f32[384,128]{1,0:T(8,128)S(1)}, f32[384,128]{1,0:T(8,128)S(1)}, u32[]{:S(2)}, u32[]{:S(2)}) collective-permute-start(f32[384,128]{1,0:T(8,128)S(1)} %get-tuple-element.42), channel_id=1, source_target_pairs={{0,112},{16,0},{32,16},{48,32},{64,48},{80,64},{96,80},{112,96},{1... | collective-permute-start | bytes 589832 | tf_op jit(solution)/shard_map/ppermute | solution.py:586
  59.8 10.2 %inner.4.acc_ref = f32[32,16,8,128]{3,2,1,0:T(8,128)S(1)} custom-call(f32[32,16,8,128]{3,2,1,0:T(8,128)S(1)} %get-tuple-element.40.p_ref, f32[3,32,16,8,128]{4,3,2,1,0:T(8,128)S(1)} %get-tuple-element.37.v_ref), custom_call_target="tpu_custom_call" | custom-call | flops 73400320 | bytes 8388608 | tf_op jit(solution)/shard_map/inner/pallas_call | solution.py:571
  70.0 0.0 collective-permute-done.4.xlo_ref
  70.0 0.0 collective-permute-done.5.xhi_ref
  70.0 3.3 %edge.4 = (f32[32,16,8,128]{3,2,1,0:T(8,128)S(1)}, f32[384,128]{1,0:T(8,128)S(1)}, f32[384,128]{1,0:T(8,128)S(1)}, f32[32,3,8,128]{3,2,1,0:T(8,128)S(1)}, f32[32,3,8,128]{3,2,1,0:T(8,128)S(1)}) custom-call(f32[32,16,8,128]{3,2,1,0:T(8,128)S(1)} %inner.4.acc_ref, f32[32,16,8,128]{3,2,1,0:T(8,128)S(1)} %get-tuple-element.33.p_ref.start_ref, ...), custom_call_target="tpu_custom_call" | custom-call | flops 15728640 | bytes 8388608 | tf_op jit(solution)/shard_map/edge/pallas_call | solution.py:571
  73.4 2.1 %collective-permute-start.10 = (f32[32,3,8,128]{3,2,1,0:T(8,128)S(1)}, f32[32,3,8,128]{3,2,1,0:T(8,128)S(1)}, u32[]{:S(2)}, u32[]{:S(2)}) collective-permute-start(f32[32,3,8,128]{3,2,1,0:T(8,128)S(1)} %get-tuple-element.48), channel_id=1, source_target_pairs={{0,1},{1,2},{2,3},{3,4},{4,5},{5,6},{6,7},{7,8},{8,9},{9,10},{10,1... | collective-permute-start | bytes 1179656 | tf_op jit(solution)/shard_map/ppermute | solution.py:586
  75.5 2.3 %collective-permute-start.11 = (f32[32,3,8,128]{3,2,1,0:T(8,128)S(1)}, f32[32,3,8,128]{3,2,1,0:T(8,128)S(1)}, u32[]{:S(2)}, u32[]{:S(2)}) collective-permute-start(f32[32,3,8,128]{3,2,1,0:T(8,128)S(1)} %get-tuple-element.49), channel_id=1, source_target_pairs={{0,15},{1,0},{2,1},{3,2},{4,3},{5,4},{6,5},{7,6},{8,7},{9,8},{10,9... | collective-permute-start | bytes 1179656 | tf_op jit(solution)/shard_map/ppermute | solution.py:586
  77.9 5.1 %collective-permute-start.9 = (f32[384,128]{1,0:T(8,128)S(1)}, f32[384,128]{1,0:T(8,128)S(1)}, u32[]{:S(2)}, u32[]{:S(2)}) collective-permute-start(f32[384,128]{1,0:T(8,128)S(1)} %get-tuple-element.47), channel_id=1, source_target_pairs={{0,112},{16,0},{32,16},{48,32},{64,48},{80,64},{96,80},{112,96},{1... | collective-permute-start | bytes 589832 | tf_op jit(solution)/shard_map/ppermute | solution.py:586
  83.0 10.3 %inner.5.acc_ref = f32[32,16,8,128]{3,2,1,0:T(8,128)S(1)} custom-call(f32[32,16,8,128]{3,2,1,0:T(8,128)S(1)} %get-tuple-element.45.p_ref, f32[3,32,16,8,128]{4,3,2,1,0:T(8,128)S(1)} %get-tuple-element.37.v_ref), custom_call_target="tpu_custom_call" | custom-call | flops 73400320 | bytes 8388608 | tf_op jit(solution)/shard_map/inner/pallas_call | solution.py:571
  93.2 0.0 collective-permute-done.9.xhi_ref
  93.2 0.0 collective-permute-done.10.ylo_ref
  93.3 3.3 %edge.5 = (f32[32,16,8,128]{3,2,1,0:T(8,128)S(1)}, f32[768,128]{1,0:T(8,128)S(1)}, f32[768,128]{1,0:T(8,128)S(1)}, f32[32,6,8,128]{3,2,1,0:T(8,128)S(1)}, f32[32,6,8,128]{3,2,1,0:T(8,128)S(1)}) custom-call(f32[32,16,8,128]{3,2,1,0:T(8,128)S(1)} %inner.5.acc_ref, f32[32,16,8,128]{3,2,1,0:T(8,128)S(1)} %get-tuple-element.33.p_ref.start_ref, ...), custom_call_target="tpu_custom_call" | custom-call | flops 15728640 | bytes 8388608 | tf_op jit(solution)/shard_map/edge/pallas_call | solution.py:571
  96.6 0.1 collective-permute-start.14
  96.7 4.4 %collective-permute-start.15 = (f32[32,6,8,128]{3,2,1,0:T(8,128)S(1)}, f32[32,6,8,128]{3,2,1,0:T(8,128)S(1)}, u32[]{:S(2)}, u32[]{:S(2)}) collective-permute-start(f32[32,6,8,128]{3,2,1,0:T(8,128)S(1)} %get-tuple-element.54), channel_id=1, source_target_pairs={{0,15},{1,0},{2,1},{3,2},{4,3},{5,4},{6,5},{7,6},{8,7},{9,8},{10,9... | collective-permute-start | bytes 2359304 | tf_op jit(solution)/shard_map/ppermute | solution.py:586
  101.1 0.0 collective-permute-start.12
  101.1 5.1 %collective-permute-start.13 = (f32[768,128]{1,0:T(8,128)S(1)}, f32[768,128]{1,0:T(8,128)S(1)}, u32[]{:S(2)}, u32[]{:S(2)}) collective-permute-start(f32[768,128]{1,0:T(8,128)S(1)} %get-tuple-element.52), channel_id=1, source_target_pairs={{0,112},{16,0},{32,16},{48,32},{64,48},{80,64},{96,80},{112,96},{1... | collective-permute-start | bytes 1179656 | tf_op jit(solution)/shard_map/ppermute | solution.py:586
  106.1 7.5 %core.1 = (f32[32,16,8,128]{3,2,1,0:T(8,128)S(1)}, f32[32,16,8,128]{3,2,1,0:T(8,128)S(1)}, f32[32,16,8,128]{3,2,1,0:T(8,128)S(1)}, f32[32,16,8,128]{3,2,1,0:T(8,128)S(1)}) custom-call(f32[32,16,8,128]{3,2,1,0:T(8,128)S(1)} %get-tuple-element.50.adv_ref), custom_call_target="tpu_custom_call" | custom-call | flops 47185920 | bytes 8388608 | tf_op jit(solution)/shard_map/core/pallas_call | solution.py:571
  113.6 7.6 %collective-permute-done.12.xlo_ref = f32[768,128]{1,0:T(8,128)S(1)} collective-permute-done((f32[768,128]{1,0:T(8,128)S(1)}, f32[768,128]{1,0:T(8,128)S(1)}, u32[]{:S(2)}, u32[]{:S(2)}) %collective-permute-start.12) | collective-permute-done | bytes 393248 | tf_op jit(solution)/shard_map/ppermute | solution.py:586
  121.3 3.8 %collective-permute-start.16 = (f32[30,8,128]{2,1,0:T(8,128)S(1)}, f32[30,8,128]{2,1,0:T(8,128)S(1)}, u32[]{:S(2)}, u32[]{:S(2)}) collective-permute-start(f32[30,8,128]{2,1,0:T(8,128)S(1)} %get-tuple-element.56), channel_id=1, source_target_pairs={{0,1},{1,2},{2,3},{3,4},{4,5},{5,6},{6,7},{7,8},{8,9},{9,10},{10,1... | collective-permute-start | bytes 368648 | tf_op jit(solution)/shard_map/ppermute | solution.py:586
  125.0 2.0 %collective-permute-start.17 = (f32[30,8,128]{2,1,0:T(8,128)S(1)}, f32[30,8,128]{2,1,0:T(8,128)S(1)}, u32[]{:S(2)}, u32[]{:S(2)}) collective-permute-start(f32[30,8,128]{2,1,0:T(8,128)S(1)} %get-tuple-element.57), channel_id=1, source_target_pairs={{0,15},{1,0},{2,1},{3,2},{4,3},{5,4},{6,5},{7,6},{8,7},{9,8},{10,9... | collective-permute-start | bytes 368648 | tf_op jit(solution)/shard_map/ppermute | solution.py:586
  127.0 0.7 collective-permute-done.16.clo_ref
  127.8 2.7 %collective-permute-done.17.chi_ref = f32[30,8,128]{2,1,0:T(8,128)S(1)} collective-permute-done((f32[30,8,128]{2,1,0:T(8,128)S(1)}, f32[30,8,128]{2,1,0:T(8,128)S(1)}, u32[]{:S(2)}, u32[]{:S(2)}) %collective-permute-start.17) | collective-permute-done | bytes 122912 | tf_op jit(solution)/shard_map/ppermute | solution.py:586
  130.5 0.0 collective-permute-done.14.ylo_ref
  130.5 22.4 %finish.1 = (f32[4096,128]{1,0:T(8,128)}, f32[16,64,128]{2,1,0:T(8,128)S(1)}) custom-call(f32[32,16,8,128]{3,2,1,0:T(8,128)S(1)} %get-tuple-element.50.adv_ref, f32[768,128]{1,0:T(8,128)S(1)} %collective-permute-done.12.xlo_ref, f32[768,128]{1,0:T(8,128)S(1)} %collective-permute-done.13.xhi_ref, f32[32,6,8,128]{3,2,1,0:T(8,128)S(1)} %collective-permute-done.14.ylo_ref, ...), custom_call_target="tpu_custom_call" | custom-call | flops 131072000 | bytes 8388608 | tf_op jit(solution)/shard_map/finish/pallas_call | solution.py:571
  152.9 17.6 %all_to_all.10 = f32[16,64,128]{2,1,0:T(8,128)S(1)} all-to-all(f32[16,64,128]{2,1,0:T(8,128)S(1)} %get-tuple-element.62), channel_id=1, replica_groups=mesh['gx'=8,'gy'=16] {'gy'}, dimensions={0} | all-to-all | bytes 1048576 | tf_op jit(solution)/shard_map/all_to_all | solution.py:647
  170.5 0.8 slice_bitcast_fusion
  (15 shorter events, 0.1 us)
Async XLA Ops:
  0.6 1.1 copy-start.1
  3.0 22.8 %all-to-all-start = ((f32[16,120,128]{2,1,0:T(8,128)}), f32[16,120,128]{2,1,0:T(8,128)S(1)}, u32[]{:S(2)}, u32[]{:S(2)}) async-start(f32[16,120,128]{2,1,0:T(8,128)} %pack.1), calls=%async_computation | async-start | bytes 1966080 | tf_op jit(solution)/shard_map/all_to_all | solution.py:600
  10.8 22.2 %copy-start.2 = (s32[2,1,64]{2,1,0:T(1,128)S(1)}, s32[2,1,64]{2,1,0:T(1,128)}, u32[]{:S(2)}) copy-start(s32[2,1,64]{2,1,0:T(1,128)} %band_ref.3) | copy-start | bytes 1540
  10.8 1.6 copy-start
  13.8 34.8 %collective-permute-start.2 = (f32[32,3,8,128]{3,2,1,0:T(8,128)}, f32[32,3,8,128]{3,2,1,0:T(8,128)S(1)}, u32[]{:S(2)}, u32[]{:S(2)}) collective-permute-start(f32[32,3,8,128]{3,2,1,0:T(8,128)} %get-tuple-element.38), channel_id=1, source_target_pairs={{0,1},{1,2},{2,3},{3,4},{4,5},{5,6},{6,7},{7,8},{8,9},{9,10},{10,1... | collective-permute-start | bytes 1179656 | tf_op jit(solution)/shard_map/ppermute | solution.py:586
  15.4 33.2 %collective-permute-start.3 = (f32[32,3,8,128]{3,2,1,0:T(8,128)}, f32[32,3,8,128]{3,2,1,0:T(8,128)}, u32[]{:S(2)}, u32[]{:S(2)}) collective-permute-start(f32[32,3,8,128]{3,2,1,0:T(8,128)} %get-tuple-element.39), channel_id=1, source_target_pairs={{0,15},{1,0},{2,1},{3,2},{4,3},{5,4},{6,5},{7,6},{8,7},{9,8},{10,9... | collective-permute-start | bytes 1179656 | tf_op jit(solution)/shard_map/ppermute | solution.py:586
  26.8 19.9 %collective-permute-start = (f32[504,128]{1,0:T(8,128)S(1)}, f32[504,128]{1,0:T(8,128)S(1)}, u32[]{:S(2)}, u32[]{:S(2)}) collective-permute-start(f32[504,128]{1,0:T(8,128)S(1)} %pad_maximum_fusion), channel_id=1, source_target_pairs={{0,16},{16,32},{32,48},{48,64},{64,80},{80,96},{96,112},{112,0},{1... | collective-permute-start | bytes 774152 | tf_op jit(solution)/shard_map/ppermute | solution.py:586
  29.2 17.6 %collective-permute-start.1 = (f32[504,128]{1,0:T(8,128)S(1)}, f32[504,128]{1,0:T(8,128)S(1)}, u32[]{:S(2)}, u32[]{:S(2)}) collective-permute-start(f32[504,128]{1,0:T(8,128)S(1)} %pad_maximum_fusion.1), channel_id=1, source_target_pairs={{0,112},{16,0},{32,16},{48,32},{64,48},{80,64},{96,80},{112,96},{1... | collective-permute-start | bytes 774152 | tf_op jit(solution)/shard_map/ppermute | solution.py:586
  52.7 17.4 %collective-permute-start.6 = (f32[32,3,8,128]{3,2,1,0:T(8,128)S(1)}, f32[32,3,8,128]{3,2,1,0:T(8,128)S(1)}, u32[]{:S(2)}, u32[]{:S(2)}) collective-permute-start(f32[32,3,8,128]{3,2,1,0:T(8,128)S(1)} %get-tuple-element.43), channel_id=1, source_target_pairs={{0,1},{1,2},{2,3},{3,4},{4,5},{5,6},{6,7},{7,8},{8,9},{9,10},{10,1... | collective-permute-start | bytes 1179656 | tf_op jit(solution)/shard_map/ppermute | solution.py:586
  54.5 15.5 %collective-permute-start.7 = (f32[32,3,8,128]{3,2,1,0:T(8,128)S(1)}, f32[32,3,8,128]{3,2,1,0:T(8,128)S(1)}, u32[]{:S(2)}, u32[]{:S(2)}) collective-permute-start(f32[32,3,8,128]{3,2,1,0:T(8,128)S(1)} %get-tuple-element.44), channel_id=1, source_target_pairs={{0,15},{1,0},{2,1},{3,2},{4,3},{5,4},{6,5},{7,6},{8,7},{9,8},{10,9... | collective-permute-start | bytes 1179656 | tf_op jit(solution)/shard_map/ppermute | solution.py:586
  54.7 15.3 %collective-permute-start.4 = (f32[384,128]{1,0:T(8,128)S(1)}, f32[384,128]{1,0:T(8,128)S(1)}, u32[]{:S(2)}, u32[]{:S(2)}) collective-permute-start(f32[384,128]{1,0:T(8,128)S(1)} %get-tuple-element.41), channel_id=1, source_target_pairs={{0,16},{16,32},{32,48},{48,64},{64,80},{80,96},{96,112},{112,0},{1... | collective-permute-start | bytes 589832 | tf_op jit(solution)/shard_map/ppermute | solution.py:586
  54.7 15.3 %collective-permute-start.5 = (f32[384,128]{1,0:T(8,128)S(1)}, f32[384,128]{1,0:T(8,128)S(1)}, u32[]{:S(2)}, u32[]{:S(2)}) collective-permute-start(f32[384,128]{1,0:T(8,128)S(1)} %get-tuple-element.42), channel_id=1, source_target_pairs={{0,112},{16,0},{32,16},{48,32},{64,48},{80,64},{96,80},{112,96},{1... | collective-permute-start | bytes 589832 | tf_op jit(solution)/shard_map/ppermute | solution.py:586
  73.4 19.9 %collective-permute-start.10 = (f32[32,3,8,128]{3,2,1,0:T(8,128)S(1)}, f32[32,3,8,128]{3,2,1,0:T(8,128)S(1)}, u32[]{:S(2)}, u32[]{:S(2)}) collective-permute-start(f32[32,3,8,128]{3,2,1,0:T(8,128)S(1)} %get-tuple-element.48), channel_id=1, source_target_pairs={{0,1},{1,2},{2,3},{3,4},{4,5},{5,6},{6,7},{7,8},{8,9},{9,10},{10,1... | collective-permute-start | bytes 1179656 | tf_op jit(solution)/shard_map/ppermute | solution.py:586
  75.5 17.7 %collective-permute-start.11 = (f32[32,3,8,128]{3,2,1,0:T(8,128)S(1)}, f32[32,3,8,128]{3,2,1,0:T(8,128)S(1)}, u32[]{:S(2)}, u32[]{:S(2)}) collective-permute-start(f32[32,3,8,128]{3,2,1,0:T(8,128)S(1)} %get-tuple-element.49), channel_id=1, source_target_pairs={{0,15},{1,0},{2,1},{3,2},{4,3},{5,4},{6,5},{7,6},{8,7},{9,8},{10,9... | collective-permute-start | bytes 1179656 | tf_op jit(solution)/shard_map/ppermute | solution.py:586
  77.9 15.3 %collective-permute-start.8 = (f32[384,128]{1,0:T(8,128)S(1)}, f32[384,128]{1,0:T(8,128)S(1)}, u32[]{:S(2)}, u32[]{:S(2)}) collective-permute-start(f32[384,128]{1,0:T(8,128)S(1)} %get-tuple-element.46), channel_id=1, source_target_pairs={{0,16},{16,32},{32,48},{48,64},{64,80},{80,96},{96,112},{112,0},{1... | collective-permute-start | bytes 589832 | tf_op jit(solution)/shard_map/ppermute | solution.py:586
  77.9 15.4 %collective-permute-start.9 = (f32[384,128]{1,0:T(8,128)S(1)}, f32[384,128]{1,0:T(8,128)S(1)}, u32[]{:S(2)}, u32[]{:S(2)}) collective-permute-start(f32[384,128]{1,0:T(8,128)S(1)} %get-tuple-element.47), channel_id=1, source_target_pairs={{0,112},{16,0},{32,16},{48,32},{64,48},{80,64},{96,80},{112,96},{1... | collective-permute-start | bytes 589832 | tf_op jit(solution)/shard_map/ppermute | solution.py:586
  96.6 33.9 %collective-permute-start.14 = (f32[32,6,8,128]{3,2,1,0:T(8,128)S(1)}, f32[32,6,8,128]{3,2,1,0:T(8,128)S(1)}, u32[]{:S(2)}, u32[]{:S(2)}) collective-permute-start(f32[32,6,8,128]{3,2,1,0:T(8,128)S(1)} %get-tuple-element.53), channel_id=1, source_target_pairs={{0,1},{1,2},{2,3},{3,4},{4,5},{5,6},{6,7},{7,8},{8,9},{9,10},{10,1... | collective-permute-start | bytes 2359304 | tf_op jit(solution)/shard_map/ppermute | solution.py:586
  96.7 33.8 %collective-permute-start.15 = (f32[32,6,8,128]{3,2,1,0:T(8,128)S(1)}, f32[32,6,8,128]{3,2,1,0:T(8,128)S(1)}, u32[]{:S(2)}, u32[]{:S(2)}) collective-permute-start(f32[32,6,8,128]{3,2,1,0:T(8,128)S(1)} %get-tuple-element.54), channel_id=1, source_target_pairs={{0,15},{1,0},{2,1},{3,2},{4,3},{5,4},{6,5},{7,6},{8,7},{9,8},{10,9... | collective-permute-start | bytes 2359304 | tf_op jit(solution)/shard_map/ppermute | solution.py:586
  101.1 20.2 %collective-permute-start.12 = (f32[768,128]{1,0:T(8,128)S(1)}, f32[768,128]{1,0:T(8,128)S(1)}, u32[]{:S(2)}, u32[]{:S(2)}) collective-permute-start(f32[768,128]{1,0:T(8,128)S(1)} %get-tuple-element.51), channel_id=1, source_target_pairs={{0,16},{16,32},{32,48},{48,64},{64,80},{80,96},{96,112},{112,0},{1... | collective-permute-start | bytes 1179656 | tf_op jit(solution)/shard_map/ppermute | solution.py:586
  101.1 20.2 %collective-permute-start.13 = (f32[768,128]{1,0:T(8,128)S(1)}, f32[768,128]{1,0:T(8,128)S(1)}, u32[]{:S(2)}, u32[]{:S(2)}) collective-permute-start(f32[768,128]{1,0:T(8,128)S(1)} %get-tuple-element.52), channel_id=1, source_target_pairs={{0,112},{16,0},{32,16},{48,32},{64,48},{80,64},{96,80},{112,96},{1... | collective-permute-start | bytes 1179656 | tf_op jit(solution)/shard_map/ppermute | solution.py:586
  121.3 6.5 %collective-permute-start.16 = (f32[30,8,128]{2,1,0:T(8,128)S(1)}, f32[30,8,128]{2,1,0:T(8,128)S(1)}, u32[]{:S(2)}, u32[]{:S(2)}) collective-permute-start(f32[30,8,128]{2,1,0:T(8,128)S(1)} %get-tuple-element.56), channel_id=1, source_target_pairs={{0,1},{1,2},{2,3},{3,4},{4,5},{5,6},{6,7},{7,8},{8,9},{9,10},{10,1... | collective-permute-start | bytes 368648 | tf_op jit(solution)/shard_map/ppermute | solution.py:586
  125.0 5.5 %collective-permute-start.17 = (f32[30,8,128]{2,1,0:T(8,128)S(1)}, f32[30,8,128]{2,1,0:T(8,128)S(1)}, u32[]{:S(2)}, u32[]{:S(2)}) collective-permute-start(f32[30,8,128]{2,1,0:T(8,128)S(1)} %get-tuple-element.57), channel_id=1, source_target_pairs={{0,15},{1,0},{2,1},{3,2},{4,3},{5,4},{6,5},{7,6},{8,7},{9,8},{10,9... | collective-permute-start | bytes 368648 | tf_op jit(solution)/shard_map/ppermute | solution.py:586

commit v3 on v2

--- a/solution.py
+++ b/solution.py
@@ -325,10 +325,16 @@
     return start * (1.0 / 3.0) + (2.0 / 3.0) * (current + rate)
 
 
+def turned_about(number, *pairs):
+    return [pair[::-1] if number % 2 else pair for pair in pairs]
+
+
 def edge_rate(
-    number, edge, acc_ref, start_ref, p_ref, v_ref, xlo_ref, xhi_ref, ylo_ref, yhi_ref,
+    number, edge, acc_ref, start_ref, p_ref, v_ref, x1_ref, x2_ref, y1_ref, y2_ref,
     new_ref, nxlo_ref, nxhi_ref, nylo_ref, nyhi_ref, side,
 ):
+    (xlo_ref, xhi_ref), (ylo_ref, yhi_ref) = turned_about(number, (x1_ref, x2_ref), (y1_ref, y2_ref))
+
     def from_rows(ref, x, y):
         return ref[pl.ds((x * 16 + y) * 8, 8), :]
 
@@ -429,7 +435,7 @@
         src = dst
 
 
-def pack_corners(xlo_ref, xhi_ref, _, low_ref, high_ref):
+def pack_corners(xhi_ref, xlo_ref, _, low_ref, high_ref):
     k = 0
     for dx in range(1, WIDE):
         for ref, x in ((xlo_ref, WIDE - dx), (xhi_ref, dx - 1)):
@@ -442,9 +448,119 @@
 CORNERS = WIDE * (WIDE - 1)
 
 
+def normals(last, xs, nx, ny, nz, at):
+    cols = {}
+
+    def col(y):
+        if y not in cols:
+            cols[y] = last[xs, y + WIDE]
+        return cols[y]
+
+    across, along, deep = {}, {}, {}
+    for y in range(-1, 17):
+        gx = last[xs + 1, y + WIDE] - last[xs - 1, y + WIDE]
+        gy = col(y + 1) - col(y - 1)
+        gz = shifted(col(y), 1) - shifted(col(y), -1)
+        scale = lax.rsqrt(gx * gx + gy * gy + gz * gz + 4.0)
+        across[y], along[y], deep[y] = gx * scale, gy * scale, gz * scale
+    for j in range(8):
+        a, b = 2 * j, 2 * j + 1
+        nx[at, j] = across[a] + across[b]
+        ny[at, j] = (along[b] + along[b + 1]) - (along[a - 1] + along[a])
+        nz[at, j] = deep[a] + deep[b]
+
+
+def gather(last, xs, nx, ny, nz, at, lump, slot, half, new, new_at):
+    a, b = at, at + 1
+    for j in range(8):
+        deep = nz[a, j] + nz[b, j]
+        total = (nx[b, j] + nx[b + 1, j]) - (nx[a - 1, j] + nx[a, j]) + (ny[a, j] + ny[b, j])
+        lump[pl.ds(slot * 64 + j * 8, 8), :] = total + (shifted(deep, 1) - shifted(deep, -1))
+        share = None
+        for x in range(2):
+            for y in range(2):
+                yy = 2 * j + y
+                col = last[xs + x, yy + WIDE]
+                new[pl.ds(new_at + x * 128 + (yy // 8) * 64 + yy % 8, 8, stride=8), :] = col
+                bend = jnp.tanh(col * (1.0 / FRONT))
+                share = bend if share is None else share + bend
+        lump[pl.ds(half + slot * 64 + j * 8, 8), :] = share
+
+
+def restrict(lump, slots, half, send, send_at):
+    k = lax.broadcasted_iota(jnp.int32, (256, 128), 0)
+    n = lax.broadcasted_iota(jnp.int32, (256, 128), 1)
+    table = jnp.where(lax.div(k, 2) == n, 1.0 / 16.0, 0.0)
+    halves = []
+    for odd_row in range(2):
+        rows = []
+        for kind in range(2):
+            for i in slots:
+                base = kind * half + i * 64 + odd_row
+                rows += [lump[pl.ds(base + 2 * z, 8, stride=8), :] for z in range(4)]
+        halves.append(jnp.concatenate(rows, axis=0))
+    out = jnp.dot(jnp.concatenate(halves, axis=1), table, precision=HIGH, preferred_element_type=jnp.float32)
+    for n, i in enumerate(slots):
+        send[send_at(i), pl.ds(0, 32), :] = out[n * 32 : n * 32 + 32]
+        send[send_at(i), pl.ds(32, 32), :] = out[(len(slots) + n) * 32 : (len(slots) + n) * 32 + 32] + 0.5
+
+
+def sweep_sides(
+    adv_ref, yhi_ref, ylo_ref, one_ref, two_ref, three_ref, four_ref,
+    rims_ref, last_ref, q0, q1, push, sign, even, odd,
+):
+    w = WIDE
+    size_y = 16 + 2 * w
+
+    def put(x, y, col):
+        q0[x, y] = col
+        push[x, y], sign[x, y] = pushes(col)
+
+    def fill(x):
+        for y in range(w):
+            put(x, y, ylo_ref[x, y])
+            put(x, y + 16 + w, yhi_ref[x, y])
+        for y in (0, 1, 2, 3, 12, 13, 14, 15):
+            put(x, y + w, adv_ref[x, y])
+
+    loop(0, 32, fill)
+    src, dst = q0, q1
+    for k, core_ref in enumerate((one_ref, two_ref, three_ref, four_ref), 1):
+        dst = last_ref if k == SWEEPS else dst
+        sides = [*range(k, k + w), *range(size_y - k - w, size_y - k)]
+        sweep_rows(src, dst, push, sign, lambda j, k=k: k + 2 * j, 16 - k, sides, even, odd)
+        inside = (k, k + 1, 14 - k, 15 - k) if k < SWEEPS else range(k, 16 - k)
+
+        def take(x, core_ref=core_ref, inside=inside, dst=dst):
+            for y in inside:
+                dst[x, y + w] = core_ref[x, y]
+
+        loop(k, 32 - k, take)
+        if k < SWEEPS:
+            for r, x in enumerate((k, k + 1, 30 - k, 31 - k)):
+                for y in range(k, size_y - k):
+                    inner = k + 2 <= y - w < 14 - k
+                    rims_ref[k - 1, r, y] = core_ref[x, y - w] if inner else dst[x, y]
+        src, dst = dst, src
+
+
+def inner_outputs(last, new_ref, send_ref, nx, ny, nz, lump):
+    loop(0, 22, lambda r: normals(last, r + 5, nx, ny, nz, r))
+
+    def planes(n):
+        gather(last, 2 * n + 6, nx, ny, nz, 2 * n + 1, lump, n, 640, new_ref, (2 * n + 6) * 128)
+
+    loop(0, 10, planes)
+    for x in (4, 5, 26, 27):
+        for y in range(16):
+            new_ref[pl.ds(x * 128 + (y // 8) * 64 + y % 8, 8, stride=8), :] = last[x, y + WIDE]
+    for part in range(2):
+        restrict(lump, range(5 * part, 5 * part + 5), 640, send_ref, lambda i: i)
+
+
 def finish(
-    adv_ref, xlo_ref, xhi_ref, ylo_ref, yhi_ref, clo_ref, chi_ref, one_ref, two_ref, three_ref, four_ref,
-    new_ref, send_ref, q0, q1, push, sign, nx, ny, nz, lump, even, odd,
+    adv_ref, xhi_ref, xlo_ref, yhi_ref, ylo_ref, clo_ref, chi_ref, rims_ref, rows_ref, send_mid_ref, _,
+    new_ref, send_ref, q0, q1, push, sign, nx, ny, nz, lump, even, odd, ends, sems,
 ):
     w = WIDE
     size_x, size_y = 32 + 2 * w, 16 + 2 * w
@@ -453,7 +569,8 @@
         q0[x, y] = col
         push[x, y], sign[x, y] = pushes(col)
 
-    def fill_mid(x):
+    def fill_mid(r):
+        x = r + jnp.where(r >= 4, 24, 0)
         for y in range(w):
             put(x + w, y, ylo_ref[x, y])
             put(x + w, y + 16 + w, yhi_ref[x, y])
@@ -465,7 +582,7 @@
             put(x, y + w, xlo_ref[pl.ds((x * 16 + y) * 8, 8), :])
             put(x + 32 + w, y + w, xhi_ref[pl.ds((x * 16 + y) * 8, 8), :])
 
-    loop(0, 32, fill_mid)
+    loop(0, 8, fill_mid)
     loop(0, w, fill_side)
     k = 0
     for dx in range(1, w):
@@ -476,89 +593,42 @@
                 k += 1
 
     src, dst = q0, q1
-    for k, core_ref in enumerate((one_ref, two_ref, three_ref, four_ref), 1):
+    for k in range(1, SWEEPS + 1):
+
         def end_rows(j, k=k):
             return k + 2 * j + jnp.where(j >= 3, 32 - 2 * k, 0)
 
         sweep_rows(src, dst, push, sign, end_rows, 6, range(k, size_y - k), even, odd)
-        sides = [*range(k, k + w), *range(size_y - k - w, size_y - k)]
-        sweep_rows(src, dst, push, sign, lambda j, k=k: w + k + 2 * j, 16 - k, sides, even, odd)
-        inside = range(k, 16 - k)
         if k < SWEEPS:
-            for x in (k, k + 1, 30 - k, 31 - k):
-                for y in inside:
-                    dst[x + w, y + w] = core_ref[x, y]
-            inside = (k, k + 1, 14 - k, 15 - k)
-
-        def take(x, core_ref=core_ref, inside=inside, dst=dst):
-            for y in inside:
-                dst[x + w, y + w] = core_ref[x, y]
-
-        loop(k, 32 - k, take)
+            for r, x in enumerate((k, k + 1, 30 - k, 31 - k)):
+                for y in range(k, size_y - k):
+                    dst[x + w, y] = rims_ref[k - 1, r, y]
         src, dst = dst, src
     last = src
 
-    def normals(x):
-        xs = x + w - 1
-        cols = {}
-
-        def at(y):
-            if y not in cols:
-                cols[y] = last[xs, y + w]
-            return cols[y]
-
-        across, along, deep = {}, {}, {}
-        for y in range(-1, 17):
-            gx = last[xs + 1, y + w] - last[xs - 1, y + w]
-            gy = at(y + 1) - at(y - 1)
-            gz = shifted(at(y), 1) - shifted(at(y), -1)
-            scale = lax.rsqrt(gx * gx + gy * gy + gz * gz + 4.0)
-            across[y], along[y], deep[y] = gx * scale, gy * scale, gz * scale
-        for j in range(8):
-            a, b = 2 * j, 2 * j + 1
-            nx[x, j] = across[a] + across[b]
-            ny[x, j] = (along[b] + along[b + 1]) - (along[a - 1] + along[a])
-            nz[x, j] = deep[a] + deep[b]
-
-    loop(0, 34, normals)
-
-    def gather(i):
-        a, b = 2 * i + 1, 2 * i + 2
-        for j in range(8):
-            deep = nz[a, j] + nz[b, j]
-            total = (nx[b, j] + nx[b + 1, j]) - (nx[a - 1, j] + nx[a, j]) + (ny[a, j] + ny[b, j])
-            lump[pl.ds(i * 64 + j * 8, 8), :] = total + (shifted(deep, 1) - shifted(deep, -1))
-            share = None
-            for x in range(2):
-                for y in range(2):
-                    xx, yy = 2 * i + x, 2 * j + y
-                    col = last[xx + w, yy + w]
-                    new_ref[pl.ds(xx * 128 + (yy // 8) * 64 + yy % 8, 8, stride=8), :] = col
-                    bend = jnp.tanh(col * (1.0 / FRONT))
-                    share = bend if share is None else share + bend
-            lump[pl.ds(1024 + i * 64 + j * 8, 8), :] = share
-
-    loop(0, 16, gather)
-
-    k = lax.broadcasted_iota(jnp.int32, (256, 128), 0)
-    n = lax.broadcasted_iota(jnp.int32, (256, 128), 1)
-    table = jnp.where(lax.div(k, 2) == n, 1.0 / 16.0, 0.0)
-
-    def restrict(g):
-        halves = []
-        for odd_row in range(2):
-            rows = []
-            for kind in range(2):
-                for i in range(4):
-                    base = kind * 1024 + (4 * g + i) * 64 + odd_row
-                    rows += [lump[pl.ds(base + 2 * z, 8, stride=8), :] for z in range(4)]
-            halves.append(jnp.concatenate(rows, axis=0))
-        out = jnp.dot(jnp.concatenate(halves, axis=1), table, precision=HIGH, preferred_element_type=jnp.float32)
-        for i in range(4):
-            send_ref[4 * g + i, pl.ds(0, 32), :] = out[i * 32 : i * 32 + 32]
-            send_ref[4 * g + i, pl.ds(32, 32), :] = out[128 + i * 32 : 160 + i * 32] + 0.5
-
-    loop(0, 4, restrict)
+    def take(r):
+        x = SWEEPS + r + jnp.where(r >= 4, 16, 0)
+        for y in range(SWEEPS, size_y - SWEEPS):
+            last[x + w, y] = rows_ref[x, y]
+
+    loop(0, 8, take)
+    loop(0, 16, lambda r: normals(last, r + w - 1 + jnp.where(r >= 8, 18, 0), nx, ny, nz, r))
+
+    def planes(n):
+        far = jnp.where(n >= 3, 1, 0)
+        gather(last, 2 * n + w + 20 * far, nx, ny, nz, 2 * n + 1 + 2 * far, lump, n, 384, ends, n * 256)
+
+    loop(0, 6, planes)
+    copies = [
+        pltpu.make_async_copy(ends.at[pl.ds(1024 * k, 512)], new_ref.at[pl.ds(3584 * k, 512)], sems.at[k])
+        for k in range(2)
+    ]
+    for copy in copies:
+        copy.start()
+    restrict(lump, range(6), 384, send_ref, lambda i: i + (10 if i >= 3 else 0))
+    send_ref[pl.ds(3, 10)] = send_mid_ref[...]
+    for copy in copies:
+        copy.wait()
 
 
 def call(kernel, outs, *args, scratch=(), mib=48, ops=1000, name=None, anywhere=(), aliases=None):
@@ -624,7 +694,7 @@
         x_edge, y_edge = f32(edge * 128, 128), f32(32, edge, *col)
         current, *edges = call(
             functools.partial(edge_rate, number, edge), (block, x_edge, x_edge, y_edge, y_edge),
-            acc, start, current, velocity, *halo,
+            acc, start, current, velocity, *sum(turned_about(number, halo[:2], halo[2:]), ()),
             scratch=[(6, 16, *col)], name="edge", mib=24, ops=512 * 30,
         )
         halo = star(*edges)
@@ -634,15 +704,26 @@
         scratch=[block.shape, block.shape, (2, 16, *col), (2, 16, *col)], name="core", mib=8, ops=512 * 90,
     )
     corner = f32(CORNERS, *col)
+    turns = [(2, 16 + 2 * WIDE, *col)] * 2
+    side = (32, 16 + 2 * WIDE, *col)
+    rims, last = call(
+        sweep_sides, (f32(3, 4, *side[1:]), f32(*side)), current, yhi, ylo, *levels,
+        scratch=[side] * 4 + turns, name="sides", mib=20, ops=512 * 70,
+    )
     corner_low, corner_high = call(
-        pack_corners, (corner, corner), xlo, xhi, levels[-1], name="corners", mib=4, anywhere=(2,)
+        pack_corners, (corner, corner), xhi, xlo, rims, name="corners", mib=4, anywhere=(2,)
+    )
+    new_rows, send_mid = call(
+        inner_outputs, (f32(4096, 128), f32(10, 64, 128)), last,
+        scratch=[(22, 8, *col)] * 3 + [(1280, 128)], name="outputs", mib=12, ops=512 * 40,
     )
     clo, chi = moved(corner_high, "gy", 1), moved(corner_low, "gy", -1)
     ext = (32 + 2 * WIDE, 16 + 2 * WIDE, *col)
     new_rows, packed = call(
-        finish, (f32(4096, 128), f32(16, 64, 128)), current, xlo, xhi, ylo, yhi, clo, chi, *levels,
-        scratch=[ext] * 4 + [(34, 8, *col)] * 3 + [(2048, 128), (2, 28, *col), (2, 28, *col)],
-        name="finish", mib=30, ops=512 * 250,
+        finish, (f32(4096, 128), f32(16, 64, 128)),
+        current, xhi, xlo, yhi, ylo, clo, chi, rims, last, send_mid, new_rows,
+        scratch=[ext] * 4 + [(16, 8, *col)] * 3 + [(768, 128)] + turns + [(1536, 128), pltpu.SemaphoreType.DMA((2,))],
+        name="finish", mib=30, ops=512 * 250, anywhere=(10,), aliases={10: 0},
     )
     returned = lax.all_to_all(packed, "gy", split_axis=0, concat_axis=0, tiled=True).reshape(16, 2, 4, 8, 128)
     new_level = new_rows.reshape(32, 2, 8, 8, 128).transpose(0, 1, 3, 2, 4).reshape(32, 16, 1024)

time: 172 us -> 159 us (0.924)
  starting transfers between devices: 46.6 us -> 33.2 us
    ppermute x18, starting transfers between devices: 38.8 us -> 25.5 us  [moved(): lax.ppermute(values, axis, [(i, (i + step) % count) for i in range(count)])]
    pallas_call x13 -> x15, Pallas kernels: 79.2 us -> 80 us  [call(): pl.pallas_call(kernel, out_shape=outs, in_specs=[spec(k) for k in range(l...]
  transfers between devices with their start and end apart: 19 -> 19, of which waited for: 4 -> 6; matrix products, arithmetic and copies ran while one was open for 2% -> 2% of each run, Pallas kernels for 26% -> 37%
where the time goes in v3:
time: 159 us; the launch traced here: 158 us
  Pallas kernels  80 us (50%)
  starting transfers between devices  33.2 us (21%)
  waiting for transfers between devices  21.4 us (13%)
  blocking collectives  16.1 us (10%)
  local copies, waits for them, and re-layouts  4.32 us (3%)
  other arithmetic  1.89 us (1%)
    pallas_call x15, Pallas kernels, call(): pl.pallas_call(kernel, out_shape=outs, in_specs=[spec(k) for k in range(l...  80 us
    ppermute x18, starting transfers between devices, moved(): lax.ppermute(values, axis, [(i, (i + step) % count) for i in range(count)])  25.5 us
    all_to_all x1, blocking collectives, per_device(): lax.all_to_all(packed, 'gy', split_axis=0, concat_axis=0, tiled=True)  16.1 us
    ppermute x18, waiting for transfers between devices, moved(): lax.ppermute(values, axis, [(i, (i + step) % count) for i in range(count)])  11.7 us
    all_to_all x1, waiting for transfers between devices, per_device(): coarse = lax.all_to_all(send, 'gy', split_axis=0, concat_axis=0, tiled=True)  9.73 us
    all_to_all x1, starting transfers between devices, per_device(): coarse = lax.all_to_all(send, 'gy', split_axis=0, concat_axis=0, tiled=True)  7.76 us
  transfers between devices with their start and end apart: 19, of which 6 were waited for; matrix products, arithmetic and copies ran while one was open for 2% of the time, Pallas kernels for 37%

profile of v3, /device:TPU:1, one launch (start us, length us, event | category | flops | bytes accessed | tf_op | source)
XLA Modules:
  0.0 157.7 jit_solution(10814178068094791566)
XLA Ops:
  0.6 1.1 copy-done.1
  1.8 1.3 pack.1
  3.0 7.8 %all-to-all-start = ((f32[16,120,128]{2,1,0:T(8,128)}), f32[16,120,128]{2,1,0:T(8,128)S(1)}, u32[]{:S(2)}, u32[]{:S(2)}) async-start(f32[16,120,128]{2,1,0:T(8,128)} %pack.1), calls=%async_computation | async-start | bytes 1966080 | tf_op jit(solution)/shard_map/all_to_all | solution.py:670
  10.8 0.0 copy-start
  10.8 1.6 %copy-done = f32[32,16,1024]{2,1,0:T(8,128)S(1)} copy-done((f32[32,16,1024]{2,1,0:T(8,128)S(1)}, f32[32,16,1024]{2,1,0:T(8,128)}, u32[]{:S(2)}) %copy-start) | copy-done | bytes 2097176
  12.4 1.4 unpack.1
  13.8 1.6 %collective-permute-start.2 = (f32[32,3,8,128]{3,2,1,0:T(8,128)}, f32[32,3,8,128]{3,2,1,0:T(8,128)S(1)}, u32[]{:S(2)}, u32[]{:S(2)}) collective-permute-start(f32[32,3,8,128]{3,2,1,0:T(8,128)} %get-tuple-element.42), channel_id=1, source_target_pairs={{0,1},{1,2},{2,3},{3,4},{4,5},{5,6},{6,7},{7,8},{8,9},{9,10},{10,1... | collective-permute-start | bytes 1179656 | tf_op jit(solution)/shard_map/ppermute | solution.py:656
  15.4 0.0 collective-permute-start.3
  15.4 0.8 fusion
  16.2 9.7 %all-to-all-done = f32[16,120,128]{2,1,0:T(8,128)S(1)} async-done(((f32[16,120,128]{2,1,0:T(8,128)}), f32[16,120,128]{2,1,0:T(8,128)S(1)}, u32[]{:S(2)}, u32[]{:S(2)}) %all-to-all-start) | async-done | bytes 983072 | tf_op jit(solution)/shard_map/all_to_all | solution.py:670
  25.9 0.9 pad_maximum_fusion
  26.8 1.4 collective-permute-start
  28.2 0.9 pad_maximum_fusion.1
  29.2 3.9 %collective-permute-start.1 = (f32[504,128]{1,0:T(8,128)S(1)}, f32[504,128]{1,0:T(8,128)S(1)}, u32[]{:S(2)}, u32[]{:S(2)}) collective-permute-start(f32[504,128]{1,0:T(8,128)S(1)} %pad_maximum_fusion.1), channel_id=1, source_target_pairs={{0,112},{16,0},{32,16},{48,32},{64,48},{80,64},{96,80},{112,96},{1... | collective-permute-start | bytes 774152 | tf_op jit(solution)/shard_map/ppermute | solution.py:656
  33.0 3.9 %refine.1 = (f32[3,32,16,8,128]{4,3,2,1,0:T(8,128)S(1)}, f32[2,240,128]{2,1,0:T(8,128)S(1)}) custom-call(f32[1920,128]{1,0:T(8,128)S(1)} %bitcast.35, s32[2,1,64]{2,1,0:T(1,128)S(1)} %copy-done.2), custom_call_target="tpu_custom_call" | custom-call | flops 1024000 | bytes 8388608 | tf_op jit(solution)/shard_map/refine/pallas_call | solution.py:641
  36.9 9.7 %inner.3.acc_in = f32[32,16,8,128]{3,2,1,0:T(8,128)S(1)} custom-call(f32[32,16,8,128]{3,2,1,0:T(8,128)S(1)} %get-tuple-element.37.p_ref.start_ref, f32[3,32,16,8,128]{4,3,2,1,0:T(8,128)S(1)} %get-tuple-element.39.v_ref.v_in), custom_call_target="tpu_custom_call" | custom-call | flops 73400320 | bytes 8388608 | tf_op jit(solution)/shard_map/inner/pallas_call | solution.py:641
  46.7 0.0 collective-permute-done.lo_ref.x1_ref
  46.7 0.0 collective-permute-done.1.hi_ref.x2_ref
  46.7 1.8 %ends.1 = (f32[3,32,16,8,128]{4,3,2,1,0:T(8,128)S(1)}, f32[32,16,8,128]{3,2,1,0:T(8,128)S(1)}) custom-call(f32[504,128]{1,0:T(8,128)S(1)} %collective-permute-done.lo_ref.x1_ref, f32[504,128]{1,0:T(8,128)S(1)} %collective-permute-done.1.hi_ref.x2_ref, f32[2,240,128]{2,1,0:T(8,128)S(1)} %get-tuple-element.38.ends_ref, ...), custom_call_target="tpu_custom_call", output_to_operand_aliasing={{0}: (5, {}), {1}: (6, {})} | custom-call | flops 1024000 | bytes 8388608 | tf_op jit(solution)/shard_map/ends/pallas_call | solution.py:641
  48.5 0.0 collective-permute-done.2.y1_ref
  48.5 4.0 %edge.3 = (f32[32,16,8,128]{3,2,1,0:T(8,128)S(1)}, f32[384,128]{1,0:T(8,128)S(1)}, f32[384,128]{1,0:T(8,128)S(1)}, f32[32,3,8,128]{3,2,1,0:T(8,128)S(1)}, f32[32,3,8,128]{3,2,1,0:T(8,128)S(1)}) custom-call(f32[32,16,8,128]{3,2,1,0:T(8,128)S(1)} %get-tuple-element.40.acc_ref, f32[32,16,8,128]{3,2,1,0:T(8,128)S(1)} %get-tuple-element.37.p_ref.start_ref, ...), custom_call_target="tpu_custom_call" | custom-call | flops 15728640 | bytes 8388608 | tf_op jit(solution)/shard_map/edge/pallas_call | solution.py:641
  52.5 2.0 %collective-permute-start.6 = (f32[32,3,8,128]{3,2,1,0:T(8,128)S(1)}, f32[32,3,8,128]{3,2,1,0:T(8,128)S(1)}, u32[]{:S(2)}, u32[]{:S(2)}) collective-permute-start(f32[32,3,8,128]{3,2,1,0:T(8,128)S(1)} %get-tuple-element.47), channel_id=1, source_target_pairs={{0,15},{1,0},{2,1},{3,2},{4,3},{5,4},{6,5},{7,6},{8,7},{9,8},{10,9... | collective-permute-start | bytes 1179656 | tf_op jit(solution)/shard_map/ppermute | solution.py:656
  54.5 1.3 collective-permute-start.4
  55.8 0.2 collective-permute-start.5
  56.0 10.3 %inner.4.acc_ref = f32[32,16,8,128]{3,2,1,0:T(8,128)S(1)} custom-call(f32[32,16,8,128]{3,2,1,0:T(8,128)S(1)} %get-tuple-element.44.p_ref, f32[3,32,16,8,128]{4,3,2,1,0:T(8,128)S(1)} %get-tuple-element.41.v_ref), custom_call_target="tpu_custom_call" | custom-call | flops 73400320 | bytes 8388608 | tf_op jit(solution)/shard_map/inner/pallas_call | solution.py:641
  66.2 1.2 collective-permute-done.4.x1_ref
  67.5 2.0 %collective-permute-done.5.x2_ref = f32[384,128]{1,0:T(8,128)S(1)} collective-permute-done((f32[384,128]{1,0:T(8,128)S(1)}, f32[384,128]{1,0:T(8,128)S(1)}, u32[]{:S(2)}, u32[]{:S(2)}) %collective-permute-start.5) | collective-permute-done | bytes 196640 | tf_op jit(solution)/shard_map/ppermute | solution.py:656
  69.5 3.3 %edge.4 = (f32[32,16,8,128]{3,2,1,0:T(8,128)S(1)}, f32[384,128]{1,0:T(8,128)S(1)}, f32[384,128]{1,0:T(8,128)S(1)}, f32[32,3,8,128]{3,2,1,0:T(8,128)S(1)}, f32[32,3,8,128]{3,2,1,0:T(8,128)S(1)}) custom-call(f32[32,16,8,128]{3,2,1,0:T(8,128)S(1)} %inner.4.acc_ref, f32[32,16,8,128]{3,2,1,0:T(8,128)S(1)} %get-tuple-element.37.p_ref.start_ref, ...), custom_call_target="tpu_custom_call" | custom-call | flops 15728640 | bytes 8388608 | tf_op jit(solution)/shard_map/edge/pallas_call | solution.py:641
  72.8 0.1 collective-permute-start.10
  72.9 0.7 collective-permute-start.11
  73.5 5.1 %collective-permute-start.9 = (f32[384,128]{1,0:T(8,128)S(1)}, f32[384,128]{1,0:T(8,128)S(1)}, u32[]{:S(2)}, u32[]{:S(2)}) collective-permute-start(f32[384,128]{1,0:T(8,128)S(1)} %get-tuple-element.51), channel_id=1, source_target_pairs={{0,112},{16,0},{32,16},{48,32},{64,48},{80,64},{96,80},{112,96},{1... | collective-permute-start | bytes 589832 | tf_op jit(solution)/shard_map/ppermute | solution.py:656
  78.6 10.3 %inner.5.acc_ref = f32[32,16,8,128]{3,2,1,0:T(8,128)S(1)} custom-call(f32[32,16,8,128]{3,2,1,0:T(8,128)S(1)} %get-tuple-element.49.p_ref, f32[3,32,16,8,128]{4,3,2,1,0:T(8,128)S(1)} %get-tuple-element.41.v_ref), custom_call_target="tpu_custom_call" | custom-call | flops 73400320 | bytes 8388608 | tf_op jit(solution)/shard_map/inner/pallas_call | solution.py:641
  88.9 3.3 %edge.5 = (f32[32,16,8,128]{3,2,1,0:T(8,128)S(1)}, f32[768,128]{1,0:T(8,128)S(1)}, f32[768,128]{1,0:T(8,128)S(1)}, f32[32,6,8,128]{3,2,1,0:T(8,128)S(1)}, f32[32,6,8,128]{3,2,1,0:T(8,128)S(1)}) custom-call(f32[32,16,8,128]{3,2,1,0:T(8,128)S(1)} %inner.5.acc_ref, f32[32,16,8,128]{3,2,1,0:T(8,128)S(1)} %get-tuple-element.37.p_ref.start_ref, ...), custom_call_target="tpu_custom_call" | custom-call | flops 15728640 | bytes 8388608 | tf_op jit(solution)/shard_map/edge/pallas_call | solution.py:641
  92.2 4.4 %collective-permute-start.14 = (f32[32,6,8,128]{3,2,1,0:T(8,128)S(1)}, f32[32,6,8,128]{3,2,1,0:T(8,128)S(1)}, u32[]{:S(2)}, u32[]{:S(2)}) collective-permute-start(f32[32,6,8,128]{3,2,1,0:T(8,128)S(1)} %get-tuple-element.57), channel_id=1, source_target_pairs={{0,15},{1,0},{2,1},{3,2},{4,3},{5,4},{6,5},{7,6},{8,7},{9,8},{10,9... | collective-permute-start | bytes 2359304 | tf_op jit(solution)/shard_map/ppermute | solution.py:656
  96.6 0.5 collective-permute-start.12
  97.1 1.0 collective-permute-start.13
  98.1 7.5 %core.1 = (f32[32,16,8,128]{3,2,1,0:T(8,128)S(1)}, f32[32,16,8,128]{3,2,1,0:T(8,128)S(1)}, f32[32,16,8,128]{3,2,1,0:T(8,128)S(1)}, f32[32,16,8,128]{3,2,1,0:T(8,128)S(1)}) custom-call(f32[32,16,8,128]{3,2,1,0:T(8,128)S(1)} %get-tuple-element.54.adv_ref), custom_call_target="tpu_custom_call" | custom-call | flops 47185920 | bytes 8388608 | tf_op jit(solution)/shard_map/core/pallas_call | solution.py:641
  105.6 6.4 %collective-permute-done.14.yhi_ref = f32[32,6,8,128]{3,2,1,0:T(8,128)S(1)} collective-permute-done((f32[32,6,8,128]{3,2,1,0:T(8,128)S(1)}, f32[32,6,8,128]{3,2,1,0:T(8,128)S(1)}, u32[]{:S(2)}, u32[]{:S(2)}) %collective-permute-start.14) | collective-permute-done | bytes 786464 | tf_op jit(solution)/shard_map/ppermute | solution.py:656
  112.0 1.8 %collective-permute-done.15.ylo_ref = f32[32,6,8,128]{3,2,1,0:T(8,128)S(1)} collective-permute-done((f32[32,6,8,128]{3,2,1,0:T(8,128)S(1)}, f32[32,6,8,128]{3,2,1,0:T(8,128)S(1)}, u32[]{:S(2)}, u32[]{:S(2)}) %collective-permute-start.15) | collective-permute-done | bytes 786464 | tf_op jit(solution)/shard_map/ppermute | solution.py:656
  113.8 8.3 %sides.1 = (f32[3,4,28,8,128]{4,3,2,1,0:T(8,128)S(1)}, f32[32,28,8,128]{3,2,1,0:T(8,128)S(1)}) custom-call(f32[32,16,8,128]{3,2,1,0:T(8,128)S(1)} %get-tuple-element.54.adv_ref, f32[32,6,8,128]{3,2,1,0:T(8,128)S(1)} %collective-permute-done.14.yhi_ref, f32[32,6,8,128]{3,2,1,0:T(8,128)S(1)} %collective-permute-done.15.ylo_ref, ...), custom_call_target="tpu_custom_call" | custom-call | flops 36700160 | bytes 8388608 | tf_op jit(solution)/shard_map/sides/pallas_call | solution.py:641
  122.1 0.1 collective-permute-done.12.xhi_ref
  122.2 0.0 collective-permute-done.13.xlo_ref
  122.3 2.4 %collective-permute-start.16 = (f32[30,8,128]{2,1,0:T(8,128)S(1)}, f32[30,8,128]{2,1,0:T(8,128)S(1)}, u32[]{:S(2)}, u32[]{:S(2)}) collective-permute-start(f32[30,8,128]{2,1,0:T(8,128)S(1)} %get-tuple-element.64), channel_id=1, source_target_pairs={{0,1},{1,2},{2,3},{3,4},{4,5},{5,6},{6,7},{7,8},{8,9},{9,10},{10,1... | collective-permute-start | bytes 368648 | tf_op jit(solution)/shard_map/ppermute | solution.py:656
  124.7 1.1 collective-permute-start.17
  125.8 5.7 %outputs.1 = (f32[4096,128]{1,0:T(8,128)}, f32[10,64,128]{2,1,0:T(8,128)S(1)}) custom-call(f32[32,28,8,128]{3,2,1,0:T(8,128)S(1)} %get-tuple-element.66.last.rows_ref), custom_call_target="tpu_custom_call" | custom-call | flops 20971520 | bytes 8388608 | tf_op jit(solution)/shard_map/outputs/pallas_call | solution.py:641
  131.5 9.4 %finish.1 = (f32[4096,128]{1,0:T(8,128)}, f32[16,64,128]{2,1,0:T(8,128)S(1)}) custom-call(f32[32,16,8,128]{3,2,1,0:T(8,128)S(1)} %get-tuple-element.54.adv_ref, f32[768,128]{1,0:T(8,128)S(1)} %collective-permute-done.12.xhi_ref, f32[768,128]{1,0:T(8,128)S(1)} %collective-permute-done.13.xlo_ref, ...), custom_call_target="tpu_custom_call", output_to_operand_aliasing={{0}: (10, {})} | custom-call | flops 131072000 | bytes 8388608 | tf_op jit(solution)/shard_map/finish/pallas_call | solution.py:641
  140.8 16.1 %all_to_all.10 = f32[16,64,128]{2,1,0:T(8,128)S(1)} all-to-all(f32[16,64,128]{2,1,0:T(8,128)S(1)} %get-tuple-element.70), channel_id=1, replica_groups=mesh['gx'=8,'gy'=16] {'gy'}, dimensions={0} | all-to-all | bytes 1048576 | tf_op jit(solution)/shard_map/all_to_all | solution.py:728
  156.9 0.8 slice_bitcast_fusion
  (17 shorter events, 0.1 us)
Async XLA Ops:
  0.6 1.1 copy-start.1
  3.0 22.8 %all-to-all-start = ((f32[16,120,128]{2,1,0:T(8,128)}), f32[16,120,128]{2,1,0:T(8,128)S(1)}, u32[]{:S(2)}, u32[]{:S(2)}) async-start(f32[16,120,128]{2,1,0:T(8,128)} %pack.1), calls=%async_computation | async-start | bytes 1966080 | tf_op jit(solution)/shard_map/all_to_all | solution.py:670
  10.8 22.2 %copy-start.2 = (s32[2,1,64]{2,1,0:T(1,128)S(1)}, s32[2,1,64]{2,1,0:T(1,128)}, u32[]{:S(2)}) copy-start(s32[2,1,64]{2,1,0:T(1,128)} %band_ref.3) | copy-start | bytes 1540
  10.8 1.6 %copy-start = (f32[32,16,1024]{2,1,0:T(8,128)S(1)}, f32[32,16,1024]{2,1,0:T(8,128)}, u32[]{:S(2)}) copy-start(f32[32,16,1024]{2,1,0:T(8,128)} %param.3) | copy-start | bytes 6291460
  13.8 34.7 %collective-permute-start.2 = (f32[32,3,8,128]{3,2,1,0:T(8,128)}, f32[32,3,8,128]{3,2,1,0:T(8,128)S(1)}, u32[]{:S(2)}, u32[]{:S(2)}) collective-permute-start(f32[32,3,8,128]{3,2,1,0:T(8,128)} %get-tuple-element.42), channel_id=1, source_target_pairs={{0,1},{1,2},{2,3},{3,4},{4,5},{5,6},{6,7},{7,8},{8,9},{9,10},{10,1... | collective-permute-start | bytes 1179656 | tf_op jit(solution)/shard_map/ppermute | solution.py:656
  15.4 33.1 %collective-permute-start.3 = (f32[32,3,8,128]{3,2,1,0:T(8,128)}, f32[32,3,8,128]{3,2,1,0:T(8,128)}, u32[]{:S(2)}, u32[]{:S(2)}) collective-permute-start(f32[32,3,8,128]{3,2,1,0:T(8,128)} %get-tuple-element.43), channel_id=1, source_target_pairs={{0,15},{1,0},{2,1},{3,2},{4,3},{5,4},{6,5},{7,6},{8,7},{9,8},{10,9... | collective-permute-start | bytes 1179656 | tf_op jit(solution)/shard_map/ppermute | solution.py:656
  26.8 19.8 %collective-permute-start = (f32[504,128]{1,0:T(8,128)S(1)}, f32[504,128]{1,0:T(8,128)S(1)}, u32[]{:S(2)}, u32[]{:S(2)}) collective-permute-start(f32[504,128]{1,0:T(8,128)S(1)} %pad_maximum_fusion), channel_id=1, source_target_pairs={{0,16},{16,32},{32,48},{48,64},{64,80},{80,96},{96,112},{112,0},{1... | collective-permute-start | bytes 774152 | tf_op jit(solution)/shard_map/ppermute | solution.py:656
  29.2 17.5 %collective-permute-start.1 = (f32[504,128]{1,0:T(8,128)S(1)}, f32[504,128]{1,0:T(8,128)S(1)}, u32[]{:S(2)}, u32[]{:S(2)}) collective-permute-start(f32[504,128]{1,0:T(8,128)S(1)} %pad_maximum_fusion.1), channel_id=1, source_target_pairs={{0,112},{16,0},{32,16},{48,32},{64,48},{80,64},{96,80},{112,96},{1... | collective-permute-start | bytes 774152 | tf_op jit(solution)/shard_map/ppermute | solution.py:656
  52.5 17.0 %collective-permute-start.6 = (f32[32,3,8,128]{3,2,1,0:T(8,128)S(1)}, f32[32,3,8,128]{3,2,1,0:T(8,128)S(1)}, u32[]{:S(2)}, u32[]{:S(2)}) collective-permute-start(f32[32,3,8,128]{3,2,1,0:T(8,128)S(1)} %get-tuple-element.47), channel_id=1, source_target_pairs={{0,15},{1,0},{2,1},{3,2},{4,3},{5,4},{6,5},{7,6},{8,7},{9,8},{10,9... | collective-permute-start | bytes 1179656 | tf_op jit(solution)/shard_map/ppermute | solution.py:656
  54.5 15.0 %collective-permute-start.7 = (f32[32,3,8,128]{3,2,1,0:T(8,128)S(1)}, f32[32,3,8,128]{3,2,1,0:T(8,128)S(1)}, u32[]{:S(2)}, u32[]{:S(2)}) collective-permute-start(f32[32,3,8,128]{3,2,1,0:T(8,128)S(1)} %get-tuple-element.48), channel_id=1, source_target_pairs={{0,1},{1,2},{2,3},{3,4},{4,5},{5,6},{6,7},{7,8},{8,9},{9,10},{10,1... | collective-permute-start | bytes 1179656 | tf_op jit(solution)/shard_map/ppermute | solution.py:656
  54.5 13.0 %collective-permute-start.4 = (f32[384,128]{1,0:T(8,128)S(1)}, f32[384,128]{1,0:T(8,128)S(1)}, u32[]{:S(2)}, u32[]{:S(2)}) collective-permute-start(f32[384,128]{1,0:T(8,128)S(1)} %get-tuple-element.45), channel_id=1, source_target_pairs={{0,112},{16,0},{32,16},{48,32},{64,48},{80,64},{96,80},{112,96},{1... | collective-permute-start | bytes 589832 | tf_op jit(solution)/shard_map/ppermute | solution.py:656
  55.8 13.7 %collective-permute-start.5 = (f32[384,128]{1,0:T(8,128)S(1)}, f32[384,128]{1,0:T(8,128)S(1)}, u32[]{:S(2)}, u32[]{:S(2)}) collective-permute-start(f32[384,128]{1,0:T(8,128)S(1)} %get-tuple-element.46), channel_id=1, source_target_pairs={{0,16},{16,32},{32,48},{48,64},{64,80},{80,96},{96,112},{112,0},{1... | collective-permute-start | bytes 589832 | tf_op jit(solution)/shard_map/ppermute | solution.py:656
  72.8 16.1 %collective-permute-start.10 = (f32[32,3,8,128]{3,2,1,0:T(8,128)S(1)}, f32[32,3,8,128]{3,2,1,0:T(8,128)S(1)}, u32[]{:S(2)}, u32[]{:S(2)}) collective-permute-start(f32[32,3,8,128]{3,2,1,0:T(8,128)S(1)} %get-tuple-element.52), channel_id=1, source_target_pairs={{0,1},{1,2},{2,3},{3,4},{4,5},{5,6},{6,7},{7,8},{8,9},{9,10},{10,1... | collective-permute-start | bytes 1179656 | tf_op jit(solution)/shard_map/ppermute | solution.py:656
  72.9 16.0 %collective-permute-start.11 = (f32[32,3,8,128]{3,2,1,0:T(8,128)S(1)}, f32[32,3,8,128]{3,2,1,0:T(8,128)S(1)}, u32[]{:S(2)}, u32[]{:S(2)}) collective-permute-start(f32[32,3,8,128]{3,2,1,0:T(8,128)S(1)} %get-tuple-element.53), channel_id=1, source_target_pairs={{0,15},{1,0},{2,1},{3,2},{4,3},{5,4},{6,5},{7,6},{8,7},{9,8},{10,9... | collective-permute-start | bytes 1179656 | tf_op jit(solution)/shard_map/ppermute | solution.py:656
  73.5 15.3 %collective-permute-start.8 = (f32[384,128]{1,0:T(8,128)S(1)}, f32[384,128]{1,0:T(8,128)S(1)}, u32[]{:S(2)}, u32[]{:S(2)}) collective-permute-start(f32[384,128]{1,0:T(8,128)S(1)} %get-tuple-element.50), channel_id=1, source_target_pairs={{0,16},{16,32},{32,48},{48,64},{64,80},{80,96},{96,112},{112,0},{1... | collective-permute-start | bytes 589832 | tf_op jit(solution)/shard_map/ppermute | solution.py:656
  73.5 15.4 %collective-permute-start.9 = (f32[384,128]{1,0:T(8,128)S(1)}, f32[384,128]{1,0:T(8,128)S(1)}, u32[]{:S(2)}, u32[]{:S(2)}) collective-permute-start(f32[384,128]{1,0:T(8,128)S(1)} %get-tuple-element.51), channel_id=1, source_target_pairs={{0,112},{16,0},{32,16},{48,32},{64,48},{80,64},{96,80},{112,96},{1... | collective-permute-start | bytes 589832 | tf_op jit(solution)/shard_map/ppermute | solution.py:656
  92.2 19.7 %collective-permute-start.14 = (f32[32,6,8,128]{3,2,1,0:T(8,128)S(1)}, f32[32,6,8,128]{3,2,1,0:T(8,128)S(1)}, u32[]{:S(2)}, u32[]{:S(2)}) collective-permute-start(f32[32,6,8,128]{3,2,1,0:T(8,128)S(1)} %get-tuple-element.57), channel_id=1, source_target_pairs={{0,15},{1,0},{2,1},{3,2},{4,3},{5,4},{6,5},{7,6},{8,7},{9,8},{10,9... | collective-permute-start | bytes 2359304 | tf_op jit(solution)/shard_map/ppermute | solution.py:656
  96.6 17.2 %collective-permute-start.15 = (f32[32,6,8,128]{3,2,1,0:T(8,128)S(1)}, f32[32,6,8,128]{3,2,1,0:T(8,128)S(1)}, u32[]{:S(2)}, u32[]{:S(2)}) collective-permute-start(f32[32,6,8,128]{3,2,1,0:T(8,128)S(1)} %get-tuple-element.58), channel_id=1, source_target_pairs={{0,1},{1,2},{2,3},{3,4},{4,5},{5,6},{6,7},{7,8},{8,9},{9,10},{10,1... | collective-permute-start | bytes 2359304 | tf_op jit(solution)/shard_map/ppermute | solution.py:656
  96.6 25.6 %collective-permute-start.12 = (f32[768,128]{1,0:T(8,128)S(1)}, f32[768,128]{1,0:T(8,128)S(1)}, u32[]{:S(2)}, u32[]{:S(2)}) collective-permute-start(f32[768,128]{1,0:T(8,128)S(1)} %get-tuple-element.55), channel_id=1, source_target_pairs={{0,112},{16,0},{32,16},{48,32},{64,48},{80,64},{96,80},{112,96},{1... | collective-permute-start | bytes 1179656 | tf_op jit(solution)/shard_map/ppermute | solution.py:656
  97.1 25.1 %collective-permute-start.13 = (f32[768,128]{1,0:T(8,128)S(1)}, f32[768,128]{1,0:T(8,128)S(1)}, u32[]{:S(2)}, u32[]{:S(2)}) collective-permute-start(f32[768,128]{1,0:T(8,128)S(1)} %get-tuple-element.56), channel_id=1, source_target_pairs={{0,16},{16,32},{32,48},{48,64},{64,80},{80,96},{96,112},{112,0},{1... | collective-permute-start | bytes 1179656 | tf_op jit(solution)/shard_map/ppermute | solution.py:656
  122.3 9.2 %collective-permute-start.16 = (f32[30,8,128]{2,1,0:T(8,128)S(1)}, f32[30,8,128]{2,1,0:T(8,128)S(1)}, u32[]{:S(2)}, u32[]{:S(2)}) collective-permute-start(f32[30,8,128]{2,1,0:T(8,128)S(1)} %get-tuple-element.64), channel_id=1, source_target_pairs={{0,1},{1,2},{2,3},{3,4},{4,5},{5,6},{6,7},{7,8},{8,9},{9,10},{10,1... | collective-permute-start | bytes 368648 | tf_op jit(solution)/shard_map/ppermute | solution.py:656
  124.7 6.7 %collective-permute-start.17 = (f32[30,8,128]{2,1,0:T(8,128)S(1)}, f32[30,8,128]{2,1,0:T(8,128)S(1)}, u32[]{:S(2)}, u32[]{:S(2)}) collective-permute-start(f32[30,8,128]{2,1,0:T(8,128)S(1)} %get-tuple-element.65), channel_id=1, source_target_pairs={{0,15},{1,0},{2,1},{3,2},{4,3},{5,4},{6,5},{7,6},{8,7},{9,8},{10,9... | collective-permute-start | bytes 368648 | tf_op jit(solution)/shard_map/ppermute | solution.py:656

commit v4 on v3

--- a/solution.py
+++ b/solution.py
@@ -133,12 +133,6 @@
     return upwind_part(speed, slope - (p1 - m1), corr)
 
 
-def depth_part(col, speed):
-    before, after = shifted(col, -1), shifted(col, 1)
-    here = (after - col) - (col - before)
-    return depth_rate(6.0 * (after - before), here, [shifted(here, step) for step in (-2, -1, 1, 2)], speed)
-
-
 def loop(low, high, body):
     def step(i, carry):
         body(i)
@@ -240,7 +234,7 @@
         v_ref[c, x, y] = 0.75 * scaled[m] + 0.25 * scaled[m - 1 + 2 * (y % 2)]
 
 
-def refine_ends(lo_ref, hi_ref, ends_ref, band_ref, p_ref, v_in, acc_in, v_out, acc_out, fine, ends, part, sems):
+def refine_ends(lo_ref, hi_ref, ends_ref, band_ref, p_ref, tips_ref, v_in, acc_in, v_out, acc_out, fine, ends, part, sems):
     table = refine_table()
     blocks = band_blocks(band_ref)
     for side, ref in enumerate((lo_ref, hi_ref)):
@@ -258,7 +252,8 @@
         x = 31 * side
         march = March(lambda y: p_ref[x, y])
         for y in range(16):
-            total = depth_part(march.p(y), ends[2, side, y])
+            speed = ends[2, side, y]
+            total = speed * jnp.where(speed < 0, tips_ref[side, 0, y], tips_ref[side, 1, y])
             if 3 <= y < 13:
                 total = total + march.part(y, ends[1, side, y])
             part[side, y] = total
@@ -274,7 +269,7 @@
         copy.wait()
 
 
-def inner_rate(first, p_ref, v_ref, acc_ref, curve, slope, even, odd):
+def inner_rate(p_ref, v_ref, acc_ref, curve, slope, even, odd):
     def x_line(y):
         march = March(lambda x: p_ref[x, y])
         for x in range(32):
@@ -303,18 +298,104 @@
                 total = total + march.part(y, v_ref[1, x, y])
             acc_ref[x, y] = total
 
-    low = 1 if first else 0
-    count = 30 if first else 32
-    turn(low, even)
+    turn(0, even)
 
     def two(k):
-        x = low + 2 * k
+        x = 2 * k
         turn(x + 1, odd)
         y_line(x, even)
         turn(jnp.minimum(x + 2, 31), even)
         y_line(x + 1, odd)
 
-    loop(0, count // 2, two)
+    loop(0, 16, two)
+
+
+def depth_both(slope, here, turned):
+    m2, m1, p1, p2 = turned
+    gm2, gm1, g0, g1 = m1 - m2, here - m1, p1 - here, p2 - p1
+    bm2, bm1, b0, b1 = [(4.0 / 3.0) * (g * g) + EPS for g in (gm2, gm1, g0, g1)]
+    third = g0 - gm1
+    below = correction(bm2 + m1 * (m1 + gm2), bm1 + m1 * here, b0 + here * (here - g0), gm1 - gm2, third)
+    above = correction(b1 + p1 * (p1 - g1), b0 + p1 * here, bm1 + here * (here + gm1), g1 - g0, third)
+    central = slope - (p1 - m1)
+    return central - below, central + above
+
+
+def depth_sides(p_ref, both_ref, tips_ref, curve, slope, even, odd):
+    def curves(x):
+        for y in range(16):
+            col = p_ref[x, y]
+            before, after = shifted(col, -1), shifted(col, 1)
+            curve[x, y] = (after - col) - (col - before)
+            slope[x, y] = 6.0 * (after - before)
+
+    def turned_row(x, turned):
+        for y in range(16):
+            col = curve[x, y]
+            for k, step in enumerate((-2, -1, 1, 2)):
+                turned[k, y] = shifted(col, step)
+
+    def rates(x, turned):
+        for y in range(16):
+            both = depth_both(slope[x, y], curve[x, y], [turned[k, y] for k in range(4)])
+            both_ref[0, x, y], both_ref[1, x, y] = both
+
+    for x in range(3):
+        curves(x)
+    turned_row(0, even)
+
+    def two(k):
+        x = 2 * k
+        turned_row(x + 1, odd)
+        rates(x, even)
+        turned_row(jnp.minimum(x + 2, 31), even)
+        rates(x + 1, odd)
+        curves(jnp.minimum(x + 3, 31))
+        curves(jnp.minimum(x + 4, 31))
+
+    loop(0, 16, two)
+    for side in range(2):
+        for k in range(2):
+            for y in range(16):
+                tips_ref[side, k, y] = both_ref[k, 31 * side, y]
+
+
+def inner_rate_first(p_ref, v_ref, both_ref, acc_ref):
+    def x_line(y):
+        march = March(lambda x: p_ref[x, y])
+        for x in range(32):
+            if 3 <= x < 29:
+                acc_ref[x, y] = march.part(x, v_ref[0, x, y])
+            else:
+                acc_ref[x, y] = jnp.zeros((ROWS, LANES), jnp.float32)
+
+    def y_line(x):
+        march = March(lambda y: p_ref[x, y])
+        for y in range(16):
+            speed = v_ref[2, x, y]
+            total = acc_ref[x, y] + speed * jnp.where(speed < 0, both_ref[0, x, y], both_ref[1, x, y])
+            if 3 <= y < 13:
+                total = total + march.part(y, v_ref[1, x, y])
+            acc_ref[x, y] = total
+
+    loop(0, 16, x_line)
+    loop(1, 31, y_line)
+
+
+def refine_and_rate(mid_ref, band_ref, p_ref, both_ref, v_ref, ends_ref, acc_ref, fine, band):
+    refine_inner(mid_ref, band_ref, v_ref, ends_ref, fine, band)
+    inner_rate_first(p_ref, v_ref, both_ref, acc_ref)
+
+
+def join_x(p_ref, coarse_ref, mark_ref, low_ref, high_ref):
+    for x in range(3):
+        for y in range(16):
+            at = pl.ds((x * 16 + y) * 8, 8)
+            low_ref[at, :] = p_ref[x, y]
+            high_ref[at, :] = p_ref[29 + x, y]
+    for k in range(15):
+        low_ref[pl.ds(384 + 8 * k, 8), :] = coarse_ref[pl.ds(8 * k, 8), :]
+        high_ref[pl.ds(384 + 8 * k, 8), :] = coarse_ref[pl.ds(1800 + 8 * k, 8), :]
 
 
 def section(start, current, rate, number):
@@ -563,7 +644,7 @@
     new_ref, send_ref, q0, q1, push, sign, nx, ny, nz, lump, even, odd, ends, sems,
 ):
     w = WIDE
-    size_x, size_y = 32 + 2 * w, 16 + 2 * w
+    size_y = 16 + 2 * w
 
     def put(x, y, col):
         q0[x, y] = col
@@ -571,22 +652,23 @@
 
     def fill_mid(r):
         x = r + jnp.where(r >= 4, 24, 0)
+        at = r + w + jnp.where(r >= 4, 8, 0)
         for y in range(w):
-            put(x + w, y, ylo_ref[x, y])
-            put(x + w, y + 16 + w, yhi_ref[x, y])
-        for y in range(16):
-            put(x + w, y + w, adv_ref[x, y])
+            put(at, y, ylo_ref[x, y])
+            put(at, y + 16 + w, yhi_ref[x, y])
+        for y in range(16):
+            put(at, y + w, adv_ref[x, y])
 
     def fill_side(x):
         for y in range(16):
             put(x, y + w, xlo_ref[pl.ds((x * 16 + y) * 8, 8), :])
-            put(x + 32 + w, y + w, xhi_ref[pl.ds((x * 16 + y) * 8, 8), :])
+            put(x + 16 + w, y + w, xhi_ref[pl.ds((x * 16 + y) * 8, 8), :])
 
     loop(0, 8, fill_mid)
     loop(0, w, fill_side)
     k = 0
     for dx in range(1, w):
-        for x in (w - dx, w + 31 + dx):
+        for x in (w - dx, w + 15 + dx):
             for dy in range(1, w - dx + 1):
                 put(x, w - dy, clo_ref[k])
                 put(x, w + 15 + dy, chi_ref[k])
@@ -596,11 +678,11 @@
     for k in range(1, SWEEPS + 1):
 
         def end_rows(j, k=k):
-            return k + 2 * j + jnp.where(j >= 3, 32 - 2 * k, 0)
+            return k + 2 * j + jnp.where(j >= 3, 16 - 2 * k, 0)
 
         sweep_rows(src, dst, push, sign, end_rows, 6, range(k, size_y - k), even, odd)
         if k < SWEEPS:
-            for r, x in enumerate((k, k + 1, 30 - k, 31 - k)):
+            for r, x in enumerate((k, k + 1, 14 - k, 15 - k)):
                 for y in range(k, size_y - k):
                     dst[x + w, y] = rims_ref[k - 1, r, y]
         src, dst = dst, src
@@ -609,14 +691,14 @@
     def take(r):
         x = SWEEPS + r + jnp.where(r >= 4, 16, 0)
         for y in range(SWEEPS, size_y - SWEEPS):
-            last[x + w, y] = rows_ref[x, y]
+            last[SWEEPS + r + w, y] = rows_ref[x, y]
 
     loop(0, 8, take)
-    loop(0, 16, lambda r: normals(last, r + w - 1 + jnp.where(r >= 8, 18, 0), nx, ny, nz, r))
+    loop(0, 16, lambda r: normals(last, r + w - 1 + jnp.where(r >= 8, 2, 0), nx, ny, nz, r))
 
     def planes(n):
         far = jnp.where(n >= 3, 1, 0)
-        gather(last, 2 * n + w + 20 * far, nx, ny, nz, 2 * n + 1 + 2 * far, lump, n, 384, ends, n * 256)
+        gather(last, 2 * n + w + 4 * far, nx, ny, nz, 2 * n + 1 + 2 * far, lump, n, 384, ends, n * 256)
 
     loop(0, 6, planes)
     copies = [
@@ -666,36 +748,43 @@
     level_rows = level_set.reshape(32, 2, 8, 8, 128).transpose(0, 1, 3, 2, 4).reshape(4096, 128)
     flow_rows = flow_velocity.reshape(3, 16, 8, 4, 128).transpose(0, 1, 3, 2, 4).reshape(1536, 128)
 
-    send = call(pack_velocity, f32(16, 120, 128), flow_rows, name="pack", mib=8)
+    send = call(pack_velocity, f32(16, 120, 128), flow_rows, name="pack", mib=4)
     coarse = lax.all_to_all(send, "gy", split_axis=0, concat_axis=0, tiled=True)
     start, ylo, yhi = call(
-        unpack_level, (block, f32(32, 3, *col), f32(32, 3, *col)), level_rows, name="unpack", mib=8
-    )
-    xlo = jnp.concatenate([start[:3].reshape(384, 128), coarse[0]], axis=0)
-    xhi = jnp.concatenate([start[29:].reshape(384, 128), coarse[15]], axis=0)
+        unpack_level, (block, f32(32, 3, *col), f32(32, 3, *col)), level_rows, name="unpack", mib=4
+    )
+    both, tips = call(
+        depth_sides, (f32(2, 32, 16, *col), f32(2, 2, 16, *col)), start,
+        scratch=[block.shape, block.shape, (4, 16, *col), (4, 16, *col)], name="depth", mib=8, ops=512 * 90,
+    )
+    coarse = coarse.reshape(1920, 128)
+    xlo, xhi = call(join_x, (f32(504, 128), f32(504, 128)), start, coarse, tips, name="join", mib=4)
     halo = star(xlo, xhi, ylo, yhi)
-    velocity, ends = call(
-        refine_inner, (f32(3, 32, 16, *col), f32(2, 240, 128)), coarse.reshape(1920, 128), band_mask,
-        scratch=[(3840, 128), (2, *col)], name="refine", mib=24,
+    velocity, ends, acc = call(
+        refine_and_rate, (f32(3, 32, 16, *col), f32(2, 240, 128), block), coarse, band_mask, start, both,
+        scratch=[(3840, 128), (2, *col)], name="refine", mib=10, ops=512 * 110,
     )
     current = start
     for number in range(3):
-        acc = call(
-            functools.partial(inner_rate, number == 0), block, current, velocity,
-            scratch=[block.shape, block.shape, (4, 16, *col), (4, 16, *col)], name="inner", mib=24, ops=512 * 140,
-        )
         if number == 0:
             velocity, acc = call(
-                refine_ends, (f32(3, 32, 16, *col), block), halo[0], halo[1], ends, band_mask, current, velocity, acc,
+                refine_ends, (f32(3, 32, 16, *col), block),
+                halo[0], halo[1], ends, band_mask, current, tips, velocity, acc,
                 scratch=[(480, 128), (3, 2, 16, *col), (2, 16, *col), pltpu.SemaphoreType.DMA((8,))],
-                name="ends", mib=16, anywhere=(5, 6), aliases={5: 0, 6: 1},
+                name="ends", mib=4, anywhere=(6, 7), aliases={6: 0, 7: 1},
+            )
+        else:
+            acc = call(
+                inner_rate, block, current, velocity,
+                scratch=[block.shape, block.shape, (4, 16, *col), (4, 16, *col)],
+                name="inner", mib=8, ops=512 * 140,
             )
         edge = WIDE if number == 2 else 3
         x_edge, y_edge = f32(edge * 128, 128), f32(32, edge, *col)
         current, *edges = call(
             functools.partial(edge_rate, number, edge), (block, x_edge, x_edge, y_edge, y_edge),
             acc, start, current, velocity, *sum(turned_about(number, halo[:2], halo[2:]), ()),
-            scratch=[(6, 16, *col)], name="edge", mib=24, ops=512 * 30,
+            scratch=[(6, 16, *col)], name="edge", mib=4, ops=512 * 30,
         )
         halo = star(*edges)
     xlo, xhi, ylo, yhi = halo
@@ -708,7 +797,7 @@
     side = (32, 16 + 2 * WIDE, *col)
     rims, last = call(
         sweep_sides, (f32(3, 4, *side[1:]), f32(*side)), current, yhi, ylo, *levels,
-        scratch=[side] * 4 + turns, name="sides", mib=20, ops=512 * 70,
+        scratch=[side] * 4 + turns, name="sides", mib=17, ops=512 * 70,
     )
     corner_low, corner_high = call(
         pack_corners, (corner, corner), xhi, xlo, rims, name="corners", mib=4, anywhere=(2,)
@@ -718,12 +807,12 @@
         scratch=[(22, 8, *col)] * 3 + [(1280, 128)], name="outputs", mib=12, ops=512 * 40,
     )
     clo, chi = moved(corner_high, "gy", 1), moved(corner_low, "gy", -1)
-    ext = (32 + 2 * WIDE, 16 + 2 * WIDE, *col)
+    ext = (16 + 2 * WIDE, 16 + 2 * WIDE, *col)
     new_rows, packed = call(
         finish, (f32(4096, 128), f32(16, 64, 128)),
         current, xhi, xlo, yhi, ylo, clo, chi, rims, last, send_mid, new_rows,
         scratch=[ext] * 4 + [(16, 8, *col)] * 3 + [(768, 128)] + turns + [(1536, 128), pltpu.SemaphoreType.DMA((2,))],
-        name="finish", mib=30, ops=512 * 250, anywhere=(10,), aliases={10: 0},
+        name="finish", mib=18, ops=512 * 250, anywhere=(10,), aliases={10: 0},
     )
     returned = lax.all_to_all(packed, "gy", split_axis=0, concat_axis=0, tiled=True).reshape(16, 2, 4, 8, 128)
     new_level = new_rows.reshape(32, 2, 8, 8, 128).transpose(0, 1, 3, 2, 4).reshape(32, 16, 1024)

time: 159 us -> 156 us (0.981)
  waiting for transfers between devices: 21.4 us -> 13.3 us
  local copies, waits for them, and re-layouts: 4.32 us -> 7.69 us
  Pallas kernels: 80 us -> 82.9 us
  other arithmetic: 1.89 us -> 0 us
    all_to_all x1, waiting for transfers between devices: 9.73 us -> 1.03 us  [per_device(): coarse = lax.all_to_all(send, 'gy', split_axis=0, concat_axis=0, tiled=True)]
    unnamed x6 -> x10, local copies, waits for them, and re-layouts: 2.72 us -> 6.87 us
    pallas_call x15 -> x16, Pallas kernels: 80 us -> 82.9 us  [call(): pl.pallas_call(kernel, out_shape=outs, in_specs=[spec(k) for k in range(l...]
    concatenate x2 -> x0, other arithmetic: 1.89 us -> none  [the longest x1 0.95 us: per_device(): xhi = jnp.concatenate([start[29:].reshape(384, 128), coarse[15]], axis=0)]
  transfers between devices with their start and end apart: 19 -> 19, of which waited for: 6 -> 7; matrix products, arithmetic and copies ran while one was open for 2% -> 0% of each run, Pallas kernels for 37% -> 40%
where the time goes in v4:
time: 156 us; the launch traced here: 155 us
  Pallas kernels  82.9 us (53%)
  starting transfers between devices  34.5 us (22%)
  blocking collectives  16.1 us (10%)
  waiting for transfers between devices  13.3 us (9%)
  local copies, waits for them, and re-layouts  7.69 us (5%)
    pallas_call x16, Pallas kernels, call(): pl.pallas_call(kernel, out_shape=outs, in_specs=[spec(k) for k in range(l...  82.9 us
    ppermute x18, starting transfers between devices, moved(): lax.ppermute(values, axis, [(i, (i + step) % count) for i in range(count)])  26.8 us
    all_to_all x1, blocking collectives, per_device(): lax.all_to_all(packed, 'gy', split_axis=0, concat_axis=0, tiled=True)  16.1 us
    ppermute x18, waiting for transfers between devices, moved(): lax.ppermute(values, axis, [(i, (i + step) % count) for i in range(count)])  12.3 us
    all_to_all x1, starting transfers between devices, per_device(): coarse = lax.all_to_all(send, 'gy', split_axis=0, concat_axis=0, tiled=True)  7.76 us
    unnamed x10, local copies, waits for them, and re-layouts  6.87 us
  transfers between devices with their start and end apart: 19, of which 7 were waited for; matrix products, arithmetic and copies ran while one was open for 0% of the time, Pallas kernels for 40%

profile of v4, /device:TPU:1, one launch (start us, length us, event | category | flops | bytes accessed | tf_op | source)
XLA Modules:
  0.0 155.4 jit_solution(4888602522987937999)
XLA Ops:
  0.6 1.1 copy-done.3
  1.8 1.3 pack.1
  3.0 7.8 %all-to-all-start = ((f32[16,120,128]{2,1,0:T(8,128)}), f32[16,120,128]{2,1,0:T(8,128)S(1)}, u32[]{:S(2)}, u32[]{:S(2)}) async-start(f32[16,120,128]{2,1,0:T(8,128)} %pack.1), calls=%async_computation | async-start | bytes 1966080 | tf_op jit(solution)/shard_map/all_to_all | solution.py:752
  10.8 1.6 %copy-done.2 = f32[32,16,1024]{2,1,0:T(8,128)S(1)} copy-done((f32[32,16,1024]{2,1,0:T(8,128)S(1)}, f32[32,16,1024]{2,1,0:T(8,128)}, u32[]{:S(2)}) %copy-start.2) | copy-done | bytes 2097176
  12.4 1.4 unpack.1
  13.8 1.6 %collective-permute-start.2 = (f32[32,3,8,128]{3,2,1,0:T(8,128)}, f32[32,3,8,128]{3,2,1,0:T(8,128)}, u32[]{:S(2)}, u32[]{:S(2)}) collective-permute-start(f32[32,3,8,128]{3,2,1,0:T(8,128)} %get-tuple-element.52), channel_id=1, source_target_pairs={{0,1},{1,2},{2,3},{3,4},{4,5},{5,6},{6,7},{7,8},{8,9},{9,10},{10,1... | collective-permute-start | bytes 1179656 | tf_op jit(solution)/shard_map/ppermute | solution.py:738
  15.4 7.5 %depth.1 = (f32[2,32,16,8,128]{4,3,2,1,0:T(8,128)S(1)}, f32[2,2,16,8,128]{4,3,2,1,0:T(8,128)S(1)}) custom-call(f32[32,16,8,128]{3,2,1,0:T(8,128)S(1)} %get-tuple-element.42.p_ref.start_ref), custom_call_target="tpu_custom_call" | custom-call | flops 47185920 | bytes 8388608 | tf_op jit(solution)/shard_map/depth/pallas_call | solution.py:723
  22.9 2.0 %copy-done = f32[2,32,16,8,128]{4,3,2,1,0:T(8,128)} copy-done((f32[2,32,16,8,128]{4,3,2,1,0:T(8,128)}, f32[2,32,16,8,128]{4,3,2,1,0:T(8,128)S(1)}, u32[]{:S(2)}) %copy-start) | copy-done | bytes 4194328
  24.9 1.0 all-to-all-done
  25.9 1.4 collective-permute-start
  27.3 3.8 %collective-permute-start.1 = (f32[504,128]{1,0:T(8,128)S(1)}, f32[504,128]{1,0:T(8,128)S(1)}, u32[]{:S(2)}, u32[]{:S(2)}) collective-permute-start(f32[504,128]{1,0:T(8,128)S(1)} %get-tuple-element.45), channel_id=1, source_target_pairs={{0,112},{16,0},{32,16},{48,32},{64,48},{80,64},{96,80},{112,96},{1... | collective-permute-start | bytes 774152 | tf_op jit(solution)/shard_map/ppermute | solution.py:738
  31.1 2.2 %copy-done.1 = f32[2,32,16,8,128]{4,3,2,1,0:T(8,128)S(1)} copy-done((f32[2,32,16,8,128]{4,3,2,1,0:T(8,128)S(1)}, f32[2,32,16,8,128]{4,3,2,1,0:T(8,128)}, u32[]{:S(2)}) %copy-start.1) | copy-done | bytes 4194328
  33.3 9.3 %refine.1 = (f32[3,32,16,8,128]{4,3,2,1,0:T(8,128)S(1)}, f32[2,240,128]{2,1,0:T(8,128)S(1)}, f32[32,16,8,128]{3,2,1,0:T(8,128)S(1)}) custom-call(f32[1920,128]{1,0:T(8,128)S(1)} %bitcast.30, s32[2,1,64]{2,1,0:T(1,128)S(1)} %copy-done.4, f32[32,16,8,128]{3,2,1,0:T(8,128)S(1)} %get-tuple-element.42.p_ref.start_ref, f32[2,32,16,8,128]{4,3,2,1,0:T(8,128)S(1)} %copy-done.1), custom_call_target="tpu_custom_call" | custom-call | flops 57671680 | bytes 8388608 | tf_op jit(solution)/shard_map/refine/pallas_call | solution.py:723
  42.6 0.0 collective-permute-done.lo_ref.x1_ref
  42.6 0.0 collective-permute-done.1.hi_ref.x2_ref
  42.6 1.4 ends.1
  44.0 0.0 collective-permute-done.2.y1_ref
  44.1 4.2 %edge.3 = (f32[32,16,8,128]{3,2,1,0:T(8,128)S(1)}, f32[384,128]{1,0:T(8,128)S(1)}, f32[384,128]{1,0:T(8,128)S(1)}, f32[32,3,8,128]{3,2,1,0:T(8,128)S(1)}, f32[32,3,8,128]{3,2,1,0:T(8,128)S(1)}) custom-call(f32[32,16,8,128]{3,2,1,0:T(8,128)S(1)} %get-tuple-element.50.acc_ref, f32[32,16,8,128]{3,2,1,0:T(8,128)S(1)} %get-tuple-element.42.p_ref.start_ref, ...), custom_call_target="tpu_custom_call" | custom-call | flops 15728640 | bytes 8388608 | tf_op jit(solution)/shard_map/edge/pallas_call | solution.py:723
  48.2 2.0 %collective-permute-start.6 = (f32[32,3,8,128]{3,2,1,0:T(8,128)S(1)}, f32[32,3,8,128]{3,2,1,0:T(8,128)S(1)}, u32[]{:S(2)}, u32[]{:S(2)}) collective-permute-start(f32[32,3,8,128]{3,2,1,0:T(8,128)S(1)} %get-tuple-element.57), channel_id=1, source_target_pairs={{0,15},{1,0},{2,1},{3,2},{4,3},{5,4},{6,5},{7,6},{8,7},{9,8},{10,9... | collective-permute-start | bytes 1179656 | tf_op jit(solution)/shard_map/ppermute | solution.py:738
  50.2 1.3 collective-permute-start.4
  51.5 0.2 collective-permute-start.5
  51.7 10.3 %inner.2.acc_ref = f32[32,16,8,128]{3,2,1,0:T(8,128)S(1)} custom-call(f32[32,16,8,128]{3,2,1,0:T(8,128)S(1)} %get-tuple-element.54.p_ref, f32[3,32,16,8,128]{4,3,2,1,0:T(8,128)S(1)} %get-tuple-element.51.v_ref), custom_call_target="tpu_custom_call" | custom-call | flops 73400320 | bytes 8388608 | tf_op jit(solution)/shard_map/inner/pallas_call | solution.py:723
  61.9 1.2 collective-permute-done.4.x1_ref
  63.1 2.0 %collective-permute-done.5.x2_ref = f32[384,128]{1,0:T(8,128)S(1)} collective-permute-done((f32[384,128]{1,0:T(8,128)S(1)}, f32[384,128]{1,0:T(8,128)S(1)}, u32[]{:S(2)}, u32[]{:S(2)}) %collective-permute-start.5) | collective-permute-done | bytes 196640 | tf_op jit(solution)/shard_map/ppermute | solution.py:738
  65.2 0.0 collective-permute-done.6.y1_ref
  65.2 0.0 collective-permute-done.7.y2_ref
  65.2 3.3 %edge.4 = (f32[32,16,8,128]{3,2,1,0:T(8,128)S(1)}, f32[384,128]{1,0:T(8,128)S(1)}, f32[384,128]{1,0:T(8,128)S(1)}, f32[32,3,8,128]{3,2,1,0:T(8,128)S(1)}, f32[32,3,8,128]{3,2,1,0:T(8,128)S(1)}) custom-call(f32[32,16,8,128]{3,2,1,0:T(8,128)S(1)} %inner.2.acc_ref, f32[32,16,8,128]{3,2,1,0:T(8,128)S(1)} %get-tuple-element.42.p_ref.start_ref, ...), custom_call_target="tpu_custom_call" | custom-call | flops 15728640 | bytes 8388608 | tf_op jit(solution)/shard_map/edge/pallas_call | solution.py:723
  68.5 0.1 collective-permute-start.10
  68.6 0.7 collective-permute-start.11
  69.2 0.0 collective-permute-start.8
  69.2 5.1 %collective-permute-start.9 = (f32[384,128]{1,0:T(8,128)S(1)}, f32[384,128]{1,0:T(8,128)S(1)}, u32[]{:S(2)}, u32[]{:S(2)}) collective-permute-start(f32[384,128]{1,0:T(8,128)S(1)} %get-tuple-element.61), channel_id=1, source_target_pairs={{0,112},{16,0},{32,16},{48,32},{64,48},{80,64},{96,80},{112,96},{1... | collective-permute-start | bytes 589832 | tf_op jit(solution)/shard_map/ppermute | solution.py:738
  74.3 10.2 %inner.3.acc_ref = f32[32,16,8,128]{3,2,1,0:T(8,128)S(1)} custom-call(f32[32,16,8,128]{3,2,1,0:T(8,128)S(1)} %get-tuple-element.59.p_ref, f32[3,32,16,8,128]{4,3,2,1,0:T(8,128)S(1)} %get-tuple-element.51.v_ref), custom_call_target="tpu_custom_call" | custom-call | flops 73400320 | bytes 8388608 | tf_op jit(solution)/shard_map/inner/pallas_call | solution.py:723
  84.6 3.3 %edge.5 = (f32[32,16,8,128]{3,2,1,0:T(8,128)S(1)}, f32[768,128]{1,0:T(8,128)S(1)}, f32[768,128]{1,0:T(8,128)S(1)}, f32[32,6,8,128]{3,2,1,0:T(8,128)S(1)}, f32[32,6,8,128]{3,2,1,0:T(8,128)S(1)}) custom-call(f32[32,16,8,128]{3,2,1,0:T(8,128)S(1)} %inner.3.acc_ref, f32[32,16,8,128]{3,2,1,0:T(8,128)S(1)} %get-tuple-element.42.p_ref.start_ref, ...), custom_call_target="tpu_custom_call" | custom-call | flops 15728640 | bytes 8388608 | tf_op jit(solution)/shard_map/edge/pallas_call | solution.py:723
  87.9 4.4 %collective-permute-start.14 = (f32[32,6,8,128]{3,2,1,0:T(8,128)S(1)}, f32[32,6,8,128]{3,2,1,0:T(8,128)S(1)}, u32[]{:S(2)}, u32[]{:S(2)}) collective-permute-start(f32[32,6,8,128]{3,2,1,0:T(8,128)S(1)} %get-tuple-element.67), channel_id=1, source_target_pairs={{0,15},{1,0},{2,1},{3,2},{4,3},{5,4},{6,5},{7,6},{8,7},{9,8},{10,9... | collective-permute-start | bytes 2359304 | tf_op jit(solution)/shard_map/ppermute | solution.py:738
  92.3 1.6 %collective-permute-start.12 = (f32[768,128]{1,0:T(8,128)S(1)}, f32[768,128]{1,0:T(8,128)S(1)}, u32[]{:S(2)}, u32[]{:S(2)}) collective-permute-start(f32[768,128]{1,0:T(8,128)S(1)} %get-tuple-element.65), channel_id=1, source_target_pairs={{0,112},{16,0},{32,16},{48,32},{64,48},{80,64},{96,80},{112,96},{1... | collective-permute-start | bytes 1179656 | tf_op jit(solution)/shard_map/ppermute | solution.py:738
  93.9 0.0 collective-permute-start.13
  93.9 7.5 %core.1 = (f32[32,16,8,128]{3,2,1,0:T(8,128)S(1)}, f32[32,16,8,128]{3,2,1,0:T(8,128)S(1)}, f32[32,16,8,128]{3,2,1,0:T(8,128)S(1)}, f32[32,16,8,128]{3,2,1,0:T(8,128)S(1)}) custom-call(f32[32,16,8,128]{3,2,1,0:T(8,128)S(1)} %get-tuple-element.64.adv_ref), custom_call_target="tpu_custom_call" | custom-call | flops 47185920 | bytes 8388608 | tf_op jit(solution)/shard_map/core/pallas_call | solution.py:723
  101.4 6.2 %collective-permute-done.14.yhi_ref = f32[32,6,8,128]{3,2,1,0:T(8,128)S(1)} collective-permute-done((f32[32,6,8,128]{3,2,1,0:T(8,128)S(1)}, f32[32,6,8,128]{3,2,1,0:T(8,128)S(1)}, u32[]{:S(2)}, u32[]{:S(2)}) %collective-permute-start.14) | collective-permute-done | bytes 786464 | tf_op jit(solution)/shard_map/ppermute | solution.py:738
  107.6 1.4 collective-permute-done.15.ylo_ref
  108.9 8.3 %sides.1 = (f32[3,4,28,8,128]{4,3,2,1,0:T(8,128)S(1)}, f32[32,28,8,128]{3,2,1,0:T(8,128)S(1)}) custom-call(f32[32,16,8,128]{3,2,1,0:T(8,128)S(1)} %get-tuple-element.64.adv_ref, f32[32,6,8,128]{3,2,1,0:T(8,128)S(1)} %collective-permute-done.14.yhi_ref, f32[32,6,8,128]{3,2,1,0:T(8,128)S(1)} %collective-permute-done.15.ylo_ref, ...), custom_call_target="tpu_custom_call" | custom-call | flops 36700160 | bytes 8388608 | tf_op jit(solution)/shard_map/sides/pallas_call | solution.py:723
  117.2 0.1 collective-permute-done.12.xhi_ref
  117.3 1.3 collective-permute-done.13.xlo_ref
  118.7 1.1 collective-permute-start.16
  119.8 3.6 %collective-permute-start.17 = (f32[30,8,128]{2,1,0:T(8,128)S(1)}, f32[30,8,128]{2,1,0:T(8,128)S(1)}, u32[]{:S(2)}, u32[]{:S(2)}) collective-permute-start(f32[30,8,128]{2,1,0:T(8,128)S(1)} %get-tuple-element.75), channel_id=1, source_target_pairs={{0,15},{1,0},{2,1},{3,2},{4,3},{5,4},{6,5},{7,6},{8,7},{9,8},{10,9... | collective-permute-start | bytes 368648 | tf_op jit(solution)/shard_map/ppermute | solution.py:738
  123.4 5.7 %outputs.1 = (f32[4096,128]{1,0:T(8,128)}, f32[10,64,128]{2,1,0:T(8,128)S(1)}) custom-call(f32[32,28,8,128]{3,2,1,0:T(8,128)S(1)} %get-tuple-element.76.last.rows_ref), custom_call_target="tpu_custom_call" | custom-call | flops 20971520 | bytes 8388608 | tf_op jit(solution)/shard_map/outputs/pallas_call | solution.py:723
  129.1 9.4 %finish.1 = (f32[4096,128]{1,0:T(8,128)}, f32[16,64,128]{2,1,0:T(8,128)S(1)}) custom-call(f32[32,16,8,128]{3,2,1,0:T(8,128)S(1)} %get-tuple-element.64.adv_ref, f32[768,128]{1,0:T(8,128)S(1)} %collective-permute-done.12.xhi_ref, f32[768,128]{1,0:T(8,128)S(1)} %collective-permute-done.13.xlo_ref, ...), custom_call_target="tpu_custom_call", output_to_operand_aliasing={{0}: (10, {})} | custom-call | flops 131072000 | bytes 8388608 | tf_op jit(solution)/shard_map/finish/pallas_call | solution.py:723
  138.5 16.1 %all_to_all.10 = f32[16,64,128]{2,1,0:T(8,128)S(1)} all-to-all(f32[16,64,128]{2,1,0:T(8,128)S(1)} %get-tuple-element.80), channel_id=1, replica_groups=mesh['gx'=8,'gy'=16] {'gy'}, dimensions={0} | all-to-all | bytes 1048576 | tf_op jit(solution)/shard_map/all_to_all | solution.py:817
  154.6 0.8 slice_bitcast_fusion
  (18 shorter events, 0.1 us)
Async XLA Ops:
  0.6 1.1 copy-start.3
  3.0 22.8 %all-to-all-start = ((f32[16,120,128]{2,1,0:T(8,128)}), f32[16,120,128]{2,1,0:T(8,128)S(1)}, u32[]{:S(2)}, u32[]{:S(2)}) async-start(f32[16,120,128]{2,1,0:T(8,128)} %pack.1), calls=%async_computation | async-start | bytes 1966080 | tf_op jit(solution)/shard_map/all_to_all | solution.py:752
  10.8 1.6 %copy-start.2 = (f32[32,16,1024]{2,1,0:T(8,128)S(1)}, f32[32,16,1024]{2,1,0:T(8,128)}, u32[]{:S(2)}) copy-start(f32[32,16,1024]{2,1,0:T(8,128)} %param.3) | copy-start | bytes 6291460
  13.8 30.3 %collective-permute-start.2 = (f32[32,3,8,128]{3,2,1,0:T(8,128)}, f32[32,3,8,128]{3,2,1,0:T(8,128)}, u32[]{:S(2)}, u32[]{:S(2)}) collective-permute-start(f32[32,3,8,128]{3,2,1,0:T(8,128)} %get-tuple-element.52), channel_id=1, source_target_pairs={{0,1},{1,2},{2,3},{3,4},{4,5},{5,6},{6,7},{7,8},{8,9},{9,10},{10,1... | collective-permute-start | bytes 1179656 | tf_op jit(solution)/shard_map/ppermute | solution.py:738
  15.4 28.7 %collective-permute-start.3 = (f32[32,3,8,128]{3,2,1,0:T(8,128)}, f32[32,3,8,128]{3,2,1,0:T(8,128)}, u32[]{:S(2)}, u32[]{:S(2)}) collective-permute-start(f32[32,3,8,128]{3,2,1,0:T(8,128)} %get-tuple-element.53), channel_id=1, source_target_pairs={{0,15},{1,0},{2,1},{3,2},{4,3},{5,4},{6,5},{7,6},{8,7},{9,8},{10,9... | collective-permute-start | bytes 1179656 | tf_op jit(solution)/shard_map/ppermute | solution.py:738
  22.9 2.0 %copy-start = (f32[2,32,16,8,128]{4,3,2,1,0:T(8,128)}, f32[2,32,16,8,128]{4,3,2,1,0:T(8,128)S(1)}, u32[]{:S(2)}) copy-start(f32[2,32,16,8,128]{4,3,2,1,0:T(8,128)S(1)} %get-tuple-element.46.both_ref) | copy-start | bytes 12582916
  24.9 6.2 %copy-start.4 = (s32[2,1,64]{2,1,0:T(1,128)S(1)}, s32[2,1,64]{2,1,0:T(1,128)}, u32[]{:S(2)}) copy-start(s32[2,1,64]{2,1,0:T(1,128)} %band_ref.3) | copy-start | bytes 1540
  25.9 16.7 %collective-permute-start = (f32[504,128]{1,0:T(8,128)S(1)}, f32[504,128]{1,0:T(8,128)S(1)}, u32[]{:S(2)}, u32[]{:S(2)}) collective-permute-start(f32[504,128]{1,0:T(8,128)S(1)} %get-tuple-element.44), channel_id=1, source_target_pairs={{0,16},{16,32},{32,48},{48,64},{64,80},{80,96},{96,112},{112,0},{1... | collective-permute-start | bytes 774152 | tf_op jit(solution)/shard_map/ppermute | solution.py:738
  27.3 15.3 %collective-permute-start.1 = (f32[504,128]{1,0:T(8,128)S(1)}, f32[504,128]{1,0:T(8,128)S(1)}, u32[]{:S(2)}, u32[]{:S(2)}) collective-permute-start(f32[504,128]{1,0:T(8,128)S(1)} %get-tuple-element.45), channel_id=1, source_target_pairs={{0,112},{16,0},{32,16},{48,32},{64,48},{80,64},{96,80},{112,96},{1... | collective-permute-start | bytes 774152 | tf_op jit(solution)/shard_map/ppermute | solution.py:738
  31.1 2.2 %copy-start.1 = (f32[2,32,16,8,128]{4,3,2,1,0:T(8,128)S(1)}, f32[2,32,16,8,128]{4,3,2,1,0:T(8,128)}, u32[]{:S(2)}) copy-start(f32[2,32,16,8,128]{4,3,2,1,0:T(8,128)} %copy-done) | copy-start | bytes 12582916
  48.2 17.0 %collective-permute-start.6 = (f32[32,3,8,128]{3,2,1,0:T(8,128)S(1)}, f32[32,3,8,128]{3,2,1,0:T(8,128)S(1)}, u32[]{:S(2)}, u32[]{:S(2)}) collective-permute-start(f32[32,3,8,128]{3,2,1,0:T(8,128)S(1)} %get-tuple-element.57), channel_id=1, source_target_pairs={{0,15},{1,0},{2,1},{3,2},{4,3},{5,4},{6,5},{7,6},{8,7},{9,8},{10,9... | collective-permute-start | bytes 1179656 | tf_op jit(solution)/shard_map/ppermute | solution.py:738
  50.2 15.0 %collective-permute-start.7 = (f32[32,3,8,128]{3,2,1,0:T(8,128)S(1)}, f32[32,3,8,128]{3,2,1,0:T(8,128)S(1)}, u32[]{:S(2)}, u32[]{:S(2)}) collective-permute-start(f32[32,3,8,128]{3,2,1,0:T(8,128)S(1)} %get-tuple-element.58), channel_id=1, source_target_pairs={{0,1},{1,2},{2,3},{3,4},{4,5},{5,6},{6,7},{7,8},{8,9},{9,10},{10,1... | collective-permute-start | bytes 1179656 | tf_op jit(solution)/shard_map/ppermute | solution.py:738
  50.2 12.9 %collective-permute-start.4 = (f32[384,128]{1,0:T(8,128)S(1)}, f32[384,128]{1,0:T(8,128)S(1)}, u32[]{:S(2)}, u32[]{:S(2)}) collective-permute-start(f32[384,128]{1,0:T(8,128)S(1)} %get-tuple-element.55), channel_id=1, source_target_pairs={{0,112},{16,0},{32,16},{48,32},{64,48},{80,64},{96,80},{112,96},{1... | collective-permute-start | bytes 589832 | tf_op jit(solution)/shard_map/ppermute | solution.py:738
  51.5 13.7 %collective-permute-start.5 = (f32[384,128]{1,0:T(8,128)S(1)}, f32[384,128]{1,0:T(8,128)S(1)}, u32[]{:S(2)}, u32[]{:S(2)}) collective-permute-start(f32[384,128]{1,0:T(8,128)S(1)} %get-tuple-element.56), channel_id=1, source_target_pairs={{0,16},{16,32},{32,48},{48,64},{64,80},{80,96},{96,112},{112,0},{1... | collective-permute-start | bytes 589832 | tf_op jit(solution)/shard_map/ppermute | solution.py:738
  68.5 16.0 %collective-permute-start.10 = (f32[32,3,8,128]{3,2,1,0:T(8,128)S(1)}, f32[32,3,8,128]{3,2,1,0:T(8,128)S(1)}, u32[]{:S(2)}, u32[]{:S(2)}) collective-permute-start(f32[32,3,8,128]{3,2,1,0:T(8,128)S(1)} %get-tuple-element.62), channel_id=1, source_target_pairs={{0,1},{1,2},{2,3},{3,4},{4,5},{5,6},{6,7},{7,8},{8,9},{9,10},{10,1... | collective-permute-start | bytes 1179656 | tf_op jit(solution)/shard_map/ppermute | solution.py:738
  68.6 16.0 %collective-permute-start.11 = (f32[32,3,8,128]{3,2,1,0:T(8,128)S(1)}, f32[32,3,8,128]{3,2,1,0:T(8,128)S(1)}, u32[]{:S(2)}, u32[]{:S(2)}) collective-permute-start(f32[32,3,8,128]{3,2,1,0:T(8,128)S(1)} %get-tuple-element.63), channel_id=1, source_target_pairs={{0,15},{1,0},{2,1},{3,2},{4,3},{5,4},{6,5},{7,6},{8,7},{9,8},{10,9... | collective-permute-start | bytes 1179656 | tf_op jit(solution)/shard_map/ppermute | solution.py:738
  69.2 15.3 %collective-permute-start.8 = (f32[384,128]{1,0:T(8,128)S(1)}, f32[384,128]{1,0:T(8,128)S(1)}, u32[]{:S(2)}, u32[]{:S(2)}) collective-permute-start(f32[384,128]{1,0:T(8,128)S(1)} %get-tuple-element.60), channel_id=1, source_target_pairs={{0,16},{16,32},{32,48},{48,64},{64,80},{80,96},{96,112},{112,0},{1... | collective-permute-start | bytes 589832 | tf_op jit(solution)/shard_map/ppermute | solution.py:738
  69.2 15.3 %collective-permute-start.9 = (f32[384,128]{1,0:T(8,128)S(1)}, f32[384,128]{1,0:T(8,128)S(1)}, u32[]{:S(2)}, u32[]{:S(2)}) collective-permute-start(f32[384,128]{1,0:T(8,128)S(1)} %get-tuple-element.61), channel_id=1, source_target_pairs={{0,112},{16,0},{32,16},{48,32},{64,48},{80,64},{96,80},{112,96},{1... | collective-permute-start | bytes 589832 | tf_op jit(solution)/shard_map/ppermute | solution.py:738
  87.9 19.6 %collective-permute-start.14 = (f32[32,6,8,128]{3,2,1,0:T(8,128)S(1)}, f32[32,6,8,128]{3,2,1,0:T(8,128)S(1)}, u32[]{:S(2)}, u32[]{:S(2)}) collective-permute-start(f32[32,6,8,128]{3,2,1,0:T(8,128)S(1)} %get-tuple-element.67), channel_id=1, source_target_pairs={{0,15},{1,0},{2,1},{3,2},{4,3},{5,4},{6,5},{7,6},{8,7},{9,8},{10,9... | collective-permute-start | bytes 2359304 | tf_op jit(solution)/shard_map/ppermute | solution.py:738
  92.3 16.6 %collective-permute-start.15 = (f32[32,6,8,128]{3,2,1,0:T(8,128)S(1)}, f32[32,6,8,128]{3,2,1,0:T(8,128)S(1)}, u32[]{:S(2)}, u32[]{:S(2)}) collective-permute-start(f32[32,6,8,128]{3,2,1,0:T(8,128)S(1)} %get-tuple-element.68), channel_id=1, source_target_pairs={{0,1},{1,2},{2,3},{3,4},{4,5},{5,6},{6,7},{7,8},{8,9},{9,10},{10,1... | collective-permute-start | bytes 2359304 | tf_op jit(solution)/shard_map/ppermute | solution.py:738
  92.3 25.0 %collective-permute-start.12 = (f32[768,128]{1,0:T(8,128)S(1)}, f32[768,128]{1,0:T(8,128)S(1)}, u32[]{:S(2)}, u32[]{:S(2)}) collective-permute-start(f32[768,128]{1,0:T(8,128)S(1)} %get-tuple-element.65), channel_id=1, source_target_pairs={{0,112},{16,0},{32,16},{48,32},{64,48},{80,64},{96,80},{112,96},{1... | collective-permute-start | bytes 1179656 | tf_op jit(solution)/shard_map/ppermute | solution.py:738
  93.9 24.8 %collective-permute-start.13 = (f32[768,128]{1,0:T(8,128)S(1)}, f32[768,128]{1,0:T(8,128)S(1)}, u32[]{:S(2)}, u32[]{:S(2)}) collective-permute-start(f32[768,128]{1,0:T(8,128)S(1)} %get-tuple-element.66), channel_id=1, source_target_pairs={{0,16},{16,32},{32,48},{48,64},{64,80},{80,96},{96,112},{112,0},{1... | collective-permute-start | bytes 1179656 | tf_op jit(solution)/shard_map/ppermute | solution.py:738
  118.7 10.4 %collective-permute-start.16 = (f32[30,8,128]{2,1,0:T(8,128)S(1)}, f32[30,8,128]{2,1,0:T(8,128)S(1)}, u32[]{:S(2)}, u32[]{:S(2)}) collective-permute-start(f32[30,8,128]{2,1,0:T(8,128)S(1)} %get-tuple-element.74), channel_id=1, source_target_pairs={{0,1},{1,2},{2,3},{3,4},{4,5},{5,6},{6,7},{7,8},{8,9},{9,10},{10,1... | collective-permute-start | bytes 368648 | tf_op jit(solution)/shard_map/ppermute | solution.py:738
  119.8 9.3 %collective-permute-start.17 = (f32[30,8,128]{2,1,0:T(8,128)S(1)}, f32[30,8,128]{2,1,0:T(8,128)S(1)}, u32[]{:S(2)}, u32[]{:S(2)}) collective-permute-start(f32[30,8,128]{2,1,0:T(8,128)S(1)} %get-tuple-element.75), channel_id=1, source_target_pairs={{0,15},{1,0},{2,1},{3,2},{4,3},{5,4},{6,5},{7,6},{8,7},{9,8},{10,9... | collective-permute-start | bytes 368648 | tf_op jit(solution)/shard_map/ppermute | solution.py:738

commit v5 on v4

--- a/solution.py
+++ b/solution.py
@@ -131,6 +131,15 @@
         g3 - g2,
     )
     return upwind_part(speed, slope - (p1 - m1), corr)
+
+
+def loop_pairs(low, high, body):
+    def step(i, carry):
+        body(low + 2 * i)
+        body(low + 2 * i + 1)
+        return carry
+
+    lax.fori_loop(0, (high - low) // 2, step, 0)
 
 
 def loop(low, high, body):
@@ -379,7 +388,7 @@
             acc_ref[x, y] = total
 
     loop(0, 16, x_line)
-    loop(1, 31, y_line)
+    loop_pairs(1, 31, y_line)
 
 
 def refine_and_rate(mid_ref, band_ref, p_ref, both_ref, v_ref, ends_ref, acc_ref, fine, band):
@@ -426,7 +435,7 @@
             side[k, y] = low.part(k, v_ref[0, k, y])
             side[k + 3, y] = high.part(29 + k, v_ref[0, 29 + k, y])
 
-    loop(0, 16, x_line)
+    loop_pairs(0, 16, x_line)
 
     def y_line(x, side_x, outs):
         low = March(lambda y: ylo_ref[x, y + 3] if y < 0 else p_ref[x, y])
@@ -454,7 +463,7 @@
     if edge > 3:
         loop(3, edge, lambda x: y_line(x, None, (nxlo_ref, x)))
         loop(32 - edge, 29, lambda x: y_line(x, None, (nxhi_ref, x - (32 - edge))))
-    loop(edge, 32 - edge, lambda x: y_line(x, None, None))
+    loop_pairs(edge, 32 - edge, lambda x: y_line(x, None, None))
 
 
 def pushes(col):
@@ -508,7 +517,7 @@
         for y in range(16):
             push[x, y], sign[x, y] = pushes(adv_ref[x, y])
 
-    loop(0, 32, prepare)
+    loop_pairs(0, 32, prepare)
     src = adv_ref
     for k in range(1, SWEEPS + 1):
         dst = levels[k - 1]
@@ -604,7 +613,7 @@
         for y in (0, 1, 2, 3, 12, 13, 14, 15):
             put(x, y + w, adv_ref[x, y])
 
-    loop(0, 32, fill)
+    loop_pairs(0, 32, fill)
     src, dst = q0, q1
     for k, core_ref in enumerate((one_ref, two_ref, three_ref, four_ref), 1):
         dst = last_ref if k == SWEEPS else dst
@@ -616,7 +625,7 @@
             for y in inside:
                 dst[x, y + w] = core_ref[x, y]
 
-        loop(k, 32 - k, take)
+        loop_pairs(k, 32 - k, take)
         if k < SWEEPS:
             for r, x in enumerate((k, k + 1, 30 - k, 31 - k)):
                 for y in range(k, size_y - k):
@@ -626,12 +635,12 @@
 
 
 def inner_outputs(last, new_ref, send_ref, nx, ny, nz, lump):
-    loop(0, 22, lambda r: normals(last, r + 5, nx, ny, nz, r))
+    loop_pairs(0, 22, lambda r: normals(last, r + 5, nx, ny, nz, r))
 
     def planes(n):
         gather(last, 2 * n + 6, nx, ny, nz, 2 * n + 1, lump, n, 640, new_ref, (2 * n + 6) * 128)
 
-    loop(0, 10, planes)
+    loop_pairs(0, 10, planes)
     for x in (4, 5, 26, 27):
         for y in range(16):
             new_ref[pl.ds(x * 128 + (y // 8) * 64 + y % 8, 8, stride=8), :] = last[x, y + WIDE]
@@ -664,8 +673,8 @@
             put(x, y + w, xlo_ref[pl.ds((x * 16 + y) * 8, 8), :])
             put(x + 16 + w, y + w, xhi_ref[pl.ds((x * 16 + y) * 8, 8), :])
 
-    loop(0, 8, fill_mid)
-    loop(0, w, fill_side)
+    loop_pairs(0, 8, fill_mid)
+    loop_pairs(0, w, fill_side)
     k = 0
     for dx in range(1, w):
         for x in (w - dx, w + 15 + dx):
@@ -694,13 +703,13 @@
             last[SWEEPS + r + w, y] = rows_ref[x, y]
 
     loop(0, 8, take)
-    loop(0, 16, lambda r: normals(last, r + w - 1 + jnp.where(r >= 8, 2, 0), nx, ny, nz, r))
+    loop_pairs(0, 16, lambda r: normals(last, r + w - 1 + jnp.where(r >= 8, 2, 0), nx, ny, nz, r))
 
     def planes(n):
         far = jnp.where(n >= 3, 1, 0)
         gather(last, 2 * n + w + 4 * far, nx, ny, nz, 2 * n + 1 + 2 * far, lump, n, 384, ends, n * 256)
 
-    loop(0, 6, planes)
+    loop_pairs(0, 6, planes)
     copies = [
         pltpu.make_async_copy(ends.at[pl.ds(1024 * k, 512)], new_ref.at[pl.ds(3584 * k, 512)], sems.at[k])
         for k in range(2)
@@ -748,21 +757,21 @@
     level_rows = level_set.reshape(32, 2, 8, 8, 128).transpose(0, 1, 3, 2, 4).reshape(4096, 128)
     flow_rows = flow_velocity.reshape(3, 16, 8, 4, 128).transpose(0, 1, 3, 2, 4).reshape(1536, 128)
 
-    send = call(pack_velocity, f32(16, 120, 128), flow_rows, name="pack", mib=4)
+    send = call(pack_velocity, f32(16, 120, 128), flow_rows, name="pack", mib=8)
     coarse = lax.all_to_all(send, "gy", split_axis=0, concat_axis=0, tiled=True)
     start, ylo, yhi = call(
-        unpack_level, (block, f32(32, 3, *col), f32(32, 3, *col)), level_rows, name="unpack", mib=4
+        unpack_level, (block, f32(32, 3, *col), f32(32, 3, *col)), level_rows, name="unpack", mib=8
     )
     both, tips = call(
         depth_sides, (f32(2, 32, 16, *col), f32(2, 2, 16, *col)), start,
-        scratch=[block.shape, block.shape, (4, 16, *col), (4, 16, *col)], name="depth", mib=8, ops=512 * 90,
+        scratch=[block.shape, block.shape, (4, 16, *col), (4, 16, *col)], name="depth", mib=14, ops=512 * 90,
     )
     coarse = coarse.reshape(1920, 128)
     xlo, xhi = call(join_x, (f32(504, 128), f32(504, 128)), start, coarse, tips, name="join", mib=4)
     halo = star(xlo, xhi, ylo, yhi)
     velocity, ends, acc = call(
         refine_and_rate, (f32(3, 32, 16, *col), f32(2, 240, 128), block), coarse, band_mask, start, both,
-        scratch=[(3840, 128), (2, *col)], name="refine", mib=10, ops=512 * 110,
+        scratch=[(3840, 128), (2, *col)], name="refine", mib=20, ops=512 * 110,
     )
     current = start
     for number in range(3):
@@ -771,40 +780,40 @@
                 refine_ends, (f32(3, 32, 16, *col), block),
                 halo[0], halo[1], ends, band_mask, current, tips, velocity, acc,
                 scratch=[(480, 128), (3, 2, 16, *col), (2, 16, *col), pltpu.SemaphoreType.DMA((8,))],
-                name="ends", mib=4, anywhere=(6, 7), aliases={6: 0, 7: 1},
+                name="ends", mib=8, anywhere=(6, 7), aliases={6: 0, 7: 1},
             )
         else:
             acc = call(
                 inner_rate, block, current, velocity,
                 scratch=[block.shape, block.shape, (4, 16, *col), (4, 16, *col)],
-                name="inner", mib=8, ops=512 * 140,
+                name="inner", mib=12, ops=512 * 140,
             )
         edge = WIDE if number == 2 else 3
         x_edge, y_edge = f32(edge * 128, 128), f32(32, edge, *col)
         current, *edges = call(
             functools.partial(edge_rate, number, edge), (block, x_edge, x_edge, y_edge, y_edge),
             acc, start, current, velocity, *sum(turned_about(number, halo[:2], halo[2:]), ()),
-            scratch=[(6, 16, *col)], name="edge", mib=4, ops=512 * 30,
+            scratch=[(6, 16, *col)], name="edge", mib=12, ops=512 * 30,
         )
         halo = star(*edges)
     xlo, xhi, ylo, yhi = halo
     levels = call(
         sweep_core, (block,) * SWEEPS, current,
-        scratch=[block.shape, block.shape, (2, 16, *col), (2, 16, *col)], name="core", mib=8, ops=512 * 90,
+        scratch=[block.shape, block.shape, (2, 16, *col), (2, 16, *col)], name="core", mib=16, ops=512 * 90,
     )
     corner = f32(CORNERS, *col)
     turns = [(2, 16 + 2 * WIDE, *col)] * 2
     side = (32, 16 + 2 * WIDE, *col)
     rims, last = call(
         sweep_sides, (f32(3, 4, *side[1:]), f32(*side)), current, yhi, ylo, *levels,
-        scratch=[side] * 4 + turns, name="sides", mib=17, ops=512 * 70,
+        scratch=[side] * 4 + turns, name="sides", mib=24, ops=512 * 70,
     )
     corner_low, corner_high = call(
         pack_corners, (corner, corner), xhi, xlo, rims, name="corners", mib=4, anywhere=(2,)
     )
     new_rows, send_mid = call(
         inner_outputs, (f32(4096, 128), f32(10, 64, 128)), last,
-        scratch=[(22, 8, *col)] * 3 + [(1280, 128)], name="outputs", mib=12, ops=512 * 40,
+        scratch=[(22, 8, *col)] * 3 + [(1280, 128)], name="outputs", mib=14, ops=512 * 40,
     )
     clo, chi = moved(corner_high, "gy", 1), moved(corner_low, "gy", -1)
     ext = (16 + 2 * WIDE, 16 + 2 * WIDE, *col)
@@ -812,7 +821,7 @@
         finish, (f32(4096, 128), f32(16, 64, 128)),
         current, xhi, xlo, yhi, ylo, clo, chi, rims, last, send_mid, new_rows,
         scratch=[ext] * 4 + [(16, 8, *col)] * 3 + [(768, 128)] + turns + [(1536, 128), pltpu.SemaphoreType.DMA((2,))],
-        name="finish", mib=18, ops=512 * 250, anywhere=(10,), aliases={10: 0},
+        name="finish", mib=26, ops=512 * 250, anywhere=(10,), aliases={10: 0},
     )
     returned = lax.all_to_all(packed, "gy", split_axis=0, concat_axis=0, tiled=True).reshape(16, 2, 4, 8, 128)
     new_level = new_rows.reshape(32, 2, 8, 8, 128).transpose(0, 1, 3, 2, 4).reshape(32, 16, 1024)

time: 156 us -> 153 us (0.981)
  Pallas kernels: 82.9 us -> 79.3 us
    pallas_call x16, Pallas kernels: 82.9 us -> 79.3 us  [call(): pl.pallas_call(kernel, out_shape=outs, in_specs=[spec(k) for k in range(l...]
  transfers between devices with their start and end apart: 19 -> 19, of which waited for: 7 -> 7; matrix products, arithmetic and copies ran while one was open for 0% -> 0% of each run, Pallas kernels for 40% -> 39%
where the time goes in v5:
time: 153 us; the launch traced here: 152 us
  Pallas kernels  79.3 us (52%)
  starting transfers between devices  34 us (22%)
  blocking collectives  16.7 us (11%)
  waiting for transfers between devices  13.8 us (9%)
  local copies, waits for them, and re-layouts  7.69 us (5%)
    pallas_call x16, Pallas kernels, call(): pl.pallas_call(kernel, out_shape=outs, in_specs=[spec(k) for k in range(l...  79.3 us
    ppermute x18, starting transfers between devices, moved(): lax.ppermute(values, axis, [(i, (i + step) % count) for i in range(count)])  26.2 us
    all_to_all x1, blocking collectives, per_device(): lax.all_to_all(packed, 'gy', split_axis=0, concat_axis=0, tiled=True)  16.7 us
    ppermute x18, waiting for transfers between devices, moved(): lax.ppermute(values, axis, [(i, (i + step) % count) for i in range(count)])  12.8 us
    all_to_all x1, starting transfers between devices, per_device(): coarse = lax.all_to_all(send, 'gy', split_axis=0, concat_axis=0, tiled=True)  7.76 us
    unnamed x10, local copies, waits for them, and re-layouts  6.87 us
  transfers between devices with their start and end apart: 19, of which 7 were waited for; matrix products, arithmetic and copies ran while one was open for 0% of the time, Pallas kernels for 39%

profile of v5, /device:TPU:1, one launch (start us, length us, event | category | flops | bytes accessed | tf_op | source)
XLA Modules:
  0.0 152.3 jit_solution(3440142476869013816)
XLA Ops:
  0.6 1.1 copy-done.3
  1.8 1.3 pack.1
  3.0 7.8 %all-to-all-start = ((f32[16,120,128]{2,1,0:T(8,128)}), f32[16,120,128]{2,1,0:T(8,128)S(1)}, u32[]{:S(2)}, u32[]{:S(2)}) async-start(f32[16,120,128]{2,1,0:T(8,128)} %pack.1), calls=%async_computation | async-start | bytes 1966080 | tf_op jit(solution)/shard_map/all_to_all | solution.py:761
  10.8 1.6 %copy-done.2 = f32[32,16,1024]{2,1,0:T(8,128)S(1)} copy-done((f32[32,16,1024]{2,1,0:T(8,128)S(1)}, f32[32,16,1024]{2,1,0:T(8,128)}, u32[]{:S(2)}) %copy-start.2) | copy-done | bytes 2097176
  12.4 1.4 unpack.1
  13.8 1.6 %collective-permute-start.2 = (f32[32,3,8,128]{3,2,1,0:T(8,128)}, f32[32,3,8,128]{3,2,1,0:T(8,128)}, u32[]{:S(2)}, u32[]{:S(2)}) collective-permute-start(f32[32,3,8,128]{3,2,1,0:T(8,128)} %get-tuple-element.52), channel_id=1, source_target_pairs={{0,1},{1,2},{2,3},{3,4},{4,5},{5,6},{6,7},{7,8},{8,9},{9,10},{10,1... | collective-permute-start | bytes 1179656 | tf_op jit(solution)/shard_map/ppermute | solution.py:747
  15.4 0.0 collective-permute-start.3
  15.4 7.5 %depth.1 = (f32[2,32,16,8,128]{4,3,2,1,0:T(8,128)S(1)}, f32[2,2,16,8,128]{4,3,2,1,0:T(8,128)S(1)}) custom-call(f32[32,16,8,128]{3,2,1,0:T(8,128)S(1)} %get-tuple-element.42.p_ref.start_ref), custom_call_target="tpu_custom_call" | custom-call | flops 47185920 | bytes 8388608 | tf_op jit(solution)/shard_map/depth/pallas_call | solution.py:732
  22.9 2.0 %copy-done = f32[2,32,16,8,128]{4,3,2,1,0:T(8,128)} copy-done((f32[2,32,16,8,128]{4,3,2,1,0:T(8,128)}, f32[2,32,16,8,128]{4,3,2,1,0:T(8,128)S(1)}, u32[]{:S(2)}) %copy-start) | copy-done | bytes 4194328
  24.9 1.0 all-to-all-done
  25.9 1.4 collective-permute-start
  27.3 3.8 %collective-permute-start.1 = (f32[504,128]{1,0:T(8,128)S(1)}, f32[504,128]{1,0:T(8,128)S(1)}, u32[]{:S(2)}, u32[]{:S(2)}) collective-permute-start(f32[504,128]{1,0:T(8,128)S(1)} %get-tuple-element.45), channel_id=1, source_target_pairs={{0,112},{16,0},{32,16},{48,32},{64,48},{80,64},{96,80},{112,96},{1... | collective-permute-start | bytes 774152 | tf_op jit(solution)/shard_map/ppermute | solution.py:747
  31.1 2.2 %copy-done.1 = f32[2,32,16,8,128]{4,3,2,1,0:T(8,128)S(1)} copy-done((f32[2,32,16,8,128]{4,3,2,1,0:T(8,128)S(1)}, f32[2,32,16,8,128]{4,3,2,1,0:T(8,128)}, u32[]{:S(2)}) %copy-start.1) | copy-done | bytes 4194328
  33.3 9.0 %refine.1 = (f32[3,32,16,8,128]{4,3,2,1,0:T(8,128)S(1)}, f32[2,240,128]{2,1,0:T(8,128)S(1)}, f32[32,16,8,128]{3,2,1,0:T(8,128)S(1)}) custom-call(f32[1920,128]{1,0:T(8,128)S(1)} %bitcast.30, s32[2,1,64]{2,1,0:T(1,128)S(1)} %copy-done.4, f32[32,16,8,128]{3,2,1,0:T(8,128)S(1)} %get-tuple-element.42.p_ref.start_ref, f32[2,32,16,8,128]{4,3,2,1,0:T(8,128)S(1)} %copy-done.1), custom_call_target="tpu_custom_call" | custom-call | flops 57671680 | bytes 8388608 | tf_op jit(solution)/shard_map/refine/pallas_call | solution.py:732
  42.3 0.0 collective-permute-done.lo_ref.x1_ref
  42.3 1.4 ends.1
  43.8 0.0 collective-permute-done.2.y1_ref
  43.8 3.8 %edge.3 = (f32[32,16,8,128]{3,2,1,0:T(8,128)S(1)}, f32[384,128]{1,0:T(8,128)S(1)}, f32[384,128]{1,0:T(8,128)S(1)}, f32[32,3,8,128]{3,2,1,0:T(8,128)S(1)}, f32[32,3,8,128]{3,2,1,0:T(8,128)S(1)}) custom-call(f32[32,16,8,128]{3,2,1,0:T(8,128)S(1)} %get-tuple-element.50.acc_ref, f32[32,16,8,128]{3,2,1,0:T(8,128)S(1)} %get-tuple-element.42.p_ref.start_ref, ...), custom_call_target="tpu_custom_call" | custom-call | flops 15728640 | bytes 8388608 | tf_op jit(solution)/shard_map/edge/pallas_call | solution.py:732
  47.6 2.0 %collective-permute-start.6 = (f32[32,3,8,128]{3,2,1,0:T(8,128)S(1)}, f32[32,3,8,128]{3,2,1,0:T(8,128)S(1)}, u32[]{:S(2)}, u32[]{:S(2)}) collective-permute-start(f32[32,3,8,128]{3,2,1,0:T(8,128)S(1)} %get-tuple-element.57), channel_id=1, source_target_pairs={{0,15},{1,0},{2,1},{3,2},{4,3},{5,4},{6,5},{7,6},{8,7},{9,8},{10,9... | collective-permute-start | bytes 1179656 | tf_op jit(solution)/shard_map/ppermute | solution.py:747
  49.6 0.0 collective-permute-start.7
  49.6 1.3 collective-permute-start.4
  50.9 0.2 collective-permute-start.5
  51.1 10.3 %inner.2.acc_ref = f32[32,16,8,128]{3,2,1,0:T(8,128)S(1)} custom-call(f32[32,16,8,128]{3,2,1,0:T(8,128)S(1)} %get-tuple-element.54.p_ref, f32[3,32,16,8,128]{4,3,2,1,0:T(8,128)S(1)} %get-tuple-element.51.v_ref), custom_call_target="tpu_custom_call" | custom-call | flops 73400320 | bytes 8388608 | tf_op jit(solution)/shard_map/inner/pallas_call | solution.py:732
  61.3 1.0 collective-permute-done.4.x1_ref
  62.4 2.2 %collective-permute-done.5.x2_ref = f32[384,128]{1,0:T(8,128)S(1)} collective-permute-done((f32[384,128]{1,0:T(8,128)S(1)}, f32[384,128]{1,0:T(8,128)S(1)}, u32[]{:S(2)}, u32[]{:S(2)}) %collective-permute-start.5) | collective-permute-done | bytes 196640 | tf_op jit(solution)/shard_map/ppermute | solution.py:747
  64.6 0.0 collective-permute-done.6.y1_ref
  64.6 2.9 %edge.4 = (f32[32,16,8,128]{3,2,1,0:T(8,128)S(1)}, f32[384,128]{1,0:T(8,128)S(1)}, f32[384,128]{1,0:T(8,128)S(1)}, f32[32,3,8,128]{3,2,1,0:T(8,128)S(1)}, f32[32,3,8,128]{3,2,1,0:T(8,128)S(1)}) custom-call(f32[32,16,8,128]{3,2,1,0:T(8,128)S(1)} %inner.2.acc_ref, f32[32,16,8,128]{3,2,1,0:T(8,128)S(1)} %get-tuple-element.42.p_ref.start_ref, ...), custom_call_target="tpu_custom_call" | custom-call | flops 15728640 | bytes 8388608 | tf_op jit(solution)/shard_map/edge/pallas_call | solution.py:732
  67.5 0.1 collective-permute-start.10
  67.6 0.7 collective-permute-start.11
  68.3 5.1 %collective-permute-start.9 = (f32[384,128]{1,0:T(8,128)S(1)}, f32[384,128]{1,0:T(8,128)S(1)}, u32[]{:S(2)}, u32[]{:S(2)}) collective-permute-start(f32[384,128]{1,0:T(8,128)S(1)} %get-tuple-element.61), channel_id=1, source_target_pairs={{0,112},{16,0},{32,16},{48,32},{64,48},{80,64},{96,80},{112,96},{1... | collective-permute-start | bytes 589832 | tf_op jit(solution)/shard_map/ppermute | solution.py:747
  73.4 10.3 %inner.3.acc_ref = f32[32,16,8,128]{3,2,1,0:T(8,128)S(1)} custom-call(f32[32,16,8,128]{3,2,1,0:T(8,128)S(1)} %get-tuple-element.59.p_ref, f32[3,32,16,8,128]{4,3,2,1,0:T(8,128)S(1)} %get-tuple-element.51.v_ref), custom_call_target="tpu_custom_call" | custom-call | flops 73400320 | bytes 8388608 | tf_op jit(solution)/shard_map/inner/pallas_call | solution.py:732
  83.6 0.0 collective-permute-done.8.x1_ref
  83.7 3.0 %edge.5 = (f32[32,16,8,128]{3,2,1,0:T(8,128)S(1)}, f32[768,128]{1,0:T(8,128)S(1)}, f32[768,128]{1,0:T(8,128)S(1)}, f32[32,6,8,128]{3,2,1,0:T(8,128)S(1)}, f32[32,6,8,128]{3,2,1,0:T(8,128)S(1)}) custom-call(f32[32,16,8,128]{3,2,1,0:T(8,128)S(1)} %inner.3.acc_ref, f32[32,16,8,128]{3,2,1,0:T(8,128)S(1)} %get-tuple-element.42.p_ref.start_ref, ...), custom_call_target="tpu_custom_call" | custom-call | flops 15728640 | bytes 8388608 | tf_op jit(solution)/shard_map/edge/pallas_call | solution.py:732
  86.7 4.4 %collective-permute-start.14 = (f32[32,6,8,128]{3,2,1,0:T(8,128)S(1)}, f32[32,6,8,128]{3,2,1,0:T(8,128)S(1)}, u32[]{:S(2)}, u32[]{:S(2)}) collective-permute-start(f32[32,6,8,128]{3,2,1,0:T(8,128)S(1)} %get-tuple-element.67), channel_id=1, source_target_pairs={{0,15},{1,0},{2,1},{3,2},{4,3},{5,4},{6,5},{7,6},{8,7},{9,8},{10,9... | collective-permute-start | bytes 2359304 | tf_op jit(solution)/shard_map/ppermute | solution.py:747
  91.1 1.5 collective-permute-start.12
  92.6 0.0 collective-permute-start.13
  92.6 7.4 %core.1 = (f32[32,16,8,128]{3,2,1,0:T(8,128)S(1)}, f32[32,16,8,128]{3,2,1,0:T(8,128)S(1)}, f32[32,16,8,128]{3,2,1,0:T(8,128)S(1)}, f32[32,16,8,128]{3,2,1,0:T(8,128)S(1)}) custom-call(f32[32,16,8,128]{3,2,1,0:T(8,128)S(1)} %get-tuple-element.64.adv_ref), custom_call_target="tpu_custom_call" | custom-call | flops 47185920 | bytes 8388608 | tf_op jit(solution)/shard_map/core/pallas_call | solution.py:732
  100.1 5.9 %collective-permute-done.14.yhi_ref = f32[32,6,8,128]{3,2,1,0:T(8,128)S(1)} collective-permute-done((f32[32,6,8,128]{3,2,1,0:T(8,128)S(1)}, f32[32,6,8,128]{3,2,1,0:T(8,128)S(1)}, u32[]{:S(2)}, u32[]{:S(2)}) %collective-permute-start.14) | collective-permute-done | bytes 786464 | tf_op jit(solution)/shard_map/ppermute | solution.py:747
  105.9 1.8 %collective-permute-done.15.ylo_ref = f32[32,6,8,128]{3,2,1,0:T(8,128)S(1)} collective-permute-done((f32[32,6,8,128]{3,2,1,0:T(8,128)S(1)}, f32[32,6,8,128]{3,2,1,0:T(8,128)S(1)}, u32[]{:S(2)}, u32[]{:S(2)}) %collective-permute-start.15) | collective-permute-done | bytes 786464 | tf_op jit(solution)/shard_map/ppermute | solution.py:747
  107.8 7.8 %sides.1 = (f32[3,4,28,8,128]{4,3,2,1,0:T(8,128)S(1)}, f32[32,28,8,128]{3,2,1,0:T(8,128)S(1)}) custom-call(f32[32,16,8,128]{3,2,1,0:T(8,128)S(1)} %get-tuple-element.64.adv_ref, f32[32,6,8,128]{3,2,1,0:T(8,128)S(1)} %collective-permute-done.14.yhi_ref, f32[32,6,8,128]{3,2,1,0:T(8,128)S(1)} %collective-permute-done.15.ylo_ref, ...), custom_call_target="tpu_custom_call" | custom-call | flops 36700160 | bytes 8388608 | tf_op jit(solution)/shard_map/sides/pallas_call | solution.py:732
  115.6 0.6 collective-permute-done.12.xhi_ref
  116.2 1.2 collective-permute-done.13.xlo_ref
  117.4 0.8 collective-permute-start.16
  118.2 3.5 %collective-permute-start.17 = (f32[30,8,128]{2,1,0:T(8,128)S(1)}, f32[30,8,128]{2,1,0:T(8,128)S(1)}, u32[]{:S(2)}, u32[]{:S(2)}) collective-permute-start(f32[30,8,128]{2,1,0:T(8,128)S(1)} %get-tuple-element.75), channel_id=1, source_target_pairs={{0,15},{1,0},{2,1},{3,2},{4,3},{5,4},{6,5},{7,6},{8,7},{9,8},{10,9... | collective-permute-start | bytes 368648 | tf_op jit(solution)/shard_map/ppermute | solution.py:747
  121.7 4.4 %outputs.1 = (f32[4096,128]{1,0:T(8,128)}, f32[10,64,128]{2,1,0:T(8,128)S(1)}) custom-call(f32[32,28,8,128]{3,2,1,0:T(8,128)S(1)} %get-tuple-element.76.last.rows_ref), custom_call_target="tpu_custom_call" | custom-call | flops 20971520 | bytes 8388608 | tf_op jit(solution)/shard_map/outputs/pallas_call | solution.py:732
  126.1 8.7 %finish.1 = (f32[4096,128]{1,0:T(8,128)}, f32[16,64,128]{2,1,0:T(8,128)S(1)}) custom-call(f32[32,16,8,128]{3,2,1,0:T(8,128)S(1)} %get-tuple-element.64.adv_ref, f32[768,128]{1,0:T(8,128)S(1)} %collective-permute-done.12.xhi_ref, f32[768,128]{1,0:T(8,128)S(1)} %collective-permute-done.13.xlo_ref, ...), custom_call_target="tpu_custom_call", output_to_operand_aliasing={{0}: (10, {})} | custom-call | flops 131072000 | bytes 8388608 | tf_op jit(solution)/shard_map/finish/pallas_call | solution.py:732
  134.8 16.7 %all_to_all.10 = f32[16,64,128]{2,1,0:T(8,128)S(1)} all-to-all(f32[16,64,128]{2,1,0:T(8,128)S(1)} %get-tuple-element.80), channel_id=1, replica_groups=mesh['gx'=8,'gy'=16] {'gy'}, dimensions={0} | all-to-all | bytes 1048576 | tf_op jit(solution)/shard_map/all_to_all | solution.py:826
  151.4 0.8 slice_bitcast_fusion
  (18 shorter events, 0.1 us)
Async XLA Ops:
  0.6 1.1 copy-start.3
  3.0 22.8 %all-to-all-start = ((f32[16,120,128]{2,1,0:T(8,128)}), f32[16,120,128]{2,1,0:T(8,128)S(1)}, u32[]{:S(2)}, u32[]{:S(2)}) async-start(f32[16,120,128]{2,1,0:T(8,128)} %pack.1), calls=%async_computation | async-start | bytes 1966080 | tf_op jit(solution)/shard_map/all_to_all | solution.py:761
  10.8 1.6 %copy-start.2 = (f32[32,16,1024]{2,1,0:T(8,128)S(1)}, f32[32,16,1024]{2,1,0:T(8,128)}, u32[]{:S(2)}) copy-start(f32[32,16,1024]{2,1,0:T(8,128)} %param.3) | copy-start | bytes 6291460
  13.8 30.0 %collective-permute-start.2 = (f32[32,3,8,128]{3,2,1,0:T(8,128)}, f32[32,3,8,128]{3,2,1,0:T(8,128)}, u32[]{:S(2)}, u32[]{:S(2)}) collective-permute-start(f32[32,3,8,128]{3,2,1,0:T(8,128)} %get-tuple-element.52), channel_id=1, source_target_pairs={{0,1},{1,2},{2,3},{3,4},{4,5},{5,6},{6,7},{7,8},{8,9},{9,10},{10,1... | collective-permute-start | bytes 1179656 | tf_op jit(solution)/shard_map/ppermute | solution.py:747
  15.4 28.4 %collective-permute-start.3 = (f32[32,3,8,128]{3,2,1,0:T(8,128)}, f32[32,3,8,128]{3,2,1,0:T(8,128)}, u32[]{:S(2)}, u32[]{:S(2)}) collective-permute-start(f32[32,3,8,128]{3,2,1,0:T(8,128)} %get-tuple-element.53), channel_id=1, source_target_pairs={{0,15},{1,0},{2,1},{3,2},{4,3},{5,4},{6,5},{7,6},{8,7},{9,8},{10,9... | collective-permute-start | bytes 1179656 | tf_op jit(solution)/shard_map/ppermute | solution.py:747
  22.9 2.0 %copy-start = (f32[2,32,16,8,128]{4,3,2,1,0:T(8,128)}, f32[2,32,16,8,128]{4,3,2,1,0:T(8,128)S(1)}, u32[]{:S(2)}) copy-start(f32[2,32,16,8,128]{4,3,2,1,0:T(8,128)S(1)} %get-tuple-element.46.both_ref) | copy-start | bytes 12582916
  24.9 6.2 %copy-start.4 = (s32[2,1,64]{2,1,0:T(1,128)S(1)}, s32[2,1,64]{2,1,0:T(1,128)}, u32[]{:S(2)}) copy-start(s32[2,1,64]{2,1,0:T(1,128)} %band_ref.3) | copy-start | bytes 1540
  25.9 16.4 %collective-permute-start = (f32[504,128]{1,0:T(8,128)S(1)}, f32[504,128]{1,0:T(8,128)S(1)}, u32[]{:S(2)}, u32[]{:S(2)}) collective-permute-start(f32[504,128]{1,0:T(8,128)S(1)} %get-tuple-element.44), channel_id=1, source_target_pairs={{0,16},{16,32},{32,48},{48,64},{64,80},{80,96},{96,112},{112,0},{1... | collective-permute-start | bytes 774152 | tf_op jit(solution)/shard_map/ppermute | solution.py:747
  27.3 15.0 %collective-permute-start.1 = (f32[504,128]{1,0:T(8,128)S(1)}, f32[504,128]{1,0:T(8,128)S(1)}, u32[]{:S(2)}, u32[]{:S(2)}) collective-permute-start(f32[504,128]{1,0:T(8,128)S(1)} %get-tuple-element.45), channel_id=1, source_target_pairs={{0,112},{16,0},{32,16},{48,32},{64,48},{80,64},{96,80},{112,96},{1... | collective-permute-start | bytes 774152 | tf_op jit(solution)/shard_map/ppermute | solution.py:747
  31.1 2.2 %copy-start.1 = (f32[2,32,16,8,128]{4,3,2,1,0:T(8,128)S(1)}, f32[2,32,16,8,128]{4,3,2,1,0:T(8,128)}, u32[]{:S(2)}) copy-start(f32[2,32,16,8,128]{4,3,2,1,0:T(8,128)} %copy-done) | copy-start | bytes 12582916
  47.6 17.0 %collective-permute-start.6 = (f32[32,3,8,128]{3,2,1,0:T(8,128)S(1)}, f32[32,3,8,128]{3,2,1,0:T(8,128)S(1)}, u32[]{:S(2)}, u32[]{:S(2)}) collective-permute-start(f32[32,3,8,128]{3,2,1,0:T(8,128)S(1)} %get-tuple-element.57), channel_id=1, source_target_pairs={{0,15},{1,0},{2,1},{3,2},{4,3},{5,4},{6,5},{7,6},{8,7},{9,8},{10,9... | collective-permute-start | bytes 1179656 | tf_op jit(solution)/shard_map/ppermute | solution.py:747
  49.6 15.0 %collective-permute-start.7 = (f32[32,3,8,128]{3,2,1,0:T(8,128)S(1)}, f32[32,3,8,128]{3,2,1,0:T(8,128)S(1)}, u32[]{:S(2)}, u32[]{:S(2)}) collective-permute-start(f32[32,3,8,128]{3,2,1,0:T(8,128)S(1)} %get-tuple-element.58), channel_id=1, source_target_pairs={{0,1},{1,2},{2,3},{3,4},{4,5},{5,6},{6,7},{7,8},{8,9},{9,10},{10,1... | collective-permute-start | bytes 1179656 | tf_op jit(solution)/shard_map/ppermute | solution.py:747
  49.6 12.7 %collective-permute-start.4 = (f32[384,128]{1,0:T(8,128)S(1)}, f32[384,128]{1,0:T(8,128)S(1)}, u32[]{:S(2)}, u32[]{:S(2)}) collective-permute-start(f32[384,128]{1,0:T(8,128)S(1)} %get-tuple-element.55), channel_id=1, source_target_pairs={{0,112},{16,0},{32,16},{48,32},{64,48},{80,64},{96,80},{112,96},{1... | collective-permute-start | bytes 589832 | tf_op jit(solution)/shard_map/ppermute | solution.py:747
  50.9 13.7 %collective-permute-start.5 = (f32[384,128]{1,0:T(8,128)S(1)}, f32[384,128]{1,0:T(8,128)S(1)}, u32[]{:S(2)}, u32[]{:S(2)}) collective-permute-start(f32[384,128]{1,0:T(8,128)S(1)} %get-tuple-element.56), channel_id=1, source_target_pairs={{0,16},{16,32},{32,48},{48,64},{64,80},{80,96},{96,112},{112,0},{1... | collective-permute-start | bytes 589832 | tf_op jit(solution)/shard_map/ppermute | solution.py:747
  67.5 16.1 %collective-permute-start.10 = (f32[32,3,8,128]{3,2,1,0:T(8,128)S(1)}, f32[32,3,8,128]{3,2,1,0:T(8,128)S(1)}, u32[]{:S(2)}, u32[]{:S(2)}) collective-permute-start(f32[32,3,8,128]{3,2,1,0:T(8,128)S(1)} %get-tuple-element.62), channel_id=1, source_target_pairs={{0,1},{1,2},{2,3},{3,4},{4,5},{5,6},{6,7},{7,8},{8,9},{9,10},{10,1... | collective-permute-start | bytes 1179656 | tf_op jit(solution)/shard_map/ppermute | solution.py:747
  67.6 16.0 %collective-permute-start.11 = (f32[32,3,8,128]{3,2,1,0:T(8,128)S(1)}, f32[32,3,8,128]{3,2,1,0:T(8,128)S(1)}, u32[]{:S(2)}, u32[]{:S(2)}) collective-permute-start(f32[32,3,8,128]{3,2,1,0:T(8,128)S(1)} %get-tuple-element.63), channel_id=1, source_target_pairs={{0,15},{1,0},{2,1},{3,2},{4,3},{5,4},{6,5},{7,6},{8,7},{9,8},{10,9... | collective-permute-start | bytes 1179656 | tf_op jit(solution)/shard_map/ppermute | solution.py:747
  68.3 15.3 %collective-permute-start.8 = (f32[384,128]{1,0:T(8,128)S(1)}, f32[384,128]{1,0:T(8,128)S(1)}, u32[]{:S(2)}, u32[]{:S(2)}) collective-permute-start(f32[384,128]{1,0:T(8,128)S(1)} %get-tuple-element.60), channel_id=1, source_target_pairs={{0,16},{16,32},{32,48},{48,64},{64,80},{80,96},{96,112},{112,0},{1... | collective-permute-start | bytes 589832 | tf_op jit(solution)/shard_map/ppermute | solution.py:747
  68.3 15.4 %collective-permute-start.9 = (f32[384,128]{1,0:T(8,128)S(1)}, f32[384,128]{1,0:T(8,128)S(1)}, u32[]{:S(2)}, u32[]{:S(2)}) collective-permute-start(f32[384,128]{1,0:T(8,128)S(1)} %get-tuple-element.61), channel_id=1, source_target_pairs={{0,112},{16,0},{32,16},{48,32},{64,48},{80,64},{96,80},{112,96},{1... | collective-permute-start | bytes 589832 | tf_op jit(solution)/shard_map/ppermute | solution.py:747
  86.7 19.3 %collective-permute-start.14 = (f32[32,6,8,128]{3,2,1,0:T(8,128)S(1)}, f32[32,6,8,128]{3,2,1,0:T(8,128)S(1)}, u32[]{:S(2)}, u32[]{:S(2)}) collective-permute-start(f32[32,6,8,128]{3,2,1,0:T(8,128)S(1)} %get-tuple-element.67), channel_id=1, source_target_pairs={{0,15},{1,0},{2,1},{3,2},{4,3},{5,4},{6,5},{7,6},{8,7},{9,8},{10,9... | collective-permute-start | bytes 2359304 | tf_op jit(solution)/shard_map/ppermute | solution.py:747
  91.1 16.7 %collective-permute-start.15 = (f32[32,6,8,128]{3,2,1,0:T(8,128)S(1)}, f32[32,6,8,128]{3,2,1,0:T(8,128)S(1)}, u32[]{:S(2)}, u32[]{:S(2)}) collective-permute-start(f32[32,6,8,128]{3,2,1,0:T(8,128)S(1)} %get-tuple-element.68), channel_id=1, source_target_pairs={{0,1},{1,2},{2,3},{3,4},{4,5},{5,6},{6,7},{7,8},{8,9},{9,10},{10,1... | collective-permute-start | bytes 2359304 | tf_op jit(solution)/shard_map/ppermute | solution.py:747
  91.1 25.1 %collective-permute-start.12 = (f32[768,128]{1,0:T(8,128)S(1)}, f32[768,128]{1,0:T(8,128)S(1)}, u32[]{:S(2)}, u32[]{:S(2)}) collective-permute-start(f32[768,128]{1,0:T(8,128)S(1)} %get-tuple-element.65), channel_id=1, source_target_pairs={{0,112},{16,0},{32,16},{48,32},{64,48},{80,64},{96,80},{112,96},{1... | collective-permute-start | bytes 1179656 | tf_op jit(solution)/shard_map/ppermute | solution.py:747
  92.6 24.8 %collective-permute-start.13 = (f32[768,128]{1,0:T(8,128)S(1)}, f32[768,128]{1,0:T(8,128)S(1)}, u32[]{:S(2)}, u32[]{:S(2)}) collective-permute-start(f32[768,128]{1,0:T(8,128)S(1)} %get-tuple-element.66), channel_id=1, source_target_pairs={{0,16},{16,32},{32,48},{48,64},{64,80},{80,96},{96,112},{112,0},{1... | collective-permute-start | bytes 1179656 | tf_op jit(solution)/shard_map/ppermute | solution.py:747
  117.4 8.7 %collective-permute-start.16 = (f32[30,8,128]{2,1,0:T(8,128)S(1)}, f32[30,8,128]{2,1,0:T(8,128)S(1)}, u32[]{:S(2)}, u32[]{:S(2)}) collective-permute-start(f32[30,8,128]{2,1,0:T(8,128)S(1)} %get-tuple-element.74), channel_id=1, source_target_pairs={{0,1},{1,2},{2,3},{3,4},{4,5},{5,6},{6,7},{7,8},{8,9},{9,10},{10,1... | collective-permute-start | bytes 368648 | tf_op jit(solution)/shard_map/ppermute | solution.py:747
  118.2 7.9 %collective-permute-start.17 = (f32[30,8,128]{2,1,0:T(8,128)S(1)}, f32[30,8,128]{2,1,0:T(8,128)S(1)}, u32[]{:S(2)}, u32[]{:S(2)}) collective-permute-start(f32[30,8,128]{2,1,0:T(8,128)S(1)} %get-tuple-element.75), channel_id=1, source_target_pairs={{0,15},{1,0},{2,1},{3,2},{4,3},{5,4},{6,5},{7,6},{8,7},{9,8},{10,9... | collective-permute-start | bytes 368648 | tf_op jit(solution)/shard_map/ppermute | solution.py:747

commit v6 on v5

--- a/solution.py
+++ b/solution.py
@@ -391,11 +391,6 @@
     loop_pairs(1, 31, y_line)
 
 
-def refine_and_rate(mid_ref, band_ref, p_ref, both_ref, v_ref, ends_ref, acc_ref, fine, band):
-    refine_inner(mid_ref, band_ref, v_ref, ends_ref, fine, band)
-    inner_rate_first(p_ref, v_ref, both_ref, acc_ref)
-
-
 def join_x(p_ref, coarse_ref, mark_ref, low_ref, high_ref):
     for x in range(3):
         for y in range(16):
@@ -769,10 +764,11 @@
     coarse = coarse.reshape(1920, 128)
     xlo, xhi = call(join_x, (f32(504, 128), f32(504, 128)), start, coarse, tips, name="join", mib=4)
     halo = star(xlo, xhi, ylo, yhi)
-    velocity, ends, acc = call(
-        refine_and_rate, (f32(3, 32, 16, *col), f32(2, 240, 128), block), coarse, band_mask, start, both,
-        scratch=[(3840, 128), (2, *col)], name="refine", mib=20, ops=512 * 110,
-    )
+    velocity, ends = call(
+        refine_inner, (f32(3, 32, 16, *col), f32(2, 240, 128)), coarse, band_mask,
+        scratch=[(3840, 128), (2, *col)], name="refine", mib=20, ops=512 * 20,
+    )
+    acc = call(inner_rate_first, block, start, velocity, both, name="first", mib=12, ops=512 * 90)
     current = start
     for number in range(3):
         if number == 0:

time: 153 us -> 152 us (level)
  local copies, waits for them, and re-layouts: 7.69 us -> 5.51 us
  waiting for transfers between devices: 13.8 us -> 15.7 us
    unnamed x10, local copies, waits for them, and re-layouts: 6.87 us -> 4.68 us
    ppermute x18, waiting for transfers between devices: 12.8 us -> 14.6 us  [moved(): lax.ppermute(values, axis, [(i, (i + step) % count) for i in range(count)])]
    pallas_call x16 -> x17, Pallas kernels: 79.3 us -> 79.1 us  [call(): pl.pallas_call(kernel, out_shape=outs, in_specs=[spec(k) for k in range(l...]
where the time goes in v6:
time: 152 us; the launch traced here: 151 us
  Pallas kernels  79.1 us (52%)
  starting transfers between devices  33.4 us (22%)
  blocking collectives  16.7 us (11%)
  waiting for transfers between devices  15.7 us (10%)
  local copies, waits for them, and re-layouts  5.51 us (4%)
    pallas_call x17, Pallas kernels, call(): pl.pallas_call(kernel, out_shape=outs, in_specs=[spec(k) for k in range(l...  79.1 us
    ppermute x18, starting transfers between devices, moved(): lax.ppermute(values, axis, [(i, (i + step) % count) for i in range(count)])  25.6 us
    all_to_all x1, blocking collectives, per_device(): lax.all_to_all(packed, 'gy', split_axis=0, concat_axis=0, tiled=True)  16.7 us
    ppermute x18, waiting for transfers between devices, moved(): lax.ppermute(values, axis, [(i, (i + step) % count) for i in range(count)])  14.6 us
    all_to_all x1, starting transfers between devices, per_device(): coarse = lax.all_to_all(send, 'gy', split_axis=0, concat_axis=0, tiled=True)  7.76 us
    unnamed x10, local copies, waits for them, and re-layouts  4.68 us
  transfers between devices with their start and end apart: 19, of which 7 were waited for; matrix products, arithmetic and copies ran while one was open for 0% of the time, Pallas kernels for 39%

profile of v6, /device:TPU:1, one launch (start us, length us, event | category | flops | bytes accessed | tf_op | source)
XLA Modules:
  0.0 151.2 jit_solution(13938959239939531752)
XLA Ops:
  0.6 1.1 copy-done.3
  1.8 1.3 pack.1
  3.0 7.8 %all-to-all-start = ((f32[16,120,128]{2,1,0:T(8,128)}), f32[16,120,128]{2,1,0:T(8,128)S(1)}, u32[]{:S(2)}, u32[]{:S(2)}) async-start(f32[16,120,128]{2,1,0:T(8,128)} %pack.1), calls=%async_computation | async-start | bytes 1966080 | tf_op jit(solution)/shard_map/all_to_all | solution.py:756
  10.8 1.6 %copy-done.2 = f32[32,16,1024]{2,1,0:T(8,128)S(1)} copy-done((f32[32,16,1024]{2,1,0:T(8,128)S(1)}, f32[32,16,1024]{2,1,0:T(8,128)}, u32[]{:S(2)}) %copy-start.2) | copy-done | bytes 2097176
  12.4 1.4 unpack.1
  13.8 1.6 %collective-permute-start.2 = (f32[32,3,8,128]{3,2,1,0:T(8,128)}, f32[32,3,8,128]{3,2,1,0:T(8,128)}, u32[]{:S(2)}, u32[]{:S(2)}) collective-permute-start(f32[32,3,8,128]{3,2,1,0:T(8,128)} %get-tuple-element.50), channel_id=1, source_target_pairs={{0,1},{1,2},{2,3},{3,4},{4,5},{5,6},{6,7},{7,8},{8,9},{9,10},{10,1... | collective-permute-start | bytes 1179656 | tf_op jit(solution)/shard_map/ppermute | solution.py:742
  15.4 0.0 collective-permute-start.3
  15.4 7.5 %depth.1 = (f32[2,32,16,8,128]{4,3,2,1,0:T(8,128)S(1)}, f32[2,2,16,8,128]{4,3,2,1,0:T(8,128)S(1)}) custom-call(f32[32,16,8,128]{3,2,1,0:T(8,128)S(1)} %get-tuple-element.41.p_ref.start_ref), custom_call_target="tpu_custom_call" | custom-call | flops 47185920 | bytes 8388608 | tf_op jit(solution)/shard_map/depth/pallas_call | solution.py:727
  22.9 2.0 %copy-done = f32[2,32,16,8,128]{4,3,2,1,0:T(8,128)} copy-done((f32[2,32,16,8,128]{4,3,2,1,0:T(8,128)}, f32[2,32,16,8,128]{4,3,2,1,0:T(8,128)S(1)}, u32[]{:S(2)}) %copy-start) | copy-done | bytes 4194328
  24.9 1.0 all-to-all-done
  25.9 1.4 collective-permute-start
  27.3 3.8 %collective-permute-start.1 = (f32[504,128]{1,0:T(8,128)S(1)}, f32[504,128]{1,0:T(8,128)S(1)}, u32[]{:S(2)}, u32[]{:S(2)}) collective-permute-start(f32[504,128]{1,0:T(8,128)S(1)} %get-tuple-element.44), channel_id=1, source_target_pairs={{0,112},{16,0},{32,16},{48,32},{64,48},{80,64},{96,80},{112,96},{1... | collective-permute-start | bytes 774152 | tf_op jit(solution)/shard_map/ppermute | solution.py:742
  31.1 3.9 %refine.1 = (f32[3,32,16,8,128]{4,3,2,1,0:T(8,128)S(1)}, f32[2,240,128]{2,1,0:T(8,128)S(1)}) custom-call(f32[1920,128]{1,0:T(8,128)S(1)} %bitcast.30, s32[2,1,64]{2,1,0:T(1,128)S(1)} %copy-done.4), custom_call_target="tpu_custom_call" | custom-call | flops 10485760 | bytes 8388608 | tf_op jit(solution)/shard_map/refine/pallas_call | solution.py:727
  35.0 5.2 %first.1.acc_in = f32[32,16,8,128]{3,2,1,0:T(8,128)S(1)} custom-call(f32[32,16,8,128]{3,2,1,0:T(8,128)S(1)} %get-tuple-element.41.p_ref.start_ref, f32[3,32,16,8,128]{4,3,2,1,0:T(8,128)S(1)} %get-tuple-element.46.v_ref.v_in, f32[2,32,16,8,128]{4,3,2,1,0:T(8,128)S(1)} %copy-done.1), custom_call_target="tpu_custom_call" | custom-call | flops 47185920 | bytes 8388608 | tf_op jit(solution)/shard_map/first/pallas_call | solution.py:727
  40.2 1.4 collective-permute-done.lo_ref.x1_ref
  41.6 0.0 collective-permute-done.1.hi_ref.x2_ref
  41.6 1.4 ends.1
  43.0 0.0 collective-permute-done.2.y1_ref
  43.1 0.0 collective-permute-done.3.y2_ref
  43.1 3.8 %edge.3 = (f32[32,16,8,128]{3,2,1,0:T(8,128)S(1)}, f32[384,128]{1,0:T(8,128)S(1)}, f32[384,128]{1,0:T(8,128)S(1)}, f32[32,3,8,128]{3,2,1,0:T(8,128)S(1)}, f32[32,3,8,128]{3,2,1,0:T(8,128)S(1)}) custom-call(f32[32,16,8,128]{3,2,1,0:T(8,128)S(1)} %get-tuple-element.48.acc_ref, f32[32,16,8,128]{3,2,1,0:T(8,128)S(1)} %get-tuple-element.41.p_ref.start_ref, ...), custom_call_target="tpu_custom_call" | custom-call | flops 15728640 | bytes 8388608 | tf_op jit(solution)/shard_map/edge/pallas_call | solution.py:727
  46.9 0.7 collective-permute-start.6
  47.6 1.2 collective-permute-start.7
  48.7 1.4 collective-permute-start.4
  50.2 0.0 collective-permute-start.5
  50.2 10.3 %inner.2.acc_ref = f32[32,16,8,128]{3,2,1,0:T(8,128)S(1)} custom-call(f32[32,16,8,128]{3,2,1,0:T(8,128)S(1)} %get-tuple-element.52.p_ref, f32[3,32,16,8,128]{4,3,2,1,0:T(8,128)S(1)} %get-tuple-element.49.v_ref), custom_call_target="tpu_custom_call" | custom-call | flops 73400320 | bytes 8388608 | tf_op jit(solution)/shard_map/inner/pallas_call | solution.py:727
  60.4 0.0 collective-permute-done.4.x1_ref
  60.5 3.2 %collective-permute-done.5.x2_ref = f32[384,128]{1,0:T(8,128)S(1)} collective-permute-done((f32[384,128]{1,0:T(8,128)S(1)}, f32[384,128]{1,0:T(8,128)S(1)}, u32[]{:S(2)}, u32[]{:S(2)}) %collective-permute-start.5) | collective-permute-done | bytes 196640 | tf_op jit(solution)/shard_map/ppermute | solution.py:742
  63.6 2.9 %edge.4 = (f32[32,16,8,128]{3,2,1,0:T(8,128)S(1)}, f32[384,128]{1,0:T(8,128)S(1)}, f32[384,128]{1,0:T(8,128)S(1)}, f32[32,3,8,128]{3,2,1,0:T(8,128)S(1)}, f32[32,3,8,128]{3,2,1,0:T(8,128)S(1)}) custom-call(f32[32,16,8,128]{3,2,1,0:T(8,128)S(1)} %inner.2.acc_ref, f32[32,16,8,128]{3,2,1,0:T(8,128)S(1)} %get-tuple-element.41.p_ref.start_ref, ...), custom_call_target="tpu_custom_call" | custom-call | flops 15728640 | bytes 8388608 | tf_op jit(solution)/shard_map/edge/pallas_call | solution.py:727
  66.6 0.1 collective-permute-start.10
  66.6 0.9 collective-permute-start.11
  67.5 5.1 %collective-permute-start.9 = (f32[384,128]{1,0:T(8,128)S(1)}, f32[384,128]{1,0:T(8,128)S(1)}, u32[]{:S(2)}, u32[]{:S(2)}) collective-permute-start(f32[384,128]{1,0:T(8,128)S(1)} %get-tuple-element.59), channel_id=1, source_target_pairs={{0,112},{16,0},{32,16},{48,32},{64,48},{80,64},{96,80},{112,96},{1... | collective-permute-start | bytes 589832 | tf_op jit(solution)/shard_map/ppermute | solution.py:742
  72.6 10.3 %inner.3.acc_ref = f32[32,16,8,128]{3,2,1,0:T(8,128)S(1)} custom-call(f32[32,16,8,128]{3,2,1,0:T(8,128)S(1)} %get-tuple-element.57.p_ref, f32[3,32,16,8,128]{4,3,2,1,0:T(8,128)S(1)} %get-tuple-element.49.v_ref), custom_call_target="tpu_custom_call" | custom-call | flops 73400320 | bytes 8388608 | tf_op jit(solution)/shard_map/inner/pallas_call | solution.py:727
  82.9 3.0 %edge.5 = (f32[32,16,8,128]{3,2,1,0:T(8,128)S(1)}, f32[768,128]{1,0:T(8,128)S(1)}, f32[768,128]{1,0:T(8,128)S(1)}, f32[32,6,8,128]{3,2,1,0:T(8,128)S(1)}, f32[32,6,8,128]{3,2,1,0:T(8,128)S(1)}) custom-call(f32[32,16,8,128]{3,2,1,0:T(8,128)S(1)} %inner.3.acc_ref, f32[32,16,8,128]{3,2,1,0:T(8,128)S(1)} %get-tuple-element.41.p_ref.start_ref, ...), custom_call_target="tpu_custom_call" | custom-call | flops 15728640 | bytes 8388608 | tf_op jit(solution)/shard_map/edge/pallas_call | solution.py:727
  85.9 4.4 %collective-permute-start.14 = (f32[32,6,8,128]{3,2,1,0:T(8,128)S(1)}, f32[32,6,8,128]{3,2,1,0:T(8,128)S(1)}, u32[]{:S(2)}, u32[]{:S(2)}) collective-permute-start(f32[32,6,8,128]{3,2,1,0:T(8,128)S(1)} %get-tuple-element.65), channel_id=1, source_target_pairs={{0,15},{1,0},{2,1},{3,2},{4,3},{5,4},{6,5},{7,6},{8,7},{9,8},{10,9... | collective-permute-start | bytes 2359304 | tf_op jit(solution)/shard_map/ppermute | solution.py:742
  90.3 1.1 collective-permute-start.12
  91.5 0.3 collective-permute-start.13
  91.8 7.3 %core.1 = (f32[32,16,8,128]{3,2,1,0:T(8,128)S(1)}, f32[32,16,8,128]{3,2,1,0:T(8,128)S(1)}, f32[32,16,8,128]{3,2,1,0:T(8,128)S(1)}, f32[32,16,8,128]{3,2,1,0:T(8,128)S(1)}) custom-call(f32[32,16,8,128]{3,2,1,0:T(8,128)S(1)} %get-tuple-element.62.adv_ref), custom_call_target="tpu_custom_call" | custom-call | flops 47185920 | bytes 8388608 | tf_op jit(solution)/shard_map/core/pallas_call | solution.py:727
  99.1 6.6 %collective-permute-done.14.yhi_ref = f32[32,6,8,128]{3,2,1,0:T(8,128)S(1)} collective-permute-done((f32[32,6,8,128]{3,2,1,0:T(8,128)S(1)}, f32[32,6,8,128]{3,2,1,0:T(8,128)S(1)}, u32[]{:S(2)}, u32[]{:S(2)}) %collective-permute-start.14) | collective-permute-done | bytes 786464 | tf_op jit(solution)/shard_map/ppermute | solution.py:742
  105.7 1.6 %collective-permute-done.15.ylo_ref = f32[32,6,8,128]{3,2,1,0:T(8,128)S(1)} collective-permute-done((f32[32,6,8,128]{3,2,1,0:T(8,128)S(1)}, f32[32,6,8,128]{3,2,1,0:T(8,128)S(1)}, u32[]{:S(2)}, u32[]{:S(2)}) %collective-permute-start.15) | collective-permute-done | bytes 786464 | tf_op jit(solution)/shard_map/ppermute | solution.py:742
  107.3 7.8 %sides.1 = (f32[3,4,28,8,128]{4,3,2,1,0:T(8,128)S(1)}, f32[32,28,8,128]{3,2,1,0:T(8,128)S(1)}) custom-call(f32[32,16,8,128]{3,2,1,0:T(8,128)S(1)} %get-tuple-element.62.adv_ref, f32[32,6,8,128]{3,2,1,0:T(8,128)S(1)} %collective-permute-done.14.yhi_ref, f32[32,6,8,128]{3,2,1,0:T(8,128)S(1)} %collective-permute-done.15.ylo_ref, ...), custom_call_target="tpu_custom_call" | custom-call | flops 36700160 | bytes 8388608 | tf_op jit(solution)/shard_map/sides/pallas_call | solution.py:727
  115.1 0.6 collective-permute-done.12.xhi_ref
  115.7 1.2 collective-permute-done.13.xlo_ref
  117.0 0.8 collective-permute-start.16
  117.7 2.9 %collective-permute-start.17 = (f32[30,8,128]{2,1,0:T(8,128)S(1)}, f32[30,8,128]{2,1,0:T(8,128)S(1)}, u32[]{:S(2)}, u32[]{:S(2)}) collective-permute-start(f32[30,8,128]{2,1,0:T(8,128)S(1)} %get-tuple-element.73), channel_id=1, source_target_pairs={{0,15},{1,0},{2,1},{3,2},{4,3},{5,4},{6,5},{7,6},{8,7},{9,8},{10,9... | collective-permute-start | bytes 368648 | tf_op jit(solution)/shard_map/ppermute | solution.py:742
  120.6 4.4 %outputs.1 = (f32[4096,128]{1,0:T(8,128)}, f32[10,64,128]{2,1,0:T(8,128)S(1)}) custom-call(f32[32,28,8,128]{3,2,1,0:T(8,128)S(1)} %get-tuple-element.74.last.rows_ref), custom_call_target="tpu_custom_call" | custom-call | flops 20971520 | bytes 8388608 | tf_op jit(solution)/shard_map/outputs/pallas_call | solution.py:727
  125.0 8.7 %finish.1 = (f32[4096,128]{1,0:T(8,128)}, f32[16,64,128]{2,1,0:T(8,128)S(1)}) custom-call(f32[32,16,8,128]{3,2,1,0:T(8,128)S(1)} %get-tuple-element.62.adv_ref, f32[768,128]{1,0:T(8,128)S(1)} %collective-permute-done.12.xhi_ref, f32[768,128]{1,0:T(8,128)S(1)} %collective-permute-done.13.xlo_ref, ...), custom_call_target="tpu_custom_call", output_to_operand_aliasing={{0}: (10, {})} | custom-call | flops 131072000 | bytes 8388608 | tf_op jit(solution)/shard_map/finish/pallas_call | solution.py:727
  133.7 16.7 %all_to_all.10 = f32[16,64,128]{2,1,0:T(8,128)S(1)} all-to-all(f32[16,64,128]{2,1,0:T(8,128)S(1)} %get-tuple-element.78), channel_id=1, replica_groups=mesh['gx'=8,'gy'=16] {'gy'}, dimensions={0} | all-to-all | bytes 1048576 | tf_op jit(solution)/shard_map/all_to_all | solution.py:822
  150.4 0.8 slice_bitcast_fusion
  (19 shorter events, 0.1 us)
Async XLA Ops:
  0.6 1.1 copy-start.3
  3.0 22.8 %all-to-all-start = ((f32[16,120,128]{2,1,0:T(8,128)}), f32[16,120,128]{2,1,0:T(8,128)S(1)}, u32[]{:S(2)}, u32[]{:S(2)}) async-start(f32[16,120,128]{2,1,0:T(8,128)} %pack.1), calls=%async_computation | async-start | bytes 1966080 | tf_op jit(solution)/shard_map/all_to_all | solution.py:756
  10.8 1.6 %copy-start.2 = (f32[32,16,1024]{2,1,0:T(8,128)S(1)}, f32[32,16,1024]{2,1,0:T(8,128)}, u32[]{:S(2)}) copy-start(f32[32,16,1024]{2,1,0:T(8,128)} %param.3) | copy-start | bytes 6291460
  13.8 29.3 %collective-permute-start.2 = (f32[32,3,8,128]{3,2,1,0:T(8,128)}, f32[32,3,8,128]{3,2,1,0:T(8,128)}, u32[]{:S(2)}, u32[]{:S(2)}) collective-permute-start(f32[32,3,8,128]{3,2,1,0:T(8,128)} %get-tuple-element.50), channel_id=1, source_target_pairs={{0,1},{1,2},{2,3},{3,4},{4,5},{5,6},{6,7},{7,8},{8,9},{9,10},{10,1... | collective-permute-start | bytes 1179656 | tf_op jit(solution)/shard_map/ppermute | solution.py:742
  15.4 27.7 %collective-permute-start.3 = (f32[32,3,8,128]{3,2,1,0:T(8,128)}, f32[32,3,8,128]{3,2,1,0:T(8,128)}, u32[]{:S(2)}, u32[]{:S(2)}) collective-permute-start(f32[32,3,8,128]{3,2,1,0:T(8,128)} %get-tuple-element.51), channel_id=1, source_target_pairs={{0,15},{1,0},{2,1},{3,2},{4,3},{5,4},{6,5},{7,6},{8,7},{9,8},{10,9... | collective-permute-start | bytes 1179656 | tf_op jit(solution)/shard_map/ppermute | solution.py:742
  22.9 2.0 %copy-start = (f32[2,32,16,8,128]{4,3,2,1,0:T(8,128)}, f32[2,32,16,8,128]{4,3,2,1,0:T(8,128)S(1)}, u32[]{:S(2)}) copy-start(f32[2,32,16,8,128]{4,3,2,1,0:T(8,128)S(1)} %get-tuple-element.47.both_ref) | copy-start | bytes 12582916
  24.9 6.2 %copy-start.4 = (s32[2,1,64]{2,1,0:T(1,128)S(1)}, s32[2,1,64]{2,1,0:T(1,128)}, u32[]{:S(2)}) copy-start(s32[2,1,64]{2,1,0:T(1,128)} %band_ref.3) | copy-start | bytes 1540
  25.9 9.1 %copy-start.1 = (f32[2,32,16,8,128]{4,3,2,1,0:T(8,128)S(1)}, f32[2,32,16,8,128]{4,3,2,1,0:T(8,128)}, u32[]{:S(2)}) copy-start(f32[2,32,16,8,128]{4,3,2,1,0:T(8,128)} %copy-done) | copy-start | bytes 12582916
  25.9 15.7 %collective-permute-start = (f32[504,128]{1,0:T(8,128)S(1)}, f32[504,128]{1,0:T(8,128)S(1)}, u32[]{:S(2)}, u32[]{:S(2)}) collective-permute-start(f32[504,128]{1,0:T(8,128)S(1)} %get-tuple-element.43), channel_id=1, source_target_pairs={{0,16},{16,32},{32,48},{48,64},{64,80},{80,96},{96,112},{112,0},{1... | collective-permute-start | bytes 774152 | tf_op jit(solution)/shard_map/ppermute | solution.py:742
  27.3 14.3 %collective-permute-start.1 = (f32[504,128]{1,0:T(8,128)S(1)}, f32[504,128]{1,0:T(8,128)S(1)}, u32[]{:S(2)}, u32[]{:S(2)}) collective-permute-start(f32[504,128]{1,0:T(8,128)S(1)} %get-tuple-element.44), channel_id=1, source_target_pairs={{0,112},{16,0},{32,16},{48,32},{64,48},{80,64},{96,80},{112,96},{1... | collective-permute-start | bytes 774152 | tf_op jit(solution)/shard_map/ppermute | solution.py:742
  46.9 16.7 %collective-permute-start.6 = (f32[32,3,8,128]{3,2,1,0:T(8,128)S(1)}, f32[32,3,8,128]{3,2,1,0:T(8,128)S(1)}, u32[]{:S(2)}, u32[]{:S(2)}) collective-permute-start(f32[32,3,8,128]{3,2,1,0:T(8,128)S(1)} %get-tuple-element.55), channel_id=1, source_target_pairs={{0,15},{1,0},{2,1},{3,2},{4,3},{5,4},{6,5},{7,6},{8,7},{9,8},{10,9... | collective-permute-start | bytes 1179656 | tf_op jit(solution)/shard_map/ppermute | solution.py:742
  47.6 16.1 %collective-permute-start.7 = (f32[32,3,8,128]{3,2,1,0:T(8,128)S(1)}, f32[32,3,8,128]{3,2,1,0:T(8,128)S(1)}, u32[]{:S(2)}, u32[]{:S(2)}) collective-permute-start(f32[32,3,8,128]{3,2,1,0:T(8,128)S(1)} %get-tuple-element.56), channel_id=1, source_target_pairs={{0,1},{1,2},{2,3},{3,4},{4,5},{5,6},{6,7},{7,8},{8,9},{9,10},{10,1... | collective-permute-start | bytes 1179656 | tf_op jit(solution)/shard_map/ppermute | solution.py:742
  48.7 11.7 %collective-permute-start.4 = (f32[384,128]{1,0:T(8,128)S(1)}, f32[384,128]{1,0:T(8,128)S(1)}, u32[]{:S(2)}, u32[]{:S(2)}) collective-permute-start(f32[384,128]{1,0:T(8,128)S(1)} %get-tuple-element.53), channel_id=1, source_target_pairs={{0,112},{16,0},{32,16},{48,32},{64,48},{80,64},{96,80},{112,96},{1... | collective-permute-start | bytes 589832 | tf_op jit(solution)/shard_map/ppermute | solution.py:742
  50.2 13.5 %collective-permute-start.5 = (f32[384,128]{1,0:T(8,128)S(1)}, f32[384,128]{1,0:T(8,128)S(1)}, u32[]{:S(2)}, u32[]{:S(2)}) collective-permute-start(f32[384,128]{1,0:T(8,128)S(1)} %get-tuple-element.54), channel_id=1, source_target_pairs={{0,16},{16,32},{32,48},{48,64},{64,80},{80,96},{96,112},{112,0},{1... | collective-permute-start | bytes 589832 | tf_op jit(solution)/shard_map/ppermute | solution.py:742
  66.6 16.3 %collective-permute-start.10 = (f32[32,3,8,128]{3,2,1,0:T(8,128)S(1)}, f32[32,3,8,128]{3,2,1,0:T(8,128)S(1)}, u32[]{:S(2)}, u32[]{:S(2)}) collective-permute-start(f32[32,3,8,128]{3,2,1,0:T(8,128)S(1)} %get-tuple-element.60), channel_id=1, source_target_pairs={{0,1},{1,2},{2,3},{3,4},{4,5},{5,6},{6,7},{7,8},{8,9},{9,10},{10,1... | collective-permute-start | bytes 1179656 | tf_op jit(solution)/shard_map/ppermute | solution.py:742
  66.6 16.3 %collective-permute-start.11 = (f32[32,3,8,128]{3,2,1,0:T(8,128)S(1)}, f32[32,3,8,128]{3,2,1,0:T(8,128)S(1)}, u32[]{:S(2)}, u32[]{:S(2)}) collective-permute-start(f32[32,3,8,128]{3,2,1,0:T(8,128)S(1)} %get-tuple-element.61), channel_id=1, source_target_pairs={{0,15},{1,0},{2,1},{3,2},{4,3},{5,4},{6,5},{7,6},{8,7},{9,8},{10,9... | collective-permute-start | bytes 1179656 | tf_op jit(solution)/shard_map/ppermute | solution.py:742
  67.5 15.3 %collective-permute-start.8 = (f32[384,128]{1,0:T(8,128)S(1)}, f32[384,128]{1,0:T(8,128)S(1)}, u32[]{:S(2)}, u32[]{:S(2)}) collective-permute-start(f32[384,128]{1,0:T(8,128)S(1)} %get-tuple-element.58), channel_id=1, source_target_pairs={{0,16},{16,32},{32,48},{48,64},{64,80},{80,96},{96,112},{112,0},{1... | collective-permute-start | bytes 589832 | tf_op jit(solution)/shard_map/ppermute | solution.py:742
  67.5 15.4 %collective-permute-start.9 = (f32[384,128]{1,0:T(8,128)S(1)}, f32[384,128]{1,0:T(8,128)S(1)}, u32[]{:S(2)}, u32[]{:S(2)}) collective-permute-start(f32[384,128]{1,0:T(8,128)S(1)} %get-tuple-element.59), channel_id=1, source_target_pairs={{0,112},{16,0},{32,16},{48,32},{64,48},{80,64},{96,80},{112,96},{1... | collective-permute-start | bytes 589832 | tf_op jit(solution)/shard_map/ppermute | solution.py:742
  85.9 19.8 %collective-permute-start.14 = (f32[32,6,8,128]{3,2,1,0:T(8,128)S(1)}, f32[32,6,8,128]{3,2,1,0:T(8,128)S(1)}, u32[]{:S(2)}, u32[]{:S(2)}) collective-permute-start(f32[32,6,8,128]{3,2,1,0:T(8,128)S(1)} %get-tuple-element.65), channel_id=1, source_target_pairs={{0,15},{1,0},{2,1},{3,2},{4,3},{5,4},{6,5},{7,6},{8,7},{9,8},{10,9... | collective-permute-start | bytes 2359304 | tf_op jit(solution)/shard_map/ppermute | solution.py:742
  90.3 17.0 %collective-permute-start.15 = (f32[32,6,8,128]{3,2,1,0:T(8,128)S(1)}, f32[32,6,8,128]{3,2,1,0:T(8,128)S(1)}, u32[]{:S(2)}, u32[]{:S(2)}) collective-permute-start(f32[32,6,8,128]{3,2,1,0:T(8,128)S(1)} %get-tuple-element.66), channel_id=1, source_target_pairs={{0,1},{1,2},{2,3},{3,4},{4,5},{5,6},{6,7},{7,8},{8,9},{9,10},{10,1... | collective-permute-start | bytes 2359304 | tf_op jit(solution)/shard_map/ppermute | solution.py:742
  90.3 25.4 %collective-permute-start.12 = (f32[768,128]{1,0:T(8,128)S(1)}, f32[768,128]{1,0:T(8,128)S(1)}, u32[]{:S(2)}, u32[]{:S(2)}) collective-permute-start(f32[768,128]{1,0:T(8,128)S(1)} %get-tuple-element.63), channel_id=1, source_target_pairs={{0,112},{16,0},{32,16},{48,32},{64,48},{80,64},{96,80},{112,96},{1... | collective-permute-start | bytes 1179656 | tf_op jit(solution)/shard_map/ppermute | solution.py:742
  91.5 25.5 %collective-permute-start.13 = (f32[768,128]{1,0:T(8,128)S(1)}, f32[768,128]{1,0:T(8,128)S(1)}, u32[]{:S(2)}, u32[]{:S(2)}) collective-permute-start(f32[768,128]{1,0:T(8,128)S(1)} %get-tuple-element.64), channel_id=1, source_target_pairs={{0,16},{16,32},{32,48},{48,64},{64,80},{80,96},{96,112},{112,0},{1... | collective-permute-start | bytes 1179656 | tf_op jit(solution)/shard_map/ppermute | solution.py:742
  117.0 8.0 %collective-permute-start.16 = (f32[30,8,128]{2,1,0:T(8,128)S(1)}, f32[30,8,128]{2,1,0:T(8,128)S(1)}, u32[]{:S(2)}, u32[]{:S(2)}) collective-permute-start(f32[30,8,128]{2,1,0:T(8,128)S(1)} %get-tuple-element.72), channel_id=1, source_target_pairs={{0,1},{1,2},{2,3},{3,4},{4,5},{5,6},{6,7},{7,8},{8,9},{9,10},{10,1... | collective-permute-start | bytes 368648 | tf_op jit(solution)/shard_map/ppermute | solution.py:742
  117.7 7.3 %collective-permute-start.17 = (f32[30,8,128]{2,1,0:T(8,128)S(1)}, f32[30,8,128]{2,1,0:T(8,128)S(1)}, u32[]{:S(2)}, u32[]{:S(2)}) collective-permute-start(f32[30,8,128]{2,1,0:T(8,128)S(1)} %get-tuple-element.73), channel_id=1, source_target_pairs={{0,15},{1,0},{2,1},{3,2},{4,3},{5,4},{6,5},{7,6},{8,7},{9,8},{10,9... | collective-permute-start | bytes 368648 | tf_op jit(solution)/shard_map/ppermute | solution.py:742

commit v7 on v6

--- a/solution.py
+++ b/solution.py
@@ -158,7 +158,7 @@
                 start = c * 512 + lax.rem(block, 16) * 32 + low
                 out_ref[g, pl.ds((c * 10 + r) * 4, 4), :] = rows_ref[pl.ds(start, 4, stride=8), :]
 
-    loop(0, 16, to)
+    loop_pairs(0, 16, to)
 
 
 def unpack_level(rows_ref, p_ref, ylo_ref, yhi_ref):
@@ -171,7 +171,7 @@
             if y >= 13:
                 yhi_ref[x, y - 13] = col
 
-    loop(0, 32, to)
+    loop_pairs(0, 32, to)
 
 
 def refine_table():
@@ -387,7 +387,7 @@
                 total = total + march.part(y, v_ref[1, x, y])
             acc_ref[x, y] = total
 
-    loop(0, 16, x_line)
+    loop_pairs(0, 16, x_line)
     loop_pairs(1, 31, y_line)
 
 

time: 152 us -> 152 us (level)
  no operation moved by 1% of the time
where the time goes in v7:
time: 152 us; the launch traced here: 151 us
  Pallas kernels  78.9 us (52%)
  starting transfers between devices  33.5 us (22%)
  blocking collectives  16.7 us (11%)
  waiting for transfers between devices  15.7 us (10%)
  local copies, waits for them, and re-layouts  5.51 us (4%)
    pallas_call x17, Pallas kernels, call(): pl.pallas_call(kernel, out_shape=outs, in_specs=[spec(k) for k in range(l...  78.9 us
    ppermute x18, starting transfers between devices, moved(): lax.ppermute(values, axis, [(i, (i + step) % count) for i in range(count)])  25.7 us
    all_to_all x1, blocking collectives, per_device(): lax.all_to_all(packed, 'gy', split_axis=0, concat_axis=0, tiled=True)  16.7 us
    ppermute x18, waiting for transfers between devices, moved(): lax.ppermute(values, axis, [(i, (i + step) % count) for i in range(count)])  14.7 us
    all_to_all x1, starting transfers between devices, per_device(): coarse = lax.all_to_all(send, 'gy', split_axis=0, concat_axis=0, tiled=True)  7.76 us
    unnamed x10, local copies, waits for them, and re-layouts  4.68 us
  transfers between devices with their start and end apart: 19, of which 7 were waited for; matrix products, arithmetic and copies ran while one was open for 0% of the time, Pallas kernels for 39%

profile of v7, /device:TPU:1, one launch (start us, length us, event | category | flops | bytes accessed | tf_op | source)
XLA Modules:
  0.0 151.2 jit_solution(6746132073529813329)
XLA Ops:
  0.6 1.1 copy-done.3
  1.8 1.2 pack.1
  3.0 7.8 %all-to-all-start = ((f32[16,120,128]{2,1,0:T(8,128)}), f32[16,120,128]{2,1,0:T(8,128)S(1)}, u32[]{:S(2)}, u32[]{:S(2)}) async-start(f32[16,120,128]{2,1,0:T(8,128)} %pack.1), calls=%async_computation | async-start | bytes 1966080 | tf_op jit(solution)/shard_map/all_to_all | solution.py:756
  10.8 1.6 %copy-done.2 = f32[32,16,1024]{2,1,0:T(8,128)S(1)} copy-done((f32[32,16,1024]{2,1,0:T(8,128)S(1)}, f32[32,16,1024]{2,1,0:T(8,128)}, u32[]{:S(2)}) %copy-start.2) | copy-done | bytes 2097176
  12.3 1.3 unpack.1
  13.7 1.6 %collective-permute-start.2 = (f32[32,3,8,128]{3,2,1,0:T(8,128)}, f32[32,3,8,128]{3,2,1,0:T(8,128)}, u32[]{:S(2)}, u32[]{:S(2)}) collective-permute-start(f32[32,3,8,128]{3,2,1,0:T(8,128)} %get-tuple-element.50), channel_id=1, source_target_pairs={{0,1},{1,2},{2,3},{3,4},{4,5},{5,6},{6,7},{7,8},{8,9},{9,10},{10,1... | collective-permute-start | bytes 1179656 | tf_op jit(solution)/shard_map/ppermute | solution.py:742
  15.3 0.0 collective-permute-start.3
  15.3 7.5 %depth.1 = (f32[2,32,16,8,128]{4,3,2,1,0:T(8,128)S(1)}, f32[2,2,16,8,128]{4,3,2,1,0:T(8,128)S(1)}) custom-call(f32[32,16,8,128]{3,2,1,0:T(8,128)S(1)} %get-tuple-element.41.p_ref.start_ref), custom_call_target="tpu_custom_call" | custom-call | flops 47185920 | bytes 8388608 | tf_op jit(solution)/shard_map/depth/pallas_call | solution.py:727
  22.8 2.0 %copy-done = f32[2,32,16,8,128]{4,3,2,1,0:T(8,128)} copy-done((f32[2,32,16,8,128]{4,3,2,1,0:T(8,128)}, f32[2,32,16,8,128]{4,3,2,1,0:T(8,128)S(1)}, u32[]{:S(2)}) %copy-start) | copy-done | bytes 4194328
  24.8 1.1 all-to-all-done
  25.9 1.4 collective-permute-start
  27.2 3.8 %collective-permute-start.1 = (f32[504,128]{1,0:T(8,128)S(1)}, f32[504,128]{1,0:T(8,128)S(1)}, u32[]{:S(2)}, u32[]{:S(2)}) collective-permute-start(f32[504,128]{1,0:T(8,128)S(1)} %get-tuple-element.44), channel_id=1, source_target_pairs={{0,112},{16,0},{32,16},{48,32},{64,48},{80,64},{96,80},{112,96},{1... | collective-permute-start | bytes 774152 | tf_op jit(solution)/shard_map/ppermute | solution.py:742
  31.0 3.9 %refine.1 = (f32[3,32,16,8,128]{4,3,2,1,0:T(8,128)S(1)}, f32[2,240,128]{2,1,0:T(8,128)S(1)}) custom-call(f32[1920,128]{1,0:T(8,128)S(1)} %bitcast.30, s32[2,1,64]{2,1,0:T(1,128)S(1)} %copy-done.4), custom_call_target="tpu_custom_call" | custom-call | flops 10485760 | bytes 8388608 | tf_op jit(solution)/shard_map/refine/pallas_call | solution.py:727
  34.9 5.0 %first.1.acc_in = f32[32,16,8,128]{3,2,1,0:T(8,128)S(1)} custom-call(f32[32,16,8,128]{3,2,1,0:T(8,128)S(1)} %get-tuple-element.41.p_ref.start_ref, f32[3,32,16,8,128]{4,3,2,1,0:T(8,128)S(1)} %get-tuple-element.46.v_ref.v_in, f32[2,32,16,8,128]{4,3,2,1,0:T(8,128)S(1)} %copy-done.1), custom_call_target="tpu_custom_call" | custom-call | flops 47185920 | bytes 8388608 | tf_op jit(solution)/shard_map/first/pallas_call | solution.py:727
  40.0 1.6 %collective-permute-done.lo_ref.x1_ref = f32[504,128]{1,0:T(8,128)S(1)} collective-permute-done((f32[504,128]{1,0:T(8,128)S(1)}, f32[504,128]{1,0:T(8,128)S(1)}, u32[]{:S(2)}, u32[]{:S(2)}) %collective-permute-start) | collective-permute-done | bytes 258080 | tf_op jit(solution)/shard_map/ppermute | solution.py:742
  41.6 0.0 collective-permute-done.1.hi_ref.x2_ref
  41.6 1.4 ends.1
  43.0 0.0 collective-permute-done.3.y2_ref
  43.0 3.8 %edge.3 = (f32[32,16,8,128]{3,2,1,0:T(8,128)S(1)}, f32[384,128]{1,0:T(8,128)S(1)}, f32[384,128]{1,0:T(8,128)S(1)}, f32[32,3,8,128]{3,2,1,0:T(8,128)S(1)}, f32[32,3,8,128]{3,2,1,0:T(8,128)S(1)}) custom-call(f32[32,16,8,128]{3,2,1,0:T(8,128)S(1)} %get-tuple-element.48.acc_ref, f32[32,16,8,128]{3,2,1,0:T(8,128)S(1)} %get-tuple-element.41.p_ref.start_ref, ...), custom_call_target="tpu_custom_call" | custom-call | flops 15728640 | bytes 8388608 | tf_op jit(solution)/shard_map/edge/pallas_call | solution.py:727
  46.8 0.7 collective-permute-start.6
  47.5 1.2 collective-permute-start.7
  48.7 1.4 collective-permute-start.4
  50.1 0.0 collective-permute-start.5
  50.1 10.3 %inner.2.acc_ref = f32[32,16,8,128]{3,2,1,0:T(8,128)S(1)} custom-call(f32[32,16,8,128]{3,2,1,0:T(8,128)S(1)} %get-tuple-element.52.p_ref, f32[3,32,16,8,128]{4,3,2,1,0:T(8,128)S(1)} %get-tuple-element.49.v_ref), custom_call_target="tpu_custom_call" | custom-call | flops 73400320 | bytes 8388608 | tf_op jit(solution)/shard_map/inner/pallas_call | solution.py:727
  60.4 0.0 collective-permute-done.4.x1_ref
  60.4 3.1 %collective-permute-done.5.x2_ref = f32[384,128]{1,0:T(8,128)S(1)} collective-permute-done((f32[384,128]{1,0:T(8,128)S(1)}, f32[384,128]{1,0:T(8,128)S(1)}, u32[]{:S(2)}, u32[]{:S(2)}) %collective-permute-start.5) | collective-permute-done | bytes 196640 | tf_op jit(solution)/shard_map/ppermute | solution.py:742
  63.5 0.0 collective-permute-done.6.y1_ref
  63.5 2.9 %edge.4 = (f32[32,16,8,128]{3,2,1,0:T(8,128)S(1)}, f32[384,128]{1,0:T(8,128)S(1)}, f32[384,128]{1,0:T(8,128)S(1)}, f32[32,3,8,128]{3,2,1,0:T(8,128)S(1)}, f32[32,3,8,128]{3,2,1,0:T(8,128)S(1)}) custom-call(f32[32,16,8,128]{3,2,1,0:T(8,128)S(1)} %inner.2.acc_ref, f32[32,16,8,128]{3,2,1,0:T(8,128)S(1)} %get-tuple-element.41.p_ref.start_ref, ...), custom_call_target="tpu_custom_call" | custom-call | flops 15728640 | bytes 8388608 | tf_op jit(solution)/shard_map/edge/pallas_call | solution.py:727
  66.5 0.1 collective-permute-start.10
  66.5 0.9 collective-permute-start.11
  67.5 5.1 %collective-permute-start.9 = (f32[384,128]{1,0:T(8,128)S(1)}, f32[384,128]{1,0:T(8,128)S(1)}, u32[]{:S(2)}, u32[]{:S(2)}) collective-permute-start(f32[384,128]{1,0:T(8,128)S(1)} %get-tuple-element.59), channel_id=1, source_target_pairs={{0,112},{16,0},{32,16},{48,32},{64,48},{80,64},{96,80},{112,96},{1... | collective-permute-start | bytes 589832 | tf_op jit(solution)/shard_map/ppermute | solution.py:742
  72.6 10.3 %inner.3.acc_ref = f32[32,16,8,128]{3,2,1,0:T(8,128)S(1)} custom-call(f32[32,16,8,128]{3,2,1,0:T(8,128)S(1)} %get-tuple-element.57.p_ref, f32[3,32,16,8,128]{4,3,2,1,0:T(8,128)S(1)} %get-tuple-element.49.v_ref), custom_call_target="tpu_custom_call" | custom-call | flops 73400320 | bytes 8388608 | tf_op jit(solution)/shard_map/inner/pallas_call | solution.py:727
  82.9 3.0 %edge.5 = (f32[32,16,8,128]{3,2,1,0:T(8,128)S(1)}, f32[768,128]{1,0:T(8,128)S(1)}, f32[768,128]{1,0:T(8,128)S(1)}, f32[32,6,8,128]{3,2,1,0:T(8,128)S(1)}, f32[32,6,8,128]{3,2,1,0:T(8,128)S(1)}) custom-call(f32[32,16,8,128]{3,2,1,0:T(8,128)S(1)} %inner.3.acc_ref, f32[32,16,8,128]{3,2,1,0:T(8,128)S(1)} %get-tuple-element.41.p_ref.start_ref, ...), custom_call_target="tpu_custom_call" | custom-call | flops 15728640 | bytes 8388608 | tf_op jit(solution)/shard_map/edge/pallas_call | solution.py:727
  85.9 4.4 %collective-permute-start.14 = (f32[32,6,8,128]{3,2,1,0:T(8,128)S(1)}, f32[32,6,8,128]{3,2,1,0:T(8,128)S(1)}, u32[]{:S(2)}, u32[]{:S(2)}) collective-permute-start(f32[32,6,8,128]{3,2,1,0:T(8,128)S(1)} %get-tuple-element.65), channel_id=1, source_target_pairs={{0,15},{1,0},{2,1},{3,2},{4,3},{5,4},{6,5},{7,6},{8,7},{9,8},{10,9... | collective-permute-start | bytes 2359304 | tf_op jit(solution)/shard_map/ppermute | solution.py:742
  90.3 1.1 collective-permute-start.12
  91.4 0.3 collective-permute-start.13
  91.7 7.3 %core.1 = (f32[32,16,8,128]{3,2,1,0:T(8,128)S(1)}, f32[32,16,8,128]{3,2,1,0:T(8,128)S(1)}, f32[32,16,8,128]{3,2,1,0:T(8,128)S(1)}, f32[32,16,8,128]{3,2,1,0:T(8,128)S(1)}) custom-call(f32[32,16,8,128]{3,2,1,0:T(8,128)S(1)} %get-tuple-element.62.adv_ref), custom_call_target="tpu_custom_call" | custom-call | flops 47185920 | bytes 8388608 | tf_op jit(solution)/shard_map/core/pallas_call | solution.py:727
  99.1 6.6 %collective-permute-done.14.yhi_ref = f32[32,6,8,128]{3,2,1,0:T(8,128)S(1)} collective-permute-done((f32[32,6,8,128]{3,2,1,0:T(8,128)S(1)}, f32[32,6,8,128]{3,2,1,0:T(8,128)S(1)}, u32[]{:S(2)}, u32[]{:S(2)}) %collective-permute-start.14) | collective-permute-done | bytes 786464 | tf_op jit(solution)/shard_map/ppermute | solution.py:742
  105.7 1.6 %collective-permute-done.15.ylo_ref = f32[32,6,8,128]{3,2,1,0:T(8,128)S(1)} collective-permute-done((f32[32,6,8,128]{3,2,1,0:T(8,128)S(1)}, f32[32,6,8,128]{3,2,1,0:T(8,128)S(1)}, u32[]{:S(2)}, u32[]{:S(2)}) %collective-permute-start.15) | collective-permute-done | bytes 786464 | tf_op jit(solution)/shard_map/ppermute | solution.py:742
  107.3 7.8 %sides.1 = (f32[3,4,28,8,128]{4,3,2,1,0:T(8,128)S(1)}, f32[32,28,8,128]{3,2,1,0:T(8,128)S(1)}) custom-call(f32[32,16,8,128]{3,2,1,0:T(8,128)S(1)} %get-tuple-element.62.adv_ref, f32[32,6,8,128]{3,2,1,0:T(8,128)S(1)} %collective-permute-done.14.yhi_ref, f32[32,6,8,128]{3,2,1,0:T(8,128)S(1)} %collective-permute-done.15.ylo_ref, ...), custom_call_target="tpu_custom_call" | custom-call | flops 36700160 | bytes 8388608 | tf_op jit(solution)/shard_map/sides/pallas_call | solution.py:727
  115.1 0.6 collective-permute-done.12.xhi_ref
  115.7 1.2 collective-permute-done.13.xlo_ref
  116.9 0.8 collective-permute-start.16
  117.7 2.9 %collective-permute-start.17 = (f32[30,8,128]{2,1,0:T(8,128)S(1)}, f32[30,8,128]{2,1,0:T(8,128)S(1)}, u32[]{:S(2)}, u32[]{:S(2)}) collective-permute-start(f32[30,8,128]{2,1,0:T(8,128)S(1)} %get-tuple-element.73), channel_id=1, source_target_pairs={{0,15},{1,0},{2,1},{3,2},{4,3},{5,4},{6,5},{7,6},{8,7},{9,8},{10,9... | collective-permute-start | bytes 368648 | tf_op jit(solution)/shard_map/ppermute | solution.py:742
  120.6 4.4 %outputs.1 = (f32[4096,128]{1,0:T(8,128)}, f32[10,64,128]{2,1,0:T(8,128)S(1)}) custom-call(f32[32,28,8,128]{3,2,1,0:T(8,128)S(1)} %get-tuple-element.74.last.rows_ref), custom_call_target="tpu_custom_call" | custom-call | flops 20971520 | bytes 8388608 | tf_op jit(solution)/shard_map/outputs/pallas_call | solution.py:727
  125.0 8.7 %finish.1 = (f32[4096,128]{1,0:T(8,128)}, f32[16,64,128]{2,1,0:T(8,128)S(1)}) custom-call(f32[32,16,8,128]{3,2,1,0:T(8,128)S(1)} %get-tuple-element.62.adv_ref, f32[768,128]{1,0:T(8,128)S(1)} %collective-permute-done.12.xhi_ref, f32[768,128]{1,0:T(8,128)S(1)} %collective-permute-done.13.xlo_ref, ...), custom_call_target="tpu_custom_call", output_to_operand_aliasing={{0}: (10, {})} | custom-call | flops 131072000 | bytes 8388608 | tf_op jit(solution)/shard_map/finish/pallas_call | solution.py:727
  133.7 16.7 %all_to_all.10 = f32[16,64,128]{2,1,0:T(8,128)S(1)} all-to-all(f32[16,64,128]{2,1,0:T(8,128)S(1)} %get-tuple-element.78), channel_id=1, replica_groups=mesh['gx'=8,'gy'=16] {'gy'}, dimensions={0} | all-to-all | bytes 1048576 | tf_op jit(solution)/shard_map/all_to_all | solution.py:822
  150.3 0.8 slice_bitcast_fusion
  (19 shorter events, 0.1 us)
Async XLA Ops:
  0.6 1.1 copy-start.3
  3.0 22.8 %all-to-all-start = ((f32[16,120,128]{2,1,0:T(8,128)}), f32[16,120,128]{2,1,0:T(8,128)S(1)}, u32[]{:S(2)}, u32[]{:S(2)}) async-start(f32[16,120,128]{2,1,0:T(8,128)} %pack.1), calls=%async_computation | async-start | bytes 1966080 | tf_op jit(solution)/shard_map/all_to_all | solution.py:756
  10.7 1.6 %copy-start.2 = (f32[32,16,1024]{2,1,0:T(8,128)S(1)}, f32[32,16,1024]{2,1,0:T(8,128)}, u32[]{:S(2)}) copy-start(f32[32,16,1024]{2,1,0:T(8,128)} %param.3) | copy-start | bytes 6291460
  13.7 29.3 %collective-permute-start.2 = (f32[32,3,8,128]{3,2,1,0:T(8,128)}, f32[32,3,8,128]{3,2,1,0:T(8,128)}, u32[]{:S(2)}, u32[]{:S(2)}) collective-permute-start(f32[32,3,8,128]{3,2,1,0:T(8,128)} %get-tuple-element.50), channel_id=1, source_target_pairs={{0,1},{1,2},{2,3},{3,4},{4,5},{5,6},{6,7},{7,8},{8,9},{9,10},{10,1... | collective-permute-start | bytes 1179656 | tf_op jit(solution)/shard_map/ppermute | solution.py:742
  15.3 27.7 %collective-permute-start.3 = (f32[32,3,8,128]{3,2,1,0:T(8,128)}, f32[32,3,8,128]{3,2,1,0:T(8,128)}, u32[]{:S(2)}, u32[]{:S(2)}) collective-permute-start(f32[32,3,8,128]{3,2,1,0:T(8,128)} %get-tuple-element.51), channel_id=1, source_target_pairs={{0,15},{1,0},{2,1},{3,2},{4,3},{5,4},{6,5},{7,6},{8,7},{9,8},{10,9... | collective-permute-start | bytes 1179656 | tf_op jit(solution)/shard_map/ppermute | solution.py:742
  22.8 2.0 %copy-start = (f32[2,32,16,8,128]{4,3,2,1,0:T(8,128)}, f32[2,32,16,8,128]{4,3,2,1,0:T(8,128)S(1)}, u32[]{:S(2)}) copy-start(f32[2,32,16,8,128]{4,3,2,1,0:T(8,128)S(1)} %get-tuple-element.47.both_ref) | copy-start | bytes 12582916
  24.8 6.3 %copy-start.4 = (s32[2,1,64]{2,1,0:T(1,128)S(1)}, s32[2,1,64]{2,1,0:T(1,128)}, u32[]{:S(2)}) copy-start(s32[2,1,64]{2,1,0:T(1,128)} %band_ref.3) | copy-start | bytes 1540
  25.8 9.1 %copy-start.1 = (f32[2,32,16,8,128]{4,3,2,1,0:T(8,128)S(1)}, f32[2,32,16,8,128]{4,3,2,1,0:T(8,128)}, u32[]{:S(2)}) copy-start(f32[2,32,16,8,128]{4,3,2,1,0:T(8,128)} %copy-done) | copy-start | bytes 12582916
  25.9 15.7 %collective-permute-start = (f32[504,128]{1,0:T(8,128)S(1)}, f32[504,128]{1,0:T(8,128)S(1)}, u32[]{:S(2)}, u32[]{:S(2)}) collective-permute-start(f32[504,128]{1,0:T(8,128)S(1)} %get-tuple-element.43), channel_id=1, source_target_pairs={{0,16},{16,32},{32,48},{48,64},{64,80},{80,96},{96,112},{112,0},{1... | collective-permute-start | bytes 774152 | tf_op jit(solution)/shard_map/ppermute | solution.py:742
  27.2 14.3 %collective-permute-start.1 = (f32[504,128]{1,0:T(8,128)S(1)}, f32[504,128]{1,0:T(8,128)S(1)}, u32[]{:S(2)}, u32[]{:S(2)}) collective-permute-start(f32[504,128]{1,0:T(8,128)S(1)} %get-tuple-element.44), channel_id=1, source_target_pairs={{0,112},{16,0},{32,16},{48,32},{64,48},{80,64},{96,80},{112,96},{1... | collective-permute-start | bytes 774152 | tf_op jit(solution)/shard_map/ppermute | solution.py:742
  46.8 16.7 %collective-permute-start.6 = (f32[32,3,8,128]{3,2,1,0:T(8,128)S(1)}, f32[32,3,8,128]{3,2,1,0:T(8,128)S(1)}, u32[]{:S(2)}, u32[]{:S(2)}) collective-permute-start(f32[32,3,8,128]{3,2,1,0:T(8,128)S(1)} %get-tuple-element.55), channel_id=1, source_target_pairs={{0,15},{1,0},{2,1},{3,2},{4,3},{5,4},{6,5},{7,6},{8,7},{9,8},{10,9... | collective-permute-start | bytes 1179656 | tf_op jit(solution)/shard_map/ppermute | solution.py:742
  47.5 16.0 %collective-permute-start.7 = (f32[32,3,8,128]{3,2,1,0:T(8,128)S(1)}, f32[32,3,8,128]{3,2,1,0:T(8,128)S(1)}, u32[]{:S(2)}, u32[]{:S(2)}) collective-permute-start(f32[32,3,8,128]{3,2,1,0:T(8,128)S(1)} %get-tuple-element.56), channel_id=1, source_target_pairs={{0,1},{1,2},{2,3},{3,4},{4,5},{5,6},{6,7},{7,8},{8,9},{9,10},{10,1... | collective-permute-start | bytes 1179656 | tf_op jit(solution)/shard_map/ppermute | solution.py:742
  48.7 11.7 %collective-permute-start.4 = (f32[384,128]{1,0:T(8,128)S(1)}, f32[384,128]{1,0:T(8,128)S(1)}, u32[]{:S(2)}, u32[]{:S(2)}) collective-permute-start(f32[384,128]{1,0:T(8,128)S(1)} %get-tuple-element.53), channel_id=1, source_target_pairs={{0,112},{16,0},{32,16},{48,32},{64,48},{80,64},{96,80},{112,96},{1... | collective-permute-start | bytes 589832 | tf_op jit(solution)/shard_map/ppermute | solution.py:742
  50.1 13.4 %collective-permute-start.5 = (f32[384,128]{1,0:T(8,128)S(1)}, f32[384,128]{1,0:T(8,128)S(1)}, u32[]{:S(2)}, u32[]{:S(2)}) collective-permute-start(f32[384,128]{1,0:T(8,128)S(1)} %get-tuple-element.54), channel_id=1, source_target_pairs={{0,16},{16,32},{32,48},{48,64},{64,80},{80,96},{96,112},{112,0},{1... | collective-permute-start | bytes 589832 | tf_op jit(solution)/shard_map/ppermute | solution.py:742
  66.5 16.4 %collective-permute-start.10 = (f32[32,3,8,128]{3,2,1,0:T(8,128)S(1)}, f32[32,3,8,128]{3,2,1,0:T(8,128)S(1)}, u32[]{:S(2)}, u32[]{:S(2)}) collective-permute-start(f32[32,3,8,128]{3,2,1,0:T(8,128)S(1)} %get-tuple-element.60), channel_id=1, source_target_pairs={{0,1},{1,2},{2,3},{3,4},{4,5},{5,6},{6,7},{7,8},{8,9},{9,10},{10,1... | collective-permute-start | bytes 1179656 | tf_op jit(solution)/shard_map/ppermute | solution.py:742
  66.5 16.3 %collective-permute-start.11 = (f32[32,3,8,128]{3,2,1,0:T(8,128)S(1)}, f32[32,3,8,128]{3,2,1,0:T(8,128)S(1)}, u32[]{:S(2)}, u32[]{:S(2)}) collective-permute-start(f32[32,3,8,128]{3,2,1,0:T(8,128)S(1)} %get-tuple-element.61), channel_id=1, source_target_pairs={{0,15},{1,0},{2,1},{3,2},{4,3},{5,4},{6,5},{7,6},{8,7},{9,8},{10,9... | collective-permute-start | bytes 1179656 | tf_op jit(solution)/shard_map/ppermute | solution.py:742
  67.5 15.3 %collective-permute-start.8 = (f32[384,128]{1,0:T(8,128)S(1)}, f32[384,128]{1,0:T(8,128)S(1)}, u32[]{:S(2)}, u32[]{:S(2)}) collective-permute-start(f32[384,128]{1,0:T(8,128)S(1)} %get-tuple-element.58), channel_id=1, source_target_pairs={{0,16},{16,32},{32,48},{48,64},{64,80},{80,96},{96,112},{112,0},{1... | collective-permute-start | bytes 589832 | tf_op jit(solution)/shard_map/ppermute | solution.py:742
  67.5 15.4 %collective-permute-start.9 = (f32[384,128]{1,0:T(8,128)S(1)}, f32[384,128]{1,0:T(8,128)S(1)}, u32[]{:S(2)}, u32[]{:S(2)}) collective-permute-start(f32[384,128]{1,0:T(8,128)S(1)} %get-tuple-element.59), channel_id=1, source_target_pairs={{0,112},{16,0},{32,16},{48,32},{64,48},{80,64},{96,80},{112,96},{1... | collective-permute-start | bytes 589832 | tf_op jit(solution)/shard_map/ppermute | solution.py:742
  85.9 19.8 %collective-permute-start.14 = (f32[32,6,8,128]{3,2,1,0:T(8,128)S(1)}, f32[32,6,8,128]{3,2,1,0:T(8,128)S(1)}, u32[]{:S(2)}, u32[]{:S(2)}) collective-permute-start(f32[32,6,8,128]{3,2,1,0:T(8,128)S(1)} %get-tuple-element.65), channel_id=1, source_target_pairs={{0,15},{1,0},{2,1},{3,2},{4,3},{5,4},{6,5},{7,6},{8,7},{9,8},{10,9... | collective-permute-start | bytes 2359304 | tf_op jit(solution)/shard_map/ppermute | solution.py:742
  90.3 17.0 %collective-permute-start.15 = (f32[32,6,8,128]{3,2,1,0:T(8,128)S(1)}, f32[32,6,8,128]{3,2,1,0:T(8,128)S(1)}, u32[]{:S(2)}, u32[]{:S(2)}) collective-permute-start(f32[32,6,8,128]{3,2,1,0:T(8,128)S(1)} %get-tuple-element.66), channel_id=1, source_target_pairs={{0,1},{1,2},{2,3},{3,4},{4,5},{5,6},{6,7},{7,8},{8,9},{9,10},{10,1... | collective-permute-start | bytes 2359304 | tf_op jit(solution)/shard_map/ppermute | solution.py:742
  90.3 25.4 %collective-permute-start.12 = (f32[768,128]{1,0:T(8,128)S(1)}, f32[768,128]{1,0:T(8,128)S(1)}, u32[]{:S(2)}, u32[]{:S(2)}) collective-permute-start(f32[768,128]{1,0:T(8,128)S(1)} %get-tuple-element.63), channel_id=1, source_target_pairs={{0,112},{16,0},{32,16},{48,32},{64,48},{80,64},{96,80},{112,96},{1... | collective-permute-start | bytes 1179656 | tf_op jit(solution)/shard_map/ppermute | solution.py:742
  91.4 25.4 %collective-permute-start.13 = (f32[768,128]{1,0:T(8,128)S(1)}, f32[768,128]{1,0:T(8,128)S(1)}, u32[]{:S(2)}, u32[]{:S(2)}) collective-permute-start(f32[768,128]{1,0:T(8,128)S(1)} %get-tuple-element.64), channel_id=1, source_target_pairs={{0,16},{16,32},{32,48},{48,64},{64,80},{80,96},{96,112},{112,0},{1... | collective-permute-start | bytes 1179656 | tf_op jit(solution)/shard_map/ppermute | solution.py:742
  116.9 8.1 %collective-permute-start.16 = (f32[30,8,128]{2,1,0:T(8,128)S(1)}, f32[30,8,128]{2,1,0:T(8,128)S(1)}, u32[]{:S(2)}, u32[]{:S(2)}) collective-permute-start(f32[30,8,128]{2,1,0:T(8,128)S(1)} %get-tuple-element.72), channel_id=1, source_target_pairs={{0,1},{1,2},{2,3},{3,4},{4,5},{5,6},{6,7},{7,8},{8,9},{9,10},{10,1... | collective-permute-start | bytes 368648 | tf_op jit(solution)/shard_map/ppermute | solution.py:742
  117.7 7.3 %collective-permute-start.17 = (f32[30,8,128]{2,1,0:T(8,128)S(1)}, f32[30,8,128]{2,1,0:T(8,128)S(1)}, u32[]{:S(2)}, u32[]{:S(2)}) collective-permute-start(f32[30,8,128]{2,1,0:T(8,128)S(1)} %get-tuple-element.73), channel_id=1, source_target_pairs={{0,15},{1,0},{2,1},{3,2},{4,3},{5,4},{6,5},{7,6},{8,7},{9,8},{10,9... | collective-permute-start | bytes 368648 | tf_op jit(solution)/shard_map/ppermute | solution.py:742
